TPU v7x, 32 devices: a whole 2x2x4 slice. The times are simulated.
32 devices in a mesh: dp: 16 (over z, x, core), tensor: 2 (over y).
Axes of the slice: x: 2, y: 2, z: 4, core: 2. Of those that a mesh axis runs over, the one named last changes fastest.
Arguments:
- tokens: bfloat16 [16384, 768], P(('dp', 'tensor')), may hold values from -6 to 6
- segment_ids: int32 [16, 1024], P('dp'), may hold values from 0 to 4, as said below
- pad_mask: int32 [16, 1024], P('dp'), may hold values from 0 to 1, as said below
- norm1_gain: float32 [768], replicated, may hold values from 0.5 to 1.5
- norm1_shift: float32 [768], replicated, may hold values from -1 to 1
- w_query: bfloat16 [768, 768], P(None, 'tensor'), may hold values from -2 to 2
- w_key: bfloat16 [768, 768], P(None, 'tensor'), may hold values from -2 to 2
- w_value: bfloat16 [768, 768], P(None, 'tensor'), may hold values from -0.21875 to 0.21875
- w_out: bfloat16 [768, 768], P('tensor'), may hold values from -0.4375 to 0.4375
- norm2_gain: float32 [768], replicated, may hold values from 0.5 to 1.5
- norm2_shift: float32 [768], replicated, may hold values from -1 to 1
- w_up: bfloat16 [768, 3072], P(None, 'tensor'), may hold values from -0.21875 to 0.21875
- w_down: bfloat16 [3072, 768], P('tensor'), may hold values from -0.109375 to 0.109375
- cotangent: bfloat16 [16384, 768], P(('dp', 'tensor')), may hold values from -6 to 6
Outputs:
- mixed: bfloat16 [16384, 768], P(('dp', 'tensor'))
- tokens_grad: bfloat16 [16384, 768], P(('dp', 'tensor'))
- norm1_gain_grad: float32 [768], replicated
- norm1_shift_grad: float32 [768], replicated
- w_query_grad: float32 [768, 768], P(None, 'tensor')
- w_key_grad: float32 [768, 768], P(None, 'tensor')
- w_value_grad: float32 [768, 768], P(None, 'tensor')
- w_out_grad: float32 [768, 768], P('tensor')
- norm2_gain_grad: float32 [768], replicated
- norm2_shift_grad: float32 [768], replicated
- w_up_grad: float32 [768, 3072], P(None, 'tensor')
- w_down_grad: float32 [3072, 768], P('tensor')
Inputs may be any that keep to these rules, and one draw needn't show every extreme that they name: `segment_ids`: in each row the numbers never fall from one position to the next, and positions 256 to 767 lie in one document. `pad_mask`: in each row the pad slots form one nonempty run at the end, inside the row's last document.
All inputs are finite; a program needn't handle non-finite values.
Results may differ from a plain program's by a relative error of at most 0.014.
Values may be sent and summed in bfloat16 or wider, within the bound.
No kernel may reach another device: no remote copies, remote signals or barrier semaphores. Data moves between devices by JAX's collectives and lax.ppermute only.
A program may use at most 192 MiB of HBM per device.

v0:
```python
import functools

import jax
import jax.numpy as jnp
from jax import lax
from jax.experimental import pallas as pl
from jax.experimental.pallas import tpu as pltpu
from jax.sharding import PartitionSpec as P

HEAD_DIM = 64
EPS = 1e-05
FAR = 1e30
FORWARD_BLOCK = 512
BF16 = jnp.bfloat16
F32 = jnp.float32
TN = (((0,), (0,)), ((), ()))
NT = (((1,), (1,)), ((), ()))
NN = (((1,), (0,)), ((), ()))
TT = (((0,), (1,)), ((), ()))
ERF_C = (
    1.5897294934128858e-07,
    -5.985900079472216e-06,
    8.971378204617447e-05,
    -0.0006257225011275588,
    -0.0001843806018428344,
    0.10276548023357895,
    1.1283797055884355,
)
ERF_X = tuple(c * 0.5 ** (6 - i) * 0.7071067811865476 for i, c in enumerate(ERF_C))


def dot(left, right, dims):
    return lax.dot_general(left, right, dims, preferred_element_type=F32)


def sds(shape, dtype):
    return jax.ShapeDtypeStruct(shape, dtype)


SMEM = pl.BlockSpec(memory_space=pltpu.SMEM)
VMEM = pl.BlockSpec(memory_space=pltpu.VMEM)
ANY = pl.BlockSpec(memory_space=pl.ANY)


WEIGHT = 20.0


class Order:
    def __init__(self):
        self.last = None

    def run(self, us, kernel, operands, out_shape, in_specs=None, after=(), **rest):
        after = tuple(after) + (() if self.last is None else (self.last,))
        count, extra = len(operands), len(after)
        in_specs = list(in_specs or [VMEM] * count) + [ANY] * extra

        def body(*refs):
            kernel(*refs[:count], *refs[count + extra :])

        out = pl.pallas_call(
            body,
            out_shape=out_shape,
            in_specs=in_specs,
            compiler_params=pltpu.CompilerParams(vmem_limit_bytes=58 << 20),
            cost_estimate=pl.CostEstimate(
                flops=int(us * WEIGHT * 1.15e9), bytes_accessed=0, transcendentals=0
            ),
            **rest,
        )(*operands, *after)
        self.last = out[-1] if isinstance(out, (list, tuple)) else out
        return out

    def hold(self, values, after):
        count = len(values)

        def kernel(*refs):
            pass

        held = pl.pallas_call(
            kernel,
            out_shape=[sds(value.shape, value.dtype) for value in values],
            in_specs=[ANY] * (count + len(after)),
            out_specs=[ANY] * count,
            input_output_aliases={i: i for i in range(count)},
            compiler_params=pltpu.CompilerParams(has_side_effects=True),
            cost_estimate=pl.CostEstimate(flops=0, bytes_accessed=0, transcendentals=0),
        )(*values, *after)
        for value, same in zip(values, held):
            if self.last is value:
                self.last = same
        return held


def whole(shape):
    return pl.BlockSpec(shape, lambda *_: (0,) * len(shape))


def low_sum(*terms):
    total = terms[0].astype(F32)
    for term in terms[1:]:
        total = total + term.astype(F32)
    return total.astype(BF16)


def part_rows(index, size):
    return pl.ds(pl.multiple_of(index * size, size), size)


def split(place, bit, source, keep, send):
    half = keep.shape[1]
    keep[...] = source[:, part_rows(place[2 + bit], half), :]
    send[...] = source[:, part_rows(1 - place[2 + bit], half), :]


def quarter(place):
    return 2 * place[2] + place[3]


def scatter(place, source, outs):
    for partner, out in enumerate(outs):
        out[...] = source[:, part_rows(quarter(place) ^ partner, out.shape[1]), :]


def gather(place, pieces, out):
    for partner, piece in enumerate(pieces):
        out[:, part_rows(quarter(place) ^ partner, piece.shape[1]), :] = piece[...]


def normalize(values):
    center = values - jnp.mean(values, axis=-1, keepdims=True)
    inverse = lax.rsqrt(jnp.mean(center * center, axis=-1, keepdims=True) + EPS)
    return center * inverse, inverse


def norm_back(grad_normed, scaled, inverse, gain):
    grad_scaled = grad_normed * gain
    return inverse * (
        grad_scaled
        - jnp.mean(grad_scaled, axis=-1, keepdims=True)
        - scaled * jnp.mean(grad_scaled * scaled, axis=-1, keepdims=True)
    )


def gelu_pair(x):
    square = x * x
    near = jnp.minimum(square, 64.0)
    poly = ERF_X[0]
    for coefficient in ERF_X[1:]:
        poly = poly * near + coefficient
    phi = 0.5 * jnp.tanh(x * poly) + 0.5
    bell = jnp.exp(square * -0.5)
    return x * phi, phi + x * (bell * 0.3989422804014327)


def pack_first_kernel(place, w_query, w_key, w_value, qkv, qkv_send, first):
    width = qkv.shape[1] // 3
    half = qkv_send.shape[0]
    first[:, :HEAD_DIM] = w_query[:, :HEAD_DIM]
    first[:, HEAD_DIM:] = w_key[:, :HEAD_DIM]
    for core in range(2):

        @pl.when(place[0] == core)
        def _():
            narrow = slice(core * width, (core + 1) * width)
            for i, weight in enumerate((w_query, w_key, w_value)):
                qkv[:, i * width : (i + 1) * width] = weight[:, narrow]

    qkv_send[...] = qkv[pl.ds(pl.multiple_of(place[2] * half, half), half), :]


def pack_first_call(order, place, w_query, w_key, w_value):
    dim, width = w_query.shape[0], w_query.shape[1] // 2
    return order.run(
        4,
        pack_first_kernel,
        (place, w_query, w_key, w_value),
        [
            sds((dim, 3 * width), BF16),
            sds((dim // 2, 3 * width), BF16),
            sds((dim, 2 * HEAD_DIM), BF16),
        ],
        [SMEM] + [VMEM] * 3,
    )


def pack_last_kernel(place, w_out, w_up, w_down, grad, out, up, up_send, down, down_send, grad_out):
    width = out.shape[0]
    units = down.shape[0]
    half = units // 2
    grad_out[...] = grad[...]
    for core in range(2):

        @pl.when(place[0] == core)
        def _():
            wide = slice(core * units, (core + 1) * units)
            out[...] = w_out[core * width : (core + 1) * width, :]
            up[...] = w_up[:, wide]
            down[...] = w_down[wide, :]

    rows = pl.ds(pl.multiple_of(place[2] * half, half), half)
    up_send[...] = up[rows, :]
    down_send[...] = down[rows, :]


def pack_last_call(order, place, w_out, w_up, w_down, grad):
    width, dim = w_out.shape[0] // 2, w_out.shape[1]
    units = w_up.shape[1] // 2
    return order.run(
        5,
        pack_last_kernel,
        (place, w_out, w_up, w_down, grad),
        [
            sds((width, dim), BF16),
            sds((dim, units), BF16),
            sds((dim // 2, units), BF16),
            sds((units, dim), BF16),
            sds((units // 2, dim), BF16),
            sds(grad.shape, BF16),
        ],
        [SMEM] + [VMEM] * 4,
    )


def norm1_kernel(tokens, gain, shift, out):
    scaled, _ = normalize(tokens[...].astype(F32))
    out[...] = (scaled * gain[...] + shift[...]).astype(BF16)


def rows_spec(block, dim):
    return pl.BlockSpec((block, dim), lambda i: (i, 0))


def norm1_call(order, tokens, gain, shift):
    return order.run(2.5, norm1_kernel, (tokens, gain, shift), sds(tokens.shape, BF16))


def masks(seg_pad, cols, low, high):
    width = high - low
    seg_row = seg_pad[0:1, low:high]
    pad_row = seg_pad[1:2, low:high]
    row_key = jnp.where(pad_row > 0, seg_row, -2.0)
    col_seg = cols[:high, 0:1]
    col_pad = cols[:high, 1:2]
    col_key = jnp.where(col_pad > 0, col_seg, -1.0)
    key_at = lax.broadcasted_iota(jnp.int32, (high, width), 0)
    query_at = lax.broadcasted_iota(jnp.int32, (high, width), 1) + low
    allowed = ((col_key == seg_row) & (key_at <= query_at)) | (key_at == query_at)
    picked = (col_key == row_key) & (key_at < query_at)
    return allowed, picked


def penalty_kernel(
    block, place, n1_own, n1_other, first, first_moved, seg_pad, n1_out, penalty, qk0, first_out
):
    seq = n1_out.shape[0]
    half = seq // 2
    core = place[0]
    n1_out[pl.ds(pl.multiple_of(core * half, half), half), :] = n1_own[...]
    n1_out[pl.ds(pl.multiple_of((1 - core) * half, half), half), :] = n1_other[...]

    @pl.when(place[1] == 0)
    def _():
        first_out[...] = first[...]

    @pl.when(place[1] != 0)
    def _():
        first_out[...] = first_moved[...]

    qk = dot(first_out[...], n1_out[...], TT)
    q0 = (qk[:HEAD_DIM].astype(BF16) * 0.125).astype(BF16)
    k0 = qk[HEAD_DIM:].astype(BF16)
    qk0[:HEAD_DIM, :] = q0
    qk0[HEAD_DIM:, :] = k0
    seg_value = seg_pad[...]
    cols = seg_value.T
    earlier = lax.broadcasted_iota(jnp.int32, (block, block + 128), 0)
    later = lax.broadcasted_iota(jnp.int32, (block, block + 128), 1)
    sums = ((earlier < later) | (later >= block)).astype(F32).astype(BF16)
    carry = jnp.zeros((seq, 128), F32)
    for low in range(0, seq, block):
        high = low + block
        allowed, picked = masks(seg_value, cols, low, high)
        score = dot(k0[:, :high], q0[:, low:high], TN)
        small = jnp.exp(-jnp.abs(score))
        log1p = jnp.where(small < 1e-3, small - 0.5 * small * small, jnp.log(1.0 + small))
        select = jnp.where(picked, jnp.maximum(score, 0.0) + log1p, 0.0).astype(BF16)
        total = dot(select, sums, NN)
        before = jnp.concatenate([carry[:high]] * (block // 128), axis=1)
        penalty[:high, low:high] = jnp.where(allowed, total[:, :block] + before, FAR)
        if high % FORWARD_BLOCK:
            edge = high + FORWARD_BLOCK - high % FORWARD_BLOCK
            penalty[high:edge, low:high] = jnp.full((edge - high, block), FAR, F32)
        carry = jnp.concatenate([carry[:high] + total[:, block:], carry[high:]], axis=0)


def penalty_call(order, place, n1_own, n1_other, first, first_moved, seg_pad, after=()):
    half, dim = n1_own.shape
    seq = 2 * half
    return order.run(
        6.5,
        functools.partial(penalty_kernel, 256),
        (place, n1_own, n1_other, first, first_moved, seg_pad),
        [
            sds((seq, dim), BF16),
            sds((seq, seq), F32),
            sds((2 * HEAD_DIM, seq), BF16),
            sds(first.shape, BF16),
        ],
        [SMEM] + [VMEM] * 5,
        after,
    )


def forward_kernel(block, last, *refs):
    if last:
        place, n1, near, far, penalty, out_l, w_l, w_r, *refs = refs
        qkv, out, lse, weights, own, send, out_r = refs
    else:
        n1, weights, penalty, qkv, out, lse = refs
    head = pl.program_id(0)
    third = qkv.shape[0] // 3
    seq = qkv.shape[1]

    @pl.when(head == 0)
    def _():
        if last:
            join(place[2], weights, near, far)
        product = dot(weights[...], n1[...], TT).astype(BF16)
        qkv[:third, :] = (product[:third] * 0.125).astype(BF16)
        qkv[third:, :] = product[third:]

    at = pl.multiple_of(head * HEAD_DIM, HEAD_DIM)
    query = qkv[pl.ds(at, HEAD_DIM), :]
    key = qkv[pl.ds(third + at, HEAD_DIM), :]
    value = qkv[pl.ds(2 * third + at, HEAD_DIM), :]
    value = jnp.concatenate([value, jnp.ones((16, seq), BF16)], axis=0)
    for low in range(0, seq, block):
        high = low + block
        logits = dot(key[:, :high], query[:, low:high], TN) - penalty[:high, low:high]
        largest = jnp.max(logits, axis=0, keepdims=True)
        weight = jnp.exp(logits - largest).astype(BF16)
        result = dot(value[:, :high], weight, NN)
        total = result[HEAD_DIM : HEAD_DIM + 1, :]
        out[:, low:high] = (result[:HEAD_DIM] / total).astype(BF16)
        lse[:, low:high] = largest + jnp.log(total)
    if last:
        out_r[pl.ds(at, HEAD_DIM), :] = out[...]

        @pl.when(head == pl.num_programs(0) - 1)
        def _():
            project(place, out_l, out_r, w_l, w_r, own, send)


def join(bit, out, near, far):
    half = near.shape[0]
    out[pl.ds(pl.multiple_of(bit * half, half), half), :] = near[...]
    out[pl.ds(pl.multiple_of((1 - bit) * half, half), half), :] = far[...]


def forward_call(order, n1, weights, penalty, place=None, others=(), after=()):
    seq, dim = n1.shape
    last = place is not None
    width = weights[0].shape[1]
    heads = width // (3 * HEAD_DIM)
    operands = ((place,) if last else ()) + (n1,) + tuple(weights) + (penalty,) + tuple(others)
    in_specs = [SMEM] if last else []
    in_specs += [whole(x.shape) for x in operands if x is not place]
    out_specs = [
        whole((width, seq)),
        pl.BlockSpec((HEAD_DIM, seq), lambda h: (h, 0)),
        pl.BlockSpec((None, 1, seq), lambda h: (h, 0, 0)),
    ]
    out_shape = [
        sds((width, seq), BF16),
        sds((heads * HEAD_DIM, seq), BF16),
        sds((heads, 1, seq), F32),
    ]
    scratch = []
    if last:
        out_specs += [whole((dim, width)), whole((seq // 2, dim)), whole((seq // 2, dim))]
        out_shape += [sds((dim, width), BF16), sds((seq // 2, dim), F32), sds((seq // 2, dim), BF16)]
        scratch.append(pltpu.VMEM((heads * HEAD_DIM, seq), BF16))
    return order.run(
        10,
        functools.partial(forward_kernel, FORWARD_BLOCK, last),
        operands,
        out_shape,
        in_specs,
        after,
        grid=(heads,),
        out_specs=out_specs,
        scratch_shapes=scratch,
    )


def project(place, out_l, out_r, w_l, w_r, own, send):
    half = own.shape[0]
    core = place[0]
    mixed = jnp.concatenate([w_l[...], w_r[...]], axis=0)

    def part(which):
        heads = jnp.concatenate([out_l[:, part_rows(which, half)], out_r[:, part_rows(which, half)]], axis=0)
        return dot(heads, mixed, TN)

    send[...] = part(1 - core).astype(BF16)
    own[...] = part(core)


def norm2_kernel(tokens, own, received, gain, shift, hidden, out):
    total = tokens[...].astype(F32) + (own[...] + received[...].astype(F32))
    hidden[...] = total
    scaled, _ = normalize(total)
    out[...] = (scaled * gain[...] + shift[...]).astype(BF16)


def norm2_call(order, tokens, own, received, gain, shift, after=()):
    size, dim = tokens.shape
    rows = rows_spec(size // 2, dim)
    vector = whole((1, dim))
    return order.run(
        4,
        norm2_kernel,
        (tokens, own, received, gain, shift),
        [sds(tokens.shape, F32), sds(tokens.shape, BF16)],
        [rows] * 3 + [vector] * 2,
        after,
        grid=(2,),
        out_specs=[rows, rows],
    )


def mlp_kernel(first, *refs):
    place, n2_other, n2_own, g_other, g_own, *refs = refs
    if first:
        w_up, w_down, *refs = refs
        before = (None,) * 4
    else:
        up_near, up_far, down_near, down_far, *refs = refs
        before, refs = refs[:4], refs[4:]
    outs, refs = refs[:4], refs[4:]
    count = 2 if first else 4
    parts, refs = refs[:count], refs[count:]
    if not first:
        w_up, w_down, *refs = refs
        join(place[2], w_up, up_near, up_far)
        join(place[2], w_down, down_near, down_far)
    actives, grad_ups, w_grads = refs
    size = n2_own.shape[0]

    def put(out, rows, value, more):
        out[rows, :] = (value if more is None else value + more[rows, :].astype(F32)).astype(out.dtype)

    block = min(256, size)
    for at, n2, g in ((0, n2_other, g_other), (1, n2_own, g_own)):

        def work(step, _):
            rows = part_rows(step, block)
            here = part_rows(step + at * (size // block), block)
            active, slope = gelu_pair(dot(n2[rows, :], w_up[...], NN))
            active = active.astype(BF16)
            grad_up = (dot(g[rows, :], w_down[...], NT) * slope).astype(BF16)
            actives[here, :] = active
            grad_ups[here, :] = grad_up
            put(outs[2 + at], rows, dot(grad_up, w_up[...], NT), before[2 + at])
            put(outs[at], rows, dot(active, w_down[...], NN), before[at])
            return 0

        lax.fori_loop(0, size // block, work, 0)
    w_grads[0] = (
        dot(n2_other[...], grad_ups[:size, :], TN) + dot(n2_own[...], grad_ups[size:, :], TN)
    ).astype(BF16)
    w_grads[1] = (
        dot(actives[:size, :], g_other[...], TN) + dot(actives[size:, :], g_own[...], TN)
    ).astype(BF16)
    if first:
        split(place, 0, w_grads, *parts)
    else:
        scatter(place, w_grads, parts)


def mlp_call(order, place, n2_other, n2_own, g_other, g_own, weights, before=(), after=()):
    size, dim = n2_own.shape
    first = not before
    units = weights[0].shape[1]
    count = 2 if first else 4
    sent = sds((size, dim), BF16)
    kept = sent
    rows = pltpu.VMEM((2 * size, units), BF16)
    scratch = [rows, rows, pltpu.VMEM((2, units, dim), BF16)]
    if not first:
        scratch = [pltpu.VMEM((dim, units), BF16), pltpu.VMEM((units, dim), BF16)] + scratch
    operands = (n2_other, n2_own, g_other, g_own, *weights, *before)
    return order.run(
        14.6,
        functools.partial(mlp_kernel, first),
        (place, *operands),
        [sent, kept, sent, kept] + [sds((2, units // count, dim), BF16)] * count,
        [SMEM] + [VMEM] * len(operands),
        after,
        scratch_shapes=scratch,
    )


def norm2_back_kernel(hidden, own, received, grad, gain, grad_hidden, low, sums):
    normed_grad = own[...].astype(F32) + received[...].astype(F32)
    scaled, inverse = normalize(hidden[...])
    total = grad[...].astype(F32) + norm_back(normed_grad, scaled, inverse, gain[...])
    grad_hidden[...] = total
    low[...] = total.astype(BF16)
    add_sums(sums, normed_grad, scaled)


def add_sums(sums, normed_grad, scaled):
    @pl.when(pl.program_id(0) == 0)
    def _():
        sums[...] = jnp.zeros(sums.shape, F32)

    sums[0:1, :] += jnp.sum(normed_grad * scaled, axis=0, keepdims=True)
    sums[1:2, :] += jnp.sum(normed_grad, axis=0, keepdims=True)


def norm2_back_call(order, hidden, own, received, grad, gain, after=()):
    size, dim = hidden.shape
    rows = rows_spec(size // 2, dim)
    return order.run(
        5,
        norm2_back_kernel,
        (hidden, own, received, grad, gain),
        [sds(hidden.shape, F32), sds(hidden.shape, BF16), sds((8, dim), F32)],
        [rows] * 4 + [whole((1, dim))],
        after,
        grid=(2,),
        out_specs=[rows, rows, whole((8, dim))],
    )


def half_sums_kernel(place, near, far, keep, send):
    half = keep.shape[1]
    for out, which in ((keep, place[3]), (send, 1 - place[3])):
        rows = part_rows(which, half)
        out[...] = low_sum(near[:, rows, :], far[:, rows, :])


def half_sums_call(order, place, near, far):
    groups, rows, dim = near.shape
    return order.run(
        3,
        half_sums_kernel,
        (place, near, far),
        [sds((groups, rows // 2, dim), BF16)] * 2,
        [SMEM] + [VMEM] * 2,
    )


def backward_kernel(first, block, *refs):
    place, g_own, g_other, w_out, heads_out, qkv, lse, penalty, *refs = refs
    if not first:
        before, *refs = refs
    grads, w_grad, logit_sum, grad_full, key_sum, value_sum, *refs = refs
    third = qkv.shape[0] // 3
    seq = qkv.shape[1]
    half = seq // 2
    total = logit_sum if first else refs[0]
    core = place[0]
    grad_full[part_rows(core, half), :] = g_own[...]
    grad_full[part_rows(1 - core, half), :] = g_other[...]
    whole_grad = grad_full[...]
    grad_heads = dot(w_out[...], whole_grad, NT).astype(BF16)
    w_grad[...] = dot(heads_out[...], whole_grad, NN).astype(BF16)
    heads = third // HEAD_DIM
    for head in range(heads):
        rows = slice(head * HEAD_DIM, (head + 1) * HEAD_DIM)
        query = qkv[rows, :]
        key = qkv[third + head * HEAD_DIM : third + (head + 1) * HEAD_DIM, :]
        value = qkv[2 * third + head * HEAD_DIM : 2 * third + (head + 1) * HEAD_DIM, :]
        grad = grad_heads[rows]
        for low in range(0, seq, block):
            high = low + block
            cols = slice(low, high)
            score = dot(key[:, :high], query[:, cols], TN)
            probs = jnp.exp(score - penalty[:high, cols] - lse[head, :, cols])
            grad_probs = dot(value[:, :high], grad[:, cols], TN)
            row_dot = jnp.sum(probs * grad_probs, axis=0, keepdims=True)
            grad_logits = probs * (grad_probs - row_dot)
            if head:
                sum_now = total[:high, cols] + grad_logits
            elif first:
                sum_now = grad_logits
            else:
                sum_now = before[:high, cols] + grad_logits
            if first or head < heads - 1:
                total[:high, cols] = sum_now
            else:
                logit_sum[:high, cols] = sum_now.astype(BF16)
            low_logits = grad_logits.astype(BF16)
            low_probs = probs.astype(BF16)
            grads[rows, cols] = (dot(key[:, :high], low_logits, NN) * 0.125).astype(BF16)
            value_new = dot(grad[:, cols], low_probs, NT)
            key_new = dot(query[:, cols], low_logits, NT)
            if low:
                key_sum[head, :, :low] += key_new[:, :low]
                value_sum[head, :, :low] += value_new[:, :low]
            key_sum[head, :, cols] = key_new[:, low:]
            value_sum[head, :, cols] = value_new[:, low:]
        at = third + head * HEAD_DIM
        grads[at : at + HEAD_DIM, :] = key_sum[head].astype(BF16)
        at = at + third
        grads[at : at + HEAD_DIM, :] = value_sum[head].astype(BF16)


def backward_call(order, place, g_own, g_other, w_out, heads_out, qkv, lse, penalty, before=None):
    width, seq = qkv.shape
    heads = width // (3 * HEAD_DIM)
    first = before is None
    operands = (g_own, g_other, w_out, heads_out, qkv, lse, penalty)
    operands += () if first else (before,)
    sums = pltpu.VMEM((heads, HEAD_DIM, seq), F32)
    scratch = [pltpu.VMEM((seq, g_own.shape[1]), BF16), sums, sums]
    scratch += [] if first else [pltpu.VMEM((seq, seq), F32)]
    return order.run(
        16,
        functools.partial(backward_kernel, first, 256),
        (place, *operands),
        [
            sds((width, seq), BF16),
            sds(w_out.shape, BF16),
            sds((seq, seq), F32 if first else BF16),
        ],
        [SMEM] + [VMEM] * len(operands),
        scratch_shapes=scratch,
    )


def halves(value):
    high = value.astype(BF16)
    return high, (value - high.astype(F32)).astype(BF16)


def select_back(block, core, own, received, qk0, seg_pad, n1, out, w_grad, total_grad):
    seq = own.shape[0]
    q0 = qk0[:HEAD_DIM, :]
    k0 = qk0[HEAD_DIM:, :]
    seg_value = seg_pad[...]
    cols = seg_value.T
    later = lax.broadcasted_iota(jnp.int32, (block, block + 128), 0)
    earlier = lax.broadcasted_iota(jnp.int32, (block, block + 128), 1)
    sums = ((later > earlier) | (earlier >= block)).astype(F32).astype(BF16)
    carry = jnp.zeros((seq, 128), F32)
    total_grad[...] = jnp.zeros(total_grad.shape, F32)
    for low in range(seq - block, -1, -block):
        high = low + block
        logit_sum = own[:high, low:high].astype(F32) + received[:high, low:high].astype(F32)
        top, bottom = halves(logit_sum)
        total = dot(top, sums, NN) + dot(bottom, sums, NN)
        after = jnp.concatenate([carry[:high]] * (block // 128), axis=1)
        select_grad = -(total[:, :block] + after)
        carry = carry[:high] + total[:, block:]
        _, picked = masks(seg_value, cols, low, high)
        score = dot(k0[:, :high], q0[:, low:high], TN)
        through = jnp.where(picked, select_grad / (1.0 + jnp.exp(-score)), 0.0)
        top, bottom = halves(through)

        @pl.when(core == 0)
        def _():
            total_grad[:, low:high] = 0.125 * (
                dot(k0[:, :high], top, NN) + dot(k0[:, :high], bottom, NN)
            )

        @pl.when(core == 1)
        def _():
            total_grad[:, :high] += dot(q0[:, low:high], top, NT) + dot(
                q0[:, low:high], bottom, NT
            )

    out[...] = total_grad[...].astype(BF16)
    w_grad[...] = dot(out[...], n1[...], NN).astype(BF16)


def weights_first_kernel(place, n1, grads, w_out, *refs):
    parts, total = refs[:4], refs[4]
    width = grads.shape[0]
    total[0, :width, :] = dot(grads[...], n1[...], NN).astype(BF16)
    total[0, width:, :] = w_out[...]
    scatter(place, total, parts)


def weights_first_call(order, place, n1, grads, w_out):
    dim = n1.shape[1]
    rows = grads.shape[0] + w_out.shape[0]
    return order.run(
        4,
        weights_first_kernel,
        (place, n1, grads, w_out),
        [sds((1, rows // 4, dim), BF16)] * 4,
        [SMEM] + [VMEM] * 3,
        scratch_shapes=[pltpu.VMEM((1, rows, dim), BF16)],
    )


def weights_second_kernel(place, n1, grads, w_out, *refs):
    parts_r, ff_terms, refs = refs[:4], refs[4:6], refs[6:]
    move_r, ff, *refs = refs
    parts, total = refs[:4], refs[4]
    width = grads.shape[0]
    move_r[...] = low_sum(*(part[...] for part in parts_r))
    ff[...] = low_sum(*(term[...] for term in ff_terms))
    total[0, :width, :] = dot(grads[...], n1[...], NN).astype(BF16)
    total[0, width:, :] = w_out[...]
    scatter(place, total, parts)


def weights_second_call(order, place, n1, grads, w_out, parts_r, ff_terms):
    dim = n1.shape[1]
    rows = grads.shape[0] + w_out.shape[0]
    part = sds((1, rows // 4, dim), BF16)
    return order.run(
        6,
        weights_second_kernel,
        (place, n1, grads, w_out, *parts_r, *ff_terms),
        [part, sds(ff_terms[0].shape, BF16)] + [part] * 4,
        [SMEM] + [VMEM] * 9,
        scratch_shapes=[pltpu.VMEM((1, rows, dim), BF16)],
    )


def norm1_grad_kernel(block, place, logit_own, logit_got, qk0, seg_pad, n1, grads, weights, first, *refs):
    grads_r, weights_r, gain, shift, sums2, own, send, late, extra, extra_w, total_grad = refs
    select_back(
        block, place[0], logit_own, logit_got, qk0, seg_pad, n1, extra, extra_w, total_grad
    )
    half = own.shape[0]
    mine = jnp.where(place[0] == 0, first[:, :HEAD_DIM], first[:, HEAD_DIM:])
    total = dot(grads[...], weights[...], TT) + dot(grads_r[...], weights_r[...], TT)
    total = total + dot(extra[...], mine, TT)
    for core in range(2):

        @pl.when(place[0] == core)
        def _():
            own[...] = total[core * half : (core + 1) * half]
            send[...] = total[(1 - core) * half : (2 - core) * half].astype(BF16)

    scaled = (n1[...].astype(F32) - shift[...]) * (1.0 / gain[...])
    gain_sum = jnp.sum(total * scaled, axis=0, keepdims=True)
    shift_sum = jnp.sum(total, axis=0, keepdims=True)
    norms = jnp.concatenate([gain_sum, shift_sum, sums2[0:2, :], sums2[4:8, :]], axis=0)
    rows = extra_w.shape[0]
    late[:rows, :] = extra_w[...]
    high, low = halves(norms)
    late[rows : rows + 8, :] = high
    late[rows + 8 :, :] = low


def norm1_grad_call(order, place, logits, qk0, seg_pad, n1, grads, weights, first, *rest):
    seq, dim = n1.shape
    rows = HEAD_DIM
    return order.run(
        14,
        functools.partial(norm1_grad_kernel, 256),
        (place, *logits, qk0, seg_pad, n1, grads, weights, first, *rest),
        [
            sds((seq // 2, dim), F32),
            sds((seq // 2, dim), BF16),
            sds((rows + 16, dim), BF16),
        ],
        [SMEM] + [VMEM] * 13,
        scratch_shapes=[
            pltpu.VMEM((rows, seq), BF16),
            pltpu.VMEM((rows, dim), BF16),
            pltpu.VMEM((rows, seq), F32),
        ],
    )


def results_kernel(tokens, own, received, grad_hidden, gain, hidden, mixed_own, mixed_received, out):
    mixed = hidden[...] + (mixed_own[...].astype(F32) + mixed_received[...].astype(F32))
    out[0] = mixed.astype(BF16)
    normed_grad = own[...] + received[...].astype(F32)
    scaled, inverse = normalize(tokens[...].astype(F32))
    total = grad_hidden[...] + norm_back(normed_grad, scaled, inverse, gain[...])
    out[1] = total.astype(BF16)


def results_call(order, tokens, own, received, grad_hidden, gain, hidden, mixed_own, mixed_received):
    size, dim = tokens.shape
    rows = rows_spec(size // 2, dim)
    return order.run(
        5,
        results_kernel,
        (tokens, own, received, grad_hidden, gain, hidden, mixed_own, mixed_received),
        sds((2, size, dim), BF16),
        [rows] * 4 + [whole((1, dim))] + [rows] * 3,
        grid=(2,),
        out_specs=pl.BlockSpec((2, size // 2, dim), lambda i: (0, i, 0)),
    )


def add_late(terms, out):
    def pairs(values):
        while len(values) > 1:
            values = [values[i] + values[i + 1] for i in range(0, len(values), 2)]
        return values[0]

    rows = out.shape[0] - 16
    out[:rows, :] = pairs([term[:rows, :].astype(F32) for term in terms]).astype(BF16)
    norms = pairs(
        [term[rows : rows + 8, :].astype(F32) + term[rows + 8 :, :].astype(F32) for term in terms]
    )
    high, low = halves(norms)
    out[rows : rows + 8, :] = high
    out[rows + 8 :, :] = low


def first_sums_kernel(*refs):
    near, far, *refs = refs
    *parts, ff, ff_move = refs
    ff[...] = low_sum(near[...], far[...])
    ff_move[...] = low_sum(*(part[...] for part in parts))


def first_sums_call(order, terms, parts):
    shape = sds(parts[0].shape, BF16)
    return order.run(3, first_sums_kernel, (*terms, *parts), [shape, shape])


def step0_kernel(own, got, out):
    out[...] = low_sum(own[...], got[...])


def step0_call(order, terms):
    return order.run(2, step0_kernel, terms, sds(terms[0].shape, BF16))


def step1_kernel(late_own, late_got, *refs):
    *at_terms, both = refs
    size = at_terms[0].shape[1]
    both[:size, :] = low_sum(*(term[0] for term in at_terms))
    add_late((late_own, late_got), both.at[size:, :])


def step1_call(order, late_terms, at_terms):
    _, size, dim = at_terms[0].shape
    rows = size + late_terms[0].shape[0]
    return order.run(3, step1_kernel, (*late_terms, *at_terms), sds((rows, dim), BF16))


def step2_kernel(size, place, own, got, *refs):
    *parts, both, ff = refs
    both[:size, :] = low_sum(own[:size, :], got[:size, :])
    add_late((own.at[size:, :], got.at[size:, :]), both.at[size:, :])
    gather(place, parts, ff)


def step2_call(order, place, size, own, got, parts):
    groups, rows, dim = parts[0].shape
    return order.run(
        4.5,
        functools.partial(step2_kernel, size),
        (place, own, got, *parts),
        [sds(own.shape, BF16), sds((groups, 4 * rows, dim), BF16)],
        [SMEM] + [VMEM] * 6,
    )


def step3_kernel(size, place, *refs):
    parts, refs = refs[:4], refs[4:]
    results, both, mixed_out, grad_out = refs
    for partner, part in enumerate(parts):
        both[part_rows(quarter(place) ^ partner, size), :] = part[:size, :]
    add_late([part.at[size:, :] for part in parts], both.at[4 * size :, :])
    mixed_out[...] = results[0]
    grad_out[...] = results[1]


def step3_call(order, place, size, parts, results):
    rows, dim = parts[0].shape
    half = sds(results.shape[1:], BF16)
    return order.run(
        3.5,
        functools.partial(step3_kernel, size),
        (place, *parts, results),
        [sds((rows + 3 * size, dim), BF16), half, half],
        [SMEM] + [VMEM] * 5,
    )


def finish_attention_kernel(place, near, far, w_query, w_key, w_value, w_out, *norms):
    width = w_out.shape[0] // 2
    late = 4 * width
    rows = late + HEAD_DIM
    total = jnp.zeros((8, near.shape[1]), F32)
    for ref in (near, far):
        total = total + (ref[rows : rows + 8, :].astype(F32) + ref[rows + 8 :, :].astype(F32))
    for i, out in enumerate(norms):
        out[...] = total[i]
    here = (place[1] == 0).astype(F32)
    for core in range(2):

        @pl.when(place[0] == core)
        def _():
            low, high = (near, far) if core == 0 else (far, near)
            for i, out in enumerate((w_query, w_key, w_value)):
                piece = slice(i * width, (i + 1) * width)
                part = low[piece, :].astype(F32)
                if i < 2:
                    more = here * (low, high)[i][late:rows, :].astype(F32)
                    part = jnp.concatenate([part[:HEAD_DIM] + more, part[HEAD_DIM:]], axis=0)
                out[...] = jnp.concatenate([part, high[piece, :].astype(F32)], axis=0).T
            w_out[:width, :] = low[3 * width : late, :].astype(F32)
            w_out[width:, :] = high[3 * width : late, :].astype(F32)


def finish_attention_call(order, place, width, near, far):
    dim = near.shape[1]
    return order.run(
        4.5,
        finish_attention_kernel,
        (place, near, far),
        [sds((dim, 2 * width), F32)] * 3 + [sds((2 * width, dim), F32)] + [sds((dim,), F32)] * 4,
        [SMEM] + [VMEM] * 2,
    )


def finish_mlp_kernel(place, near, far, w_up, w_down):
    units = near.shape[1]
    for core in range(2):

        @pl.when(place[0] == core)
        def _():
            low, high = (near, far) if core == 0 else (far, near)
            w_up[:, :units] = low[0].astype(F32)
            w_up[:, units:] = high[0].astype(F32)
            w_down[:units, :] = low[1].astype(F32)
            w_down[units:, :] = high[1].astype(F32)


def finish_mlp_call(order, place, near, far):
    _, units, dim = near.shape
    return order.run(
        6.8,
        finish_mlp_kernel,
        (place, near, far),
        [sds((dim, 2 * units), F32), sds((2 * units, dim), F32)],
        [SMEM] + [VMEM] * 2,
    )


def make_body(devices, parts):
    axes = ("dp", "tensor")
    chips = devices // 2
    in_order = [1 << bit for bit in range(chips.bit_length() - 1)]
    turned = [in_order[1], in_order[0], *in_order[2:]]
    rounds = len(in_order)
    rounds_more = range(3, rounds)

    def pairs(move):
        found = []
        for device in range(devices):
            for part in range(parts):
                to_chip, to_core, to_part = move(device // 2, device % 2, part)
                source = device * parts + part
                found.append((source, (to_chip * 2 + to_core) * parts + to_part))
        return found

    def by_bit(bit):
        return pairs(
            lambda chip, core, part: (chip ^ (turned if core else in_order)[bit], core, part)
        )

    by_role = pairs(lambda chip, core, part: (chip, part, core))
    by_core = pairs(lambda chip, core, part: (chip, 1 - core, part))
    by_part = pairs(lambda chip, core, part: (chip, core, 1 - part))
    from_first_part = [pair for pair in by_part if pair[0] % parts == 0]
    by_chip = [by_bit(bit) for bit in range(rounds)]

    def by_quarter(partner):
        def across(chip, core, part):
            for bit in range(2):
                if partner >> (1 - bit) & 1:
                    chip ^= (turned if core else in_order)[bit]
            return chip, core, part

        return pairs(across)

    def move(value, how):
        return lax.ppermute(value, axes, how)

    def add_more(value):
        for bit in rounds_more:
            other = move(value, by_chip[bit])
            value = (value.astype(F32) + other.astype(F32)).astype(value.dtype)
        return value

    def exchange(values):
        return [values[0]] + [move(values[i], by_quarter(i)) for i in range(1, 4)]

    def body(
        tokens,
        segment_ids,
        pad_mask,
        norm1_gain,
        norm1_shift,
        w_query,
        w_key,
        w_value,
        w_out,
        norm2_gain,
        norm2_shift,
        w_up,
        w_down,
        cotangent,
    ):
        order = Order()
        device = lax.axis_index("dp")
        part = lax.axis_index("tensor")
        core = device % 2
        chip = device // 2
        bits = [
            jnp.where(core == 1, (chip & turned[i]) != 0, (chip & in_order[i]) != 0)
            for i in range(rounds)
        ]
        place = jnp.stack([core, part] + bits).astype(jnp.int32)
        gain1, shift1, gain2, shift2 = (
            vector[None, :] for vector in (norm1_gain, norm1_shift, norm2_gain, norm2_shift)
        )

        mine = move(tokens, by_role)
        ints = jnp.concatenate([segment_ids, pad_mask], axis=0)
        ints = jnp.where(core == part, ints, move(ints, by_core)).astype(F32)
        seg_pad = jnp.concatenate([ints, jnp.zeros((6, ints.shape[1]), F32)], axis=0)

        qkv_l, qkv_s, first = pack_first_call(order, place, w_query, w_key, w_value)
        first_moved = move(first, from_first_part)
        qkv_near = move(qkv_s, by_part)
        n1_own = norm1_call(order, mine, gain1, shift1)
        n1_other = move(n1_own, by_core)
        out_l, up_l, up_s, down_l, down_s, grad = pack_last_call(
            order, place, w_out, w_up, w_down, cotangent
        )
        out_r = move(out_l, by_part)
        up_near = move(up_s, by_part)
        grad_own = move(grad, by_role)
        down_near = move(down_s, by_part)
        n1, penalty, qk0, first = penalty_call(
            order, place, n1_own, n1_other, first, first_moved, seg_pad
        )
        (qkv_near,) = order.hold((qkv_near,), (penalty,))
        qkv_far = move(qkv_near, by_chip[0])
        qkvt_l, heads_l, lse_l = forward_call(order, n1, (qkv_l,), penalty)
        qkvt_r, heads_r, lse_r, qkv_r, own, send = forward_call(
            order,
            n1,
            (qkv_near, qkv_far),
            penalty,
            place,
            (heads_l, out_l, out_r),
            (up_near,),
        )
        (send,) = order.hold((send,), (down_near,))
        (up_near,) = order.hold((up_near,), (lse_r,))
        up_far = move(up_near, by_chip[0])
        (grad_own,) = order.hold((grad_own,), (lse_r,))
        grad_other = move(grad_own, by_core)
        (down_near,) = order.hold((down_near,), (lse_r,))
        down_far = move(down_near, by_chip[0])
        hidden, n2_own = norm2_call(order, mine, own, move(send, by_core), gain2, shift2)
        n2_other = move(n2_own, by_core)
        *before, keep, send = mlp_call(
            order, place, n2_other, n2_own, grad_other, grad_own, (up_l, down_l)
        )
        got = move(send, by_chip[0])
        weights = (up_near, up_far, down_near, down_far)
        mixed_send, mixed_own, back_send, back_own, *ff_r = mlp_call(
            order, place, n2_other, n2_own, grad_other, grad_own, weights, before
        )
        back_send, *ff_r = order.hold((back_send, *ff_r), (got,))
        ff_r = exchange(ff_r)
        grad_hidden, low_own, sums2 = norm2_back_call(
            order, hidden, back_own, move(back_send, by_core), grad_own, gain2
        )
        low_other = move(low_own, by_core)
        keep, send = half_sums_call(order, place, keep, got)
        got = move(send, by_chip[1])

        low = (low_own, low_other)
        grads_r, wo_r, logit_sum = backward_call(
            order, place, *low, out_r, heads_r, qkvt_r, lse_r, penalty
        )
        at_r = weights_first_call(order, place, n1, grads_r, wo_r)
        ff, ff_move = first_sums_call(order, (keep, got), ff_r)
        ff_got = move(ff_move, by_part)
        at_r = exchange(at_r)
        grads_l, wo_l, logit_sum = backward_call(
            order, place, *low, out_l, heads_l, qkvt_l, lse_l, penalty, logit_sum
        )
        logit_got = move(logit_sum, by_core)
        at_r, ff, *at = weights_second_call(
            order, place, n1, grads_l, wo_l, at_r, (ff, ff_got)
        )
        at_r = move(at_r, by_part)
        ff_got = move(ff, by_chip[2])
        at = exchange(at)
        own, send, late = norm1_grad_call(
            order,
            place,
            (logit_sum, logit_got),
            qk0,
            seg_pad,
            n1,
            grads_l,
            qkv_l,
            first,
            grads_r,
            qkv_r,
            gain1,
            shift1,
            sums2,
        )
        send, late = order.hold((send, late), (*at, at_r))
        received = move(send, by_core)
        late_got = move(late, by_part)
        ff = step0_call(order, (ff, ff_got))
        ff = exchange([add_more(ff)] * 4)
        both = step1_call(order, (late, late_got), (*at, at_r))
        size = at_r.shape[1]
        both_got = move(both, by_chip[2])
        results = results_call(
            order,
            mine,
            own,
            received,
            grad_hidden,
            gain1,
            hidden,
            mixed_own,
            move(mixed_send, by_core),
        )
        (results,) = order.hold((results,), (both_got,))
        results = move(results, by_role)
        both, ff = step2_call(order, place, size, both, both_got, ff)
        both = exchange([add_more(both)] * 4)
        ff_far = move(ff, by_core)
        up_grad, down_grad = finish_mlp_call(order, place, ff, ff_far)
        both, mixed, tokens_grad = step3_call(order, place, size, both, results)
        query_grad, key_grad, value_grad, out_grad, *norms = finish_attention_call(
            order, place, size, both, move(both, by_core)
        )
        return (
            mixed,
            tokens_grad,
            norms[0],
            norms[1],
            query_grad,
            key_grad,
            value_grad,
            out_grad,
            norms[2],
            norms[3],
            up_grad,
            down_grad,
        )

    return body


def solution(mesh):
    in_specs = (
        P(("dp", "tensor"), None),
        P("dp", None),
        P("dp", None),
        P(),
        P(),
        P(None, "tensor"),
        P(None, "tensor"),
        P(None, "tensor"),
        P("tensor", None),
        P(),
        P(),
        P(None, "tensor"),
        P("tensor", None),
        P(("dp", "tensor"), None),
    )
    out_specs = (
        P(("dp", "tensor"), None),
        P(("dp", "tensor"), None),
        P(),
        P(),
        P(None, "tensor"),
        P(None, "tensor"),
        P(None, "tensor"),
        P("tensor", None),
        P(),
        P(),
        P(None, "tensor"),
        P("tensor", None),
    )
    body = make_body(mesh.shape["dp"], mesh.shape["tensor"])
    return jax.shard_map(body, mesh=mesh, in_specs=in_specs, out_specs=out_specs, check_vma=False)
```

profile of v0, /device:TPU:1, one launch (start us, length us, event | category | flops | bytes accessed | tf_op | source)
XLA Modules:
  0.0 293.5 jit_solution(999485985084261683)
XLA Ops:
  1.5 4.5 %collective-permute-start = (bf16[512,768]{1,0:T(8,128)(2,1)}, bf16[512,768]{1,0:T(8,128)(2,1)S(1)}, u32[]{:S(2)}, u32[]{:S(2)}) collective-permute-start(bf16[512,768]{1,0:T(8,128)(2,1)} %param.14), channel_id=1, source_target_pairs={{0,0},{1,2},{2,1},{3,3},{4,4},{5,6},{6,5},{7,7},{8,8},{9,10},{10,9... | collective-permute-start | bytes 2359304 | tf_op jit(solution)/shard_map/ppermute | solution.py:985
  6.7 3.1 %shard_map.229 = (bf16[768,576]{1,0:T(8,128)(2,1)}, bf16[384,576]{1,0:T(8,128)(2,1)}, bf16[768,128]{1,0:T(8,128)(2,1)}) custom-call(s32[5]{0:T(128)} %stack.35.refs_0_, bf16[768,384]{1,0:T(8,128)(2,1)} %refs_1_.2, bf16[768,384]{1,0:T(8,128)(2,1)} %refs_2_.2, bf16[768,384]{1,0:T(8,128)(2,1)} %refs_3_.2), custom_call_target="tpu_custom_call" | custom-call | flops 92000002048 | tf_op jit(solution)/shard_map/pallas_call | solution.py:60
  9.8 2.5 collective-permute-start.2
  14.1 3.3 %collective-permute-done.refs_0_ = bf16[512,768]{1,0:T(8,128)(2,1)S(1)} collective-permute-done((bf16[512,768]{1,0:T(8,128)(2,1)}, bf16[512,768]{1,0:T(8,128)(2,1)S(1)}, u32[]{:S(2)}, u32[]{:S(2)}) %collective-permute-start) | collective-permute-done | bytes 786464 | tf_op jit(solution)/shard_map/ppermute | solution.py:985
  17.4 0.9 copy-done.11
  18.3 2.6 shard_map.230.refs_5_.refs_1_
  20.9 5.1 %shard_map.231 = (bf16[192,768]{1,0:T(8,128)(2,1)}, bf16[768,768]{1,0:T(8,128)(2,1)}, bf16[384,768]{1,0:T(8,128)(2,1)}, bf16[768,768]{1,0:T(8,128)(2,1)}, bf16[3...) custom-call(s32[5]{0:T(128)} %stack.35.refs_0_, bf16[384,768]{1,0:T(8,128)(2,1)} %refs_1_.3, bf16[768,1536]{1,0:T(8,128)(2,1)} %refs_2_.3, ...), custom_call_target="tpu_custom_call" | custom-call | flops 115000000512 | tf_op jit(solution)/shard_map/pallas_call | solution.py:60
  26.0 2.5 collective-permute-start.6
  28.5 1.4 collective-permute-start.8
  29.9 2.4 collective-permute-start.11
  32.4 6.4 %shard_map.232 = (bf16[1024,768]{1,0:T(8,128)(2,1)}, f32[1024,1024]{1,0:T(8,128)}, bf16[128,1024]{1,0:T(8,128)(2,1)}, bf16[768,128]{1,0:T(8,128)(2,1)}) custom-call(s32[5]{0:T(128)} %stack.35.refs_0_, bf16[512,768]{1,0:T(8,128)(2,1)} %shard_map.230.refs_5_.refs_1_, bf16[512,768]{1,0:T(8,128)(2,1)} %copy-done.17, bf16[768,128]{1,0:T(8,128)(2,1)} %get-tuple-element.98.refs_3_, ...), custom_call_target="tpu_custom_call" | custom-call | flops 149500002304 | tf_op jit(solution)/shard_map/pallas_call | solution.py:60
  38.7 1.5 collective-permute-start.5
  40.3 9.6 %shard_map.234 = (bf16[576,1024]{1,0:T(8,128)(2,1)}, bf16[192,1024]{1,0:T(8,128)(2,1)}, f32[3,1,1024]{2,1,0:T(1,128)}) custom-call(bf16[1024,768]{1,0:T(8,128)(2,1)} %get-tuple-element.100.refs_0_.refs_1_.refs_5_, bf16[768,576]{1,0:T(8,128)(2,1)} %get-tuple-element.103.refs_1_.refs_7_, f32[1024,1024]{1,0:T(8,128)} %get-tuple-element.102.refs_1_.refs_2_.refs_4_.refs_7_, ...), custom_call_target="tpu_custom_call" | custom-call | flops 230000001024 | tf_op jit(solution)/shard_map/pallas_call | solution.py:60
  49.9 12.2 %shard_map.235 = (bf16[576,1024]{1,0:T(8,128)(2,1)}, bf16[192,1024]{1,0:T(8,128)(2,1)}, f32[3,1,1024]{2,1,0:T(1,128)}, bf16[768,576]{1,0:T(8,128)(2,1)}, f32[512,768]{1,0:T(8,128)}, /*index=5*/bf16[512,768]{1,0:T(8,128)(2,1)}) custom-call(s32[5]{0:T(128)} %stack.35.refs_0_, bf16[1024,768]{1,0:T(8,128)(2,1)} %get-tuple-element.100.refs_0_.refs_1_.refs_5_, ...), custom_call_target="tpu_custom_call" | custom-call | flops 230000001024 | tf_op jit(solution)/shard_map/pallas_call | solution.py:60
  62.2 5.4 %collective-permute-start.9 = (bf16[512,768]{1,0:T(8,128)(2,1)}, bf16[512,768]{1,0:T(8,128)(2,1)S(1)}, u32[]{:S(2)}, u32[]{:S(2)}) collective-permute-start(bf16[512,768]{1,0:T(8,128)(2,1)} %shard_map.236.refs_5_), channel_id=1, source_target_pairs={{0,2},{1,3},{2,0},{3,1},{4,6},{5,7},{6,4},{7,5},{8,10},{9,11},{10,... | collective-permute-start | bytes 2359304 | tf_op jit(solution)/shard_map/ppermute | solution.py:985
  68.7 1.3 collective-permute-done.11.refs_0_
  70.0 0.9 copy-done.20
  70.9 3.0 %shard_map.237 = (f32[512,768]{1,0:T(8,128)}, bf16[512,768]{1,0:T(8,128)(2,1)}) custom-call(bf16[512,768]{1,0:T(8,128)(2,1)} %copy-done.11, f32[512,768]{1,0:T(8,128)} %get-tuple-element.109.refs_1_, bf16[512,768]{1,0:T(8,128)(2,1)} %copy-done.20, f32[1,768]{1,0:T(1,128)} %broadcast_in_dim.15.refs_3_.refs_4_, f32[1,768]{1,0:T(1,128)} %broadcast_in_dim.16.refs_4_, ...), custom_call_target="tpu_custom_call" | custom-call | flops 92000002048 | tf_op jit(solution)/shard_map/pallas_call | solution.py:60
  74.4 1.3 collective-permute-start.13
  77.4 13.4 %shard_map.241 = (bf16[512,768]{1,0:T(8,128)(2,1)}, bf16[512,768]{1,0:T(8,128)(2,1)}, bf16[512,768]{1,0:T(8,128)(2,1)}, bf16[512,768]{1,0:T(8,128)(2,1)}, bf16[2...) custom-call(s32[5]{0:T(128)} %stack.35.refs_0_, bf16[512,768]{1,0:T(8,128)(2,1)} %copy-done.16, ...), custom_call_target="tpu_custom_call" | custom-call | flops 335800008704 | tf_op jit(solution)/shard_map/pallas_call | solution.py:60
  90.8 1.3 collective-permute-start.15
  92.1 27.1 %shard_map.242 = (bf16[512,768]{1,0:T(8,128)(2,1)}, bf16[512,768]{1,0:T(8,128)(2,1)}, bf16[512,768]{1,0:T(8,128)(2,1)}, bf16[512,768]{1,0:T(8,128)(2,1)}, bf16[2...) custom-call(s32[5]{0:T(128)} %stack.35.refs_0_, ...), custom_call_target="tpu_custom_call" | custom-call | flops 335800008704 | tf_op jit(solution)/shard_map/pallas_call | solution.py:60
  121.4 1.1 collective-permute-start.21
  122.5 0.9 copy-done.19
  123.4 4.1 %shard_map.244 = (f32[512,768]{1,0:T(8,128)}, bf16[512,768]{1,0:T(8,128)(2,1)}, f32[8,768]{1,0:T(8,128)}) custom-call(f32[512,768]{1,0:T(8,128)} %get-tuple-element.112.refs_0_.refs_5_, bf16[512,768]{1,0:T(8,128)(2,1)} %get-tuple-element.122.refs_1_, bf16[512,768]{1,0:T(8,128)(2,1)} %copy-done.19, bf16[512,768]{1,0:T(8,128)(2,1)} %shard_map.238.refs_4_.refs_3_, ...), custom_call_target="tpu_custom_call" | custom-call | flops 115000000512 | tf_op jit(solution)/shard_map/pallas_call | solution.py:60
  127.5 1.0 collective-permute-start.17
  128.5 2.8 shard_map.245
  131.3 1.1 collective-permute-start.18
  132.4 0.9 copy-done.13
  133.3 14.1 %shard_map.246 = (bf16[576,1024]{1,0:T(8,128)(2,1)}, bf16[192,768]{1,0:T(8,128)(2,1)}, f32[1024,1024]{1,0:T(8,128)}) custom-call(s32[5]{0:T(128)} %stack.35.refs_0_, bf16[512,768]{1,0:T(8,128)(2,1)} %get-tuple-element.130.refs_1_, bf16[512,768]{1,0:T(8,128)(2,1)} %copy-done.13, bf16[192,768]{1,0:T(8,128)(2,1)} %collective-permute-done.6.refs_7_.refs_3_, ...), custom_call_target="tpu_custom_call" | custom-call | flops 368000008192 | tf_op jit(solution)/shard_map/pallas_call | solution.py:60
  147.4 4.0 %shard_map.247 = (bf16[1,192,768]{2,1,0:T(8,128)(2,1)}, bf16[1,192,768]{2,1,0:T(8,128)(2,1)}, bf16[1,192,768]{2,1,0:T(8,128)(2,1)}, bf16[1,192,768]{2,1,0:T(8,128)(2,1)}) custom-call(s32[5]{0:T(128)} %stack.35.refs_0_, bf16[1024,768]{1,0:T(8,128)(2,1)} %get-tuple-element.100.refs_0_.refs_1_.refs_5_, bf16[576,1024]{1,0:T(8,128)(2,1)} %get-tuple-element.142.refs_2_.refs_9_, ...), custom_call_target="tpu_custom_call" | custom-call | flops 92000002048 | tf_op jit(solution)/shard_map/pallas_call | solution.py:60
  151.8 1.3 collective-permute-start.24
  153.1 1.0 collective-permute-start.25
  154.5 3.2 %shard_map.248 = (bf16[2,192,768]{2,1,0:T(8,128)(2,1)}, bf16[2,192,768]{2,1,0:T(8,128)(2,1)}) custom-call(bf16[2,192,768]{2,1,0:T(8,128)(2,1)} %get-tuple-element.138.refs_0_, bf16[2,192,768]{2,1,0:T(8,128)(2,1)} %collective-permute-done.18.refs_1_, bf16[2,192,768]{2,1,0:T(8,128)(2,1)} %get-tuple-element.139.refs_2_, ...), custom_call_target="tpu_custom_call" | custom-call | flops 69000003584 | tf_op jit(solution)/shard_map/pallas_call | solution.py:60
  157.7 2.4 collective-permute-start.26
  160.1 14.6 %shard_map.249 = (bf16[576,1024]{1,0:T(8,128)(2,1)}, bf16[192,768]{1,0:T(8,128)(2,1)}, bf16[1024,1024]{1,0:T(8,128)(2,1)}) custom-call(s32[5]{0:T(128)} %stack.35.refs_0_, bf16[512,768]{1,0:T(8,128)(2,1)} %get-tuple-element.130.refs_1_, bf16[512,768]{1,0:T(8,128)(2,1)} %copy-done.13, bf16[192,768]{1,0:T(8,128)(2,1)} %get-tuple-element.106.refs_6_.refs_3_, ...), custom_call_target="tpu_custom_call" | custom-call | flops 368000008192 | tf_op jit(solution)/shard_map/pallas_call | solution.py:60
  174.7 1.5 collective-permute-start.22
  176.2 5.0 %shard_map.250 = (bf16[1,192,768]{2,1,0:T(8,128)(2,1)}, bf16[2,192,768]{2,1,0:T(8,128)(2,1)}, bf16[1,192,768]{2,1,0:T(8,128)(2,1)}, bf16[1,192,768]{2,1,0:T(8,12...) custom-call(s32[5]{0:T(128)} %stack.35.refs_0_, ...), custom_call_target="tpu_custom_call" | custom-call | flops 138000007168 | tf_op jit(solution)/shard_map/pallas_call | solution.py:60
  182.9 1.1 collective-permute-start.29
  184.0 2.3 collective-permute-start.32
  186.3 13.4 %shard_map.251 = (f32[512,768]{1,0:T(8,128)}, bf16[512,768]{1,0:T(8,128)(2,1)}, bf16[80,768]{1,0:T(8,128)(2,1)}) custom-call(s32[5]{0:T(128)} %stack.35.refs_0_, bf16[1024,1024]{1,0:T(8,128)(2,1)} %get-tuple-element.146.refs_10_.refs_1_, bf16[1024,1024]{1,0:T(8,128)(2,1)} %copy-done.9, bf16[128,1024]{1,0:T(8,128)(2,1)} %get-tuple-element.147.refs_3_, ...), custom_call_target="tpu_custom_call" | custom-call | flops 321999994880 | tf_op jit(solution)/shard_map/pallas_call | solution.py:60
  199.6 3.3 %collective-permute-start.38 = (bf16[512,768]{1,0:T(8,128)(2,1)S(1)}, bf16[512,768]{1,0:T(8,128)(2,1)S(1)}, u32[]{:S(2)}, u32[]{:S(2)}) collective-permute-start(bf16[512,768]{1,0:T(8,128)(2,1)S(1)} %copy-done.12), channel_id=1, source_target_pairs={{0,2},{1,3},{2,0},{3,1},{4,6},{5,7},{6,4},{7,5},{8,10},{9,11},{10,... | collective-permute-start | bytes 2359304 | tf_op jit(solution)/shard_map/ppermute | solution.py:985
  203.0 6.5 %collective-permute-done.29.refs_5_ = bf16[1,192,768]{2,1,0:T(8,128)(2,1)} collective-permute-done((bf16[1,192,768]{2,1,0:T(8,128)(2,1)}, bf16[1,192,768]{2,1,0:T(8,128)(2,1)}, u32[]{:S(2)}, u32[]{:S(2)}) %collective-permute-start.29) | collective-permute-done | bytes 294944 | tf_op jit(solution)/shard_map/ppermute | solution.py:985
  209.6 2.3 shard_map.253.refs_7_.refs_3_
  211.8 3.0 %collective-permute-start.36 = (bf16[2,192,768]{2,1,0:T(8,128)(2,1)}, bf16[2,192,768]{2,1,0:T(8,128)(2,1)}, u32[]{:S(2)}, u32[]{:S(2)}) collective-permute-start(bf16[2,192,768]{2,1,0:T(8,128)(2,1)} %shard_map.253.refs_7_.refs_3_), channel_id=1, source_target_pairs={{0,12},{1,13},{2,14},{3,15},{4,8},{5,9},{6,10},{7,11},{8,4},{9,5},... | collective-permute-start | bytes 1769480 | tf_op jit(solution)/shard_map/ppermute | solution.py:985
  215.6 3.8 %collective-permute-start.37 = (bf16[512,768]{1,0:T(8,128)(2,1)S(1)}, bf16[512,768]{1,0:T(8,128)(2,1)S(1)}, u32[]{:S(2)}, u32[]{:S(2)}) collective-permute-start(bf16[512,768]{1,0:T(8,128)(2,1)S(1)} %copy-done), channel_id=1, source_target_pairs={{0,2},{1,3},{2,0},{3,1},{4,6},{5,7},{6,4},{7,5},{8,10},{9,11},{10,... | collective-permute-start | bytes 2359304 | tf_op jit(solution)/shard_map/ppermute | solution.py:985
  219.4 2.4 shard_map.254.refs_8_.refs_1_
  221.8 1.4 collective-permute-start.33
  223.1 0.9 copy-done.18
  224.0 5.1 %shard_map.255.refs_0_ = bf16[2,512,768]{2,1,0:T(8,128)(2,1)} custom-call(bf16[512,768]{1,0:T(8,128)(2,1)} %copy-done.11, f32[512,768]{1,0:T(8,128)} %get-tuple-element.164.refs_1_, bf16[512,768]{1,0:T(8,128)(2,1)} %copy-done.18, f32[512,768]{1,0:T(8,128)} %get-tuple-element.166.refs_3_, f32[1,768]{1,0:T(1,128)} %broadcast_in_dim.13.refs_1_.refs_11_.refs_4_, ...), custom_call_target="tpu_custom_call" | custom-call | flops 115000000512 | tf_op jit(solution)/shard_map/pallas_call | solution.py:60
  229.1 18.9 %collective-permute-done.33.refs_1_.refs_2_ = bf16[272,768]{1,0:T(8,128)(2,1)S(1)} collective-permute-done((bf16[272,768]{1,0:T(8,128)(2,1)}, bf16[272,768]{1,0:T(8,128)(2,1)S(1)}, u32[]{:S(2)}, u32[]{:S(2)}) %collective-permute-start.33) | collective-permute-done | bytes 417824 | tf_op jit(solution)/shard_map/ppermute | solution.py:985
  248.7 3.6 %shard_map.257 = (bf16[272,768]{1,0:T(8,128)(2,1)}, bf16[2,768,768]{2,1,0:T(8,128)(2,1)}) custom-call(s32[5]{0:T(128)} %stack.35.refs_0_, bf16[272,768]{1,0:T(8,128)(2,1)} %shard_map.254.refs_8_.refs_1_, bf16[272,768]{1,0:T(8,128)(2,1)} %copy-done.1, bf16[2,192,768]{2,1,0:T(8,128)(2,1)} %shard_map.253.refs_7_.refs_3_, ...), custom_call_target="tpu_custom_call" | custom-call | flops 103499997184 | tf_op jit(solution)/shard_map/pallas_call | solution.py:60
  252.3 2.4 collective-permute-start.43
  254.7 3.3 %collective-permute-start.41 = (bf16[272,768]{1,0:T(8,128)(2,1)}, bf16[272,768]{1,0:T(8,128)(2,1)}, u32[]{:S(2)}, u32[]{:S(2)}) collective-permute-start(bf16[272,768]{1,0:T(8,128)(2,1)} %get-tuple-element.169.refs_1_), channel_id=1, source_target_pairs={{0,12},{1,13},{2,14},{3,15},{4,8},{5,9},{6,10},{7,11},{8,4},{9,5},... | collective-permute-start | bytes 1253384 | tf_op jit(solution)/shard_map/ppermute | solution.py:985
  258.2 4.1 %collective-permute-start.42 = (bf16[2,512,768]{2,1,0:T(8,128)(2,1)}, bf16[2,512,768]{2,1,0:T(8,128)(2,1)}, u32[]{:S(2)}, u32[]{:S(2)}) collective-permute-start(bf16[2,512,768]{2,1,0:T(8,128)(2,1)} %shard_map.256.refs_7_), channel_id=1, source_target_pairs={{0,0},{1,2},{2,1},{3,3},{4,4},{5,6},{6,5},{7,7},{8,8},{9,10},{10,9... | collective-permute-start | bytes 4718600 | tf_op jit(solution)/shard_map/ppermute | solution.py:985
  262.4 1.5 copy-done.8
  263.9 6.7 %shard_map.258 = (f32[768,1536]{1,0:T(8,128)}, f32[1536,768]{1,0:T(8,128)}) custom-call(s32[5]{0:T(128)} %stack.35.refs_0_, bf16[2,768,768]{2,1,0:T(8,128)(2,1)} %get-tuple-element.170.refs_1_.refs_3_, bf16[2,768,768]{2,1,0:T(8,128)(2,1)} %copy-done.8, bf16[2,768,768]{2,1,0:T(8,128)(2,1)} %get-tuple-element.170.refs_1_.refs_3_), custom_call_target="tpu_custom_call" | custom-call | flops 156399992832 | tf_op jit(solution)/shard_map/pallas_call | solution.py:60
  270.6 5.7 %collective-permute-done.40.refs_3_ = bf16[272,768]{1,0:T(8,128)(2,1)} collective-permute-done((bf16[272,768]{1,0:T(8,128)(2,1)}, bf16[272,768]{1,0:T(8,128)(2,1)}, u32[]{:S(2)}, u32[]{:S(2)}) %collective-permute-start.40) | collective-permute-done | bytes 417824 | tf_op jit(solution)/shard_map/ppermute | solution.py:985
  276.3 1.0 collective-permute-done.39.refs_2_
  277.4 3.4 %collective-permute-done.42.refs_5_ = bf16[2,512,768]{2,1,0:T(8,128)(2,1)} collective-permute-done((bf16[2,512,768]{2,1,0:T(8,128)(2,1)}, bf16[2,512,768]{2,1,0:T(8,128)(2,1)}, u32[]{:S(2)}, u32[]{:S(2)}) %collective-permute-start.42) | collective-permute-done | bytes 1572896 | tf_op jit(solution)/shard_map/ppermute | solution.py:985
  280.8 3.6 %shard_map.259 = (bf16[848,768]{1,0:T(8,128)(2,1)}, bf16[512,768]{1,0:T(8,128)(2,1)}, bf16[512,768]{1,0:T(8,128)(2,1)}) custom-call(s32[5]{0:T(128)} %stack.35.refs_0_, bf16[272,768]{1,0:T(8,128)(2,1)} %get-tuple-element.169.refs_1_, bf16[272,768]{1,0:T(8,128)(2,1)} %collective-permute-done.39.refs_2_, bf16[272,768]{1,0:T(8,128)(2,1)} %collective-permute-done.40.refs_3_, ...), custom_call_target="tpu_custom_call" | custom-call | flops 80499998720 | tf_op jit(solution)/shard_map/pallas_call | solution.py:60
  284.4 3.2 %collective-permute-done.44.refs_2_ = bf16[848,768]{1,0:T(8,128)(2,1)S(1)} collective-permute-done((bf16[848,768]{1,0:T(8,128)(2,1)}, bf16[848,768]{1,0:T(8,128)(2,1)S(1)}, u32[]{:S(2)}, u32[]{:S(2)}) %collective-permute-start.44) | collective-permute-done | bytes 1302560 | tf_op jit(solution)/shard_map/ppermute | solution.py:985
  287.7 1.1 copy-done.10
  288.7 4.6 %shard_map.260 = (f32[768,384]{1,0:T(8,128)}, f32[768,384]{1,0:T(8,128)}, f32[768,384]{1,0:T(8,128)}, f32[384,768]{1,0:T(8,128)}, f32[768]{0:T(1024)}, /*index=5*/f32[768]{0:T(1024)}, f32[768]{0:T(1024)}, f32[768]{0:T(1024)}) custom-call(s32[5]{0:T(128)} %stack.35.refs_0_, bf16[848,768]{1,0:T(8,128)(2,1)} %get-tuple-element.174.refs_1_, ...), custom_call_target="tpu_custom_call" | custom-call | flops 103499997184 | tf_op jit(solution)/shard_map/pallas_call | solution.py:60
  (110 shorter events, 13.4 us)
Async XLA Ops:
  1.4 12.1 %collective-permute-start.3 = (s32[2,1024]{1,0:T(2,128)S(1)}, s32[2,1024]{1,0:T(2,128)S(1)}, u32[]{:S(2)}, u32[]{:S(2)}) collective-permute-start(s32[2,1024]{1,0:T(2,128)S(1)} %pad_add_fusion), channel_id=1, source_target_pairs={{0,2},{1,3},{2,0},{3,1},{4,6},{5,7},{6,4},{7,5},{8,10},{9,11},{10,... | collective-permute-start | bytes 24584 | tf_op jit(solution)/shard_map/ppermute | solution.py:985
  1.5 15.9 %collective-permute-start = (bf16[512,768]{1,0:T(8,128)(2,1)}, bf16[512,768]{1,0:T(8,128)(2,1)S(1)}, u32[]{:S(2)}, u32[]{:S(2)}) collective-permute-start(bf16[512,768]{1,0:T(8,128)(2,1)} %param.14), channel_id=1, source_target_pairs={{0,0},{1,2},{2,1},{3,3},{4,4},{5,6},{6,5},{7,7},{8,8},{9,10},{10,9... | collective-permute-start | bytes 2359304 | tf_op jit(solution)/shard_map/ppermute | solution.py:985
  6.7 5.6 %copy-start.4 = (f32[768]{0:T(1024)S(1)}, f32[768]{0:T(1024)}, u32[]{:S(2)}) copy-start(f32[768]{0:T(1024)} %param.17) | copy-start | bytes 9220
  6.7 6.2 %copy-start.5 = (f32[768]{0:T(1024)S(1)}, f32[768]{0:T(1024)}, u32[]{:S(2)}) copy-start(f32[768]{0:T(1024)} %param.18) | copy-start | bytes 9220
  6.7 6.8 %copy-start.2 = (s32[1,1024]{1,0:T(1,128)S(1)}, s32[1,1024]{1,0:T(1,128)}, u32[]{:S(2)}) copy-start(s32[1,1024]{1,0:T(1,128)} %param.16) | copy-start | bytes 12292
  6.7 6.8 %copy-start.3 = (s32[1,1024]{1,0:T(1,128)S(1)}, s32[1,1024]{1,0:T(1,128)}, u32[]{:S(2)}) copy-start(s32[1,1024]{1,0:T(1,128)} %param.15) | copy-start | bytes 12292
  9.8 18.7 %collective-permute-start.2 = (bf16[768,128]{1,0:T(8,128)(2,1)}, bf16[768,128]{1,0:T(8,128)(2,1)}, u32[]{:S(2)}, u32[]{:S(2)}) collective-permute-start(bf16[768,128]{1,0:T(8,128)(2,1)} %get-tuple-element.98.refs_3_), channel_id=1, source_target_pairs={{0,1},{2,3},{4,5},{6,7},{8,9},{10,11},{12,13},{14,15},{16,17},{18,... | collective-permute-start | bytes 589832 | tf_op jit(solution)/shard_map/ppermute | solution.py:985
  12.3 26.4 %collective-permute-start.4 = (bf16[384,576]{1,0:T(8,128)(2,1)}, bf16[384,576]{1,0:T(8,128)(2,1)}, u32[]{:S(2)}, u32[]{:S(2)}) collective-permute-start(bf16[384,576]{1,0:T(8,128)(2,1)} %get-tuple-element.101), channel_id=1, source_target_pairs={{0,1},{1,0},{2,3},{3,2},{4,5},{5,4},{6,7},{7,6},{8,9},{9,8},{10,11... | collective-permute-start | bytes 1327112 | tf_op jit(solution)/shard_map/ppermute | solution.py:985
  17.4 0.9 copy-start.11
  20.9 9.1 %collective-permute-start.1 = (bf16[512,768]{1,0:T(8,128)(2,1)}, bf16[512,768]{1,0:T(8,128)(2,1)S(1)}, u32[]{:S(2)}, u32[]{:S(2)}) collective-permute-start(bf16[512,768]{1,0:T(8,128)(2,1)} %shard_map.230.refs_5_.refs_1_), channel_id=1, source_target_pairs={{0,2},{1,3},{2,0},{3,1},{4,6},{5,7},{6,4},{7,5},{8,10},{9,11},{10,... | collective-permute-start | bytes 2359304 | tf_op jit(solution)/shard_map/ppermute | solution.py:985
  26.0 23.9 %collective-permute-start.6 = (bf16[192,768]{1,0:T(8,128)(2,1)}, bf16[192,768]{1,0:T(8,128)(2,1)}, u32[]{:S(2)}, u32[]{:S(2)}) collective-permute-start(bf16[192,768]{1,0:T(8,128)(2,1)} %get-tuple-element.106.refs_6_.refs_3_), channel_id=1, source_target_pairs={{0,1},{1,0},{2,3},{3,2},{4,5},{5,4},{6,7},{7,6},{8,9},{9,8},{10,11... | collective-permute-start | bytes 884744 | tf_op jit(solution)/shard_map/ppermute | solution.py:985
  28.5 21.4 %collective-permute-start.7 = (bf16[384,768]{1,0:T(8,128)(2,1)}, bf16[384,768]{1,0:T(8,128)(2,1)}, u32[]{:S(2)}, u32[]{:S(2)}) collective-permute-start(bf16[384,768]{1,0:T(8,128)(2,1)} %get-tuple-element.107), channel_id=1, source_target_pairs={{0,1},{1,0},{2,3},{3,2},{4,5},{5,4},{6,7},{7,6},{8,9},{9,8},{10,11... | collective-permute-start | bytes 1769480 | tf_op jit(solution)/shard_map/ppermute | solution.py:985
  28.5 33.6 %collective-permute-start.8 = (bf16[384,768]{1,0:T(8,128)(2,1)}, bf16[384,768]{1,0:T(8,128)(2,1)}, u32[]{:S(2)}, u32[]{:S(2)}) collective-permute-start(bf16[384,768]{1,0:T(8,128)(2,1)} %get-tuple-element.111), channel_id=1, source_target_pairs={{0,1},{1,0},{2,3},{3,2},{4,5},{5,4},{6,7},{7,6},{8,9},{9,8},{10,11... | collective-permute-start | bytes 1769480 | tf_op jit(solution)/shard_map/ppermute | solution.py:985
  29.9 2.4 copy-start.17
  29.9 40.0 %collective-permute-start.11 = (bf16[512,768]{1,0:T(8,128)(2,1)}, bf16[512,768]{1,0:T(8,128)(2,1)}, u32[]{:S(2)}, u32[]{:S(2)}) collective-permute-start(bf16[512,768]{1,0:T(8,128)(2,1)} %get-tuple-element.99.refs_6_), channel_id=1, source_target_pairs={{0,0},{1,2},{2,1},{3,3},{4,4},{5,6},{6,5},{7,7},{8,8},{9,10},{10,9... | collective-permute-start | bytes 2359304 | tf_op jit(solution)/shard_map/ppermute | solution.py:985
  38.7 11.2 %collective-permute-start.5 = (bf16[384,576]{1,0:T(8,128)(2,1)}, bf16[384,576]{1,0:T(8,128)(2,1)}, u32[]{:S(2)}, u32[]{:S(2)}) collective-permute-start(bf16[384,576]{1,0:T(8,128)(2,1)} %shard_map.233.refs_2_), channel_id=1, source_target_pairs={{0,4},{1,5},{2,10},{3,11},{4,0},{5,1},{6,14},{7,15},{8,12},{9,13},... | collective-permute-start | bytes 1327112 | tf_op jit(solution)/shard_map/ppermute | solution.py:985
  62.1 5.4 %copy-start.6 = (f32[768]{0:T(1024)S(1)}, f32[768]{0:T(1024)}, u32[]{:S(2)}) copy-start(f32[768]{0:T(1024)} %param.23) | copy-start | bytes 9220
  62.1 6.0 %copy-start.7 = (f32[768]{0:T(1024)S(1)}, f32[768]{0:T(1024)}, u32[]{:S(2)}) copy-start(f32[768]{0:T(1024)} %param.24) | copy-start | bytes 9220
  62.2 7.8 %collective-permute-start.9 = (bf16[512,768]{1,0:T(8,128)(2,1)}, bf16[512,768]{1,0:T(8,128)(2,1)S(1)}, u32[]{:S(2)}, u32[]{:S(2)}) collective-permute-start(bf16[512,768]{1,0:T(8,128)(2,1)} %shard_map.236.refs_5_), channel_id=1, source_target_pairs={{0,2},{1,3},{2,0},{3,1},{4,6},{5,7},{6,4},{7,5},{8,10},{9,11},{10,... | collective-permute-start | bytes 2359304 | tf_op jit(solution)/shard_map/ppermute | solution.py:985
  70.0 5.9 %collective-permute-start.12 = (bf16[512,768]{1,0:T(8,128)(2,1)}, bf16[512,768]{1,0:T(8,128)(2,1)S(1)}, u32[]{:S(2)}, u32[]{:S(2)}) collective-permute-start(bf16[512,768]{1,0:T(8,128)(2,1)} %shard_map.238.refs_4_.refs_3_), channel_id=1, source_target_pairs={{0,2},{1,3},{2,0},{3,1},{4,6},{5,7},{6,4},{7,5},{8,10},{9,11},{10,... | collective-permute-start | bytes 2359304 | tf_op jit(solution)/shard_map/ppermute | solution.py:985
  73.9 2.6 collective-permute-start.10
  74.4 17.7 %collective-permute-start.13 = (bf16[384,768]{1,0:T(8,128)(2,1)}, bf16[384,768]{1,0:T(8,128)(2,1)}, u32[]{:S(2)}, u32[]{:S(2)}) collective-permute-start(bf16[384,768]{1,0:T(8,128)(2,1)} %shard_map.239.refs_5_), channel_id=1, source_target_pairs={{0,4},{1,5},{2,10},{3,11},{4,0},{5,1},{6,14},{7,15},{8,12},{9,13},... | collective-permute-start | bytes 1769480 | tf_op jit(solution)/shard_map/ppermute | solution.py:985
  75.7 16.4 %collective-permute-start.14 = (bf16[384,768]{1,0:T(8,128)(2,1)}, bf16[384,768]{1,0:T(8,128)(2,1)}, u32[]{:S(2)}, u32[]{:S(2)}) collective-permute-start(bf16[384,768]{1,0:T(8,128)(2,1)} %shard_map.240.refs_7_), channel_id=1, source_target_pairs={{0,4},{1,5},{2,10},{3,11},{4,0},{5,1},{6,14},{7,15},{8,12},{9,13},... | collective-permute-start | bytes 1769480 | tf_op jit(solution)/shard_map/ppermute | solution.py:985
  76.5 0.9 copy-start.16
  90.8 28.5 %collective-permute-start.15 = (bf16[2,384,768]{2,1,0:T(8,128)(2,1)}, bf16[2,384,768]{2,1,0:T(8,128)(2,1)}, u32[]{:S(2)}, u32[]{:S(2)}) collective-permute-start(bf16[2,384,768]{2,1,0:T(8,128)(2,1)} %get-tuple-element.121.refs_13_), channel_id=1, source_target_pairs={{0,4},{1,5},{2,10},{3,11},{4,0},{5,1},{6,14},{7,15},{8,12},{9,13},... | collective-permute-start | bytes 3538952 | tf_op jit(solution)/shard_map/ppermute | solution.py:985
  119.2 3.3 %collective-permute-start.16 = (bf16[512,768]{1,0:T(8,128)(2,1)}, bf16[512,768]{1,0:T(8,128)(2,1)S(1)}, u32[]{:S(2)}, u32[]{:S(2)}) collective-permute-start(bf16[512,768]{1,0:T(8,128)(2,1)} %get-tuple-element.128), channel_id=1, source_target_pairs={{0,2},{1,3},{2,0},{3,1},{4,6},{5,7},{6,4},{7,5},{8,10},{9,11},{10,... | collective-permute-start | bytes 2359304 | tf_op jit(solution)/shard_map/ppermute | solution.py:985
  119.9 31.9 %collective-permute-start.19 = (bf16[2,192,768]{2,1,0:T(8,128)(2,1)}, bf16[2,192,768]{2,1,0:T(8,128)(2,1)}, u32[]{:S(2)}, u32[]{:S(2)}) collective-permute-start(bf16[2,192,768]{2,1,0:T(8,128)(2,1)} %get-tuple-element.140), channel_id=1, source_target_pairs={{0,8},{1,9},{2,6},{3,7},{4,12},{5,13},{6,2},{7,3},{8,0},{9,1},{10,... | collective-permute-start | bytes 1769480 | tf_op jit(solution)/shard_map/ppermute | solution.py:985
  120.6 32.5 %collective-permute-start.20 = (bf16[2,192,768]{2,1,0:T(8,128)(2,1)}, bf16[2,192,768]{2,1,0:T(8,128)(2,1)}, u32[]{:S(2)}, u32[]{:S(2)}) collective-permute-start(bf16[2,192,768]{2,1,0:T(8,128)(2,1)} %get-tuple-element.141), channel_id=1, source_target_pairs={{0,4},{1,5},{2,10},{3,11},{4,0},{5,1},{6,14},{7,15},{8,12},{9,13},... | collective-permute-start | bytes 1769480 | tf_op jit(solution)/shard_map/ppermute | solution.py:985
  121.4 32.6 %collective-permute-start.21 = (bf16[2,192,768]{2,1,0:T(8,128)(2,1)}, bf16[2,192,768]{2,1,0:T(8,128)(2,1)}, u32[]{:S(2)}, u32[]{:S(2)}) collective-permute-start(bf16[2,192,768]{2,1,0:T(8,128)(2,1)} %get-tuple-element.129.refs_5_), channel_id=1, source_target_pairs={{0,12},{1,13},{2,14},{3,15},{4,8},{5,9},{6,10},{7,11},{8,4},{9,5},... | collective-permute-start | bytes 1769480 | tf_op jit(solution)/shard_map/ppermute | solution.py:985
  122.5 0.9 copy-start.19
  127.5 4.9 %collective-permute-start.17 = (bf16[512,768]{1,0:T(8,128)(2,1)}, bf16[512,768]{1,0:T(8,128)(2,1)S(1)}, u32[]{:S(2)}, u32[]{:S(2)}) collective-permute-start(bf16[512,768]{1,0:T(8,128)(2,1)} %get-tuple-element.130.refs_1_), channel_id=1, source_target_pairs={{0,2},{1,3},{2,0},{3,1},{4,6},{5,7},{6,4},{7,5},{8,10},{9,11},{10,... | collective-permute-start | bytes 2359304 | tf_op jit(solution)/shard_map/ppermute | solution.py:985
  131.3 23.1 %collective-permute-start.18 = (bf16[2,192,768]{2,1,0:T(8,128)(2,1)}, bf16[2,192,768]{2,1,0:T(8,128)(2,1)}, u32[]{:S(2)}, u32[]{:S(2)}) collective-permute-start(bf16[2,192,768]{2,1,0:T(8,128)(2,1)} %get-tuple-element.136.refs_8_), channel_id=1, source_target_pairs={{0,8},{1,9},{2,6},{3,7},{4,12},{5,13},{6,2},{7,3},{8,0},{9,1},{10,... | collective-permute-start | bytes 1769480 | tf_op jit(solution)/shard_map/ppermute | solution.py:985
  132.4 0.9 copy-start.13
  151.4 24.8 %collective-permute-start.23 = (bf16[1,192,768]{2,1,0:T(8,128)(2,1)}, bf16[1,192,768]{2,1,0:T(8,128)(2,1)}, u32[]{:S(2)}, u32[]{:S(2)}) collective-permute-start(bf16[1,192,768]{2,1,0:T(8,128)(2,1)} %get-tuple-element.152), channel_id=1, source_target_pairs={{0,8},{1,9},{2,6},{3,7},{4,12},{5,13},{6,2},{7,3},{8,0},{9,1},{10,... | collective-permute-start | bytes 884744 | tf_op jit(solution)/shard_map/ppermute | solution.py:985
  151.8 24.4 %collective-permute-start.24 = (bf16[1,192,768]{2,1,0:T(8,128)(2,1)}, bf16[1,192,768]{2,1,0:T(8,128)(2,1)}, u32[]{:S(2)}, u32[]{:S(2)}) collective-permute-start(bf16[1,192,768]{2,1,0:T(8,128)(2,1)} %get-tuple-element.153), channel_id=1, source_target_pairs={{0,4},{1,5},{2,10},{3,11},{4,0},{5,1},{6,14},{7,15},{8,12},{9,13},... | collective-permute-start | bytes 884744 | tf_op jit(solution)/shard_map/ppermute | solution.py:985
  153.1 23.1 %collective-permute-start.25 = (bf16[1,192,768]{2,1,0:T(8,128)(2,1)}, bf16[1,192,768]{2,1,0:T(8,128)(2,1)}, u32[]{:S(2)}, u32[]{:S(2)}) collective-permute-start(bf16[1,192,768]{2,1,0:T(8,128)(2,1)} %get-tuple-element.144.refs_6_), channel_id=1, source_target_pairs={{0,12},{1,13},{2,14},{3,15},{4,8},{5,9},{6,10},{7,11},{8,4},{9,5},... | collective-permute-start | bytes 884744 | tf_op jit(solution)/shard_map/ppermute | solution.py:985
  157.7 18.5 %collective-permute-start.26 = (bf16[2,192,768]{2,1,0:T(8,128)(2,1)}, bf16[2,192,768]{2,1,0:T(8,128)(2,1)}, u32[]{:S(2)}, u32[]{:S(2)}) collective-permute-start(bf16[2,192,768]{2,1,0:T(8,128)(2,1)} %get-tuple-element.145.refs_9_), channel_id=1, source_target_pairs={{0,1},{1,0},{2,3},{3,2},{4,5},{5,4},{6,7},{7,6},{8,9},{9,8},{10,11... | collective-permute-start | bytes 1769480 | tf_op jit(solution)/shard_map/ppermute | solution.py:985
  174.7 9.3 %collective-permute-start.22 = (bf16[1024,1024]{1,0:T(8,128)(2,1)}, bf16[1024,1024]{1,0:T(8,128)(2,1)S(1)}, u32[]{:S(2)}, u32[]{:S(2)}) collective-permute-start(bf16[1024,1024]{1,0:T(8,128)(2,1)} %get-tuple-element.146.refs_10_.refs_1_), channel_id=1, source_target_pairs={{0,2},{1,3},{2,0},{3,1},{4,6},{5,7},{6,4},{7,5},{8,10},{9,11},{10,... | collective-permute-start | bytes 6291464 | tf_op jit(solution)/shard_map/ppermute | solution.py:985
  181.2 18.4 %collective-permute-start.27 = (bf16[1,192,768]{2,1,0:T(8,128)(2,1)}, bf16[1,192,768]{2,1,0:T(8,128)(2,1)}, u32[]{:S(2)}, u32[]{:S(2)}) collective-permute-start(bf16[1,192,768]{2,1,0:T(8,128)(2,1)} %get-tuple-element.159), channel_id=1, source_target_pairs={{0,8},{1,9},{2,6},{3,7},{4,12},{5,13},{6,2},{7,3},{8,0},{9,1},{10,... | collective-permute-start | bytes 884744 | tf_op jit(solution)/shard_map/ppermute | solution.py:985
  182.0 21.0 %collective-permute-start.28 = (bf16[1,192,768]{2,1,0:T(8,128)(2,1)}, bf16[1,192,768]{2,1,0:T(8,128)(2,1)}, u32[]{:S(2)}, u32[]{:S(2)}) collective-permute-start(bf16[1,192,768]{2,1,0:T(8,128)(2,1)} %get-tuple-element.160), channel_id=1, source_target_pairs={{0,4},{1,5},{2,10},{3,11},{4,0},{5,1},{6,14},{7,15},{8,12},{9,13},... | collective-permute-start | bytes 884744 | tf_op jit(solution)/shard_map/ppermute | solution.py:985
  182.9 20.1 %collective-permute-start.30 = (bf16[1,192,768]{2,1,0:T(8,128)(2,1)}, bf16[1,192,768]{2,1,0:T(8,128)(2,1)}, u32[]{:S(2)}, u32[]{:S(2)}) collective-permute-start(bf16[1,192,768]{2,1,0:T(8,128)(2,1)} %get-tuple-element.161), channel_id=1, source_target_pairs={{0,1},{1,0},{2,3},{3,2},{4,5},{5,4},{6,7},{7,6},{8,9},{9,8},{10,11... | collective-permute-start | bytes 884744 | tf_op jit(solution)/shard_map/ppermute | solution.py:985
  182.9 26.7 %collective-permute-start.29 = (bf16[1,192,768]{2,1,0:T(8,128)(2,1)}, bf16[1,192,768]{2,1,0:T(8,128)(2,1)}, u32[]{:S(2)}, u32[]{:S(2)}) collective-permute-start(bf16[1,192,768]{2,1,0:T(8,128)(2,1)} %get-tuple-element.155.refs_14_), channel_id=1, source_target_pairs={{0,12},{1,13},{2,14},{3,15},{4,8},{5,9},{6,10},{7,11},{8,4},{9,5},... | collective-permute-start | bytes 884744 | tf_op jit(solution)/shard_map/ppermute | solution.py:985
  184.0 2.3 copy-start.9
  184.0 25.6 %collective-permute-start.32 = (bf16[2,192,768]{2,1,0:T(8,128)(2,1)}, bf16[2,192,768]{2,1,0:T(8,128)(2,1)}, u32[]{:S(2)}, u32[]{:S(2)}) collective-permute-start(bf16[2,192,768]{2,1,0:T(8,128)(2,1)} %get-tuple-element.163.refs_0_), channel_id=1, source_target_pairs={{0,16},{1,17},{2,18},{3,19},{4,20},{5,21},{6,22},{7,23},{8,24},{9,... | collective-permute-start | bytes 1769480 | tf_op jit(solution)/shard_map/ppermute | solution.py:985
  186.3 13.4 %copy-start.12 = (bf16[512,768]{1,0:T(8,128)(2,1)S(1)}, bf16[512,768]{1,0:T(8,128)(2,1)}, u32[]{:S(2)}) copy-start(bf16[512,768]{1,0:T(8,128)(2,1)} %get-tuple-element.168) | copy-start | bytes 2359300
  199.6 22.1 %collective-permute-start.38 = (bf16[512,768]{1,0:T(8,128)(2,1)S(1)}, bf16[512,768]{1,0:T(8,128)(2,1)S(1)}, u32[]{:S(2)}, u32[]{:S(2)}) collective-permute-start(bf16[512,768]{1,0:T(8,128)(2,1)S(1)} %copy-done.12), channel_id=1, source_target_pairs={{0,2},{1,3},{2,0},{3,1},{4,6},{5,7},{6,4},{7,5},{8,10},{9,11},{10,... | collective-permute-start | bytes 2359304 | tf_op jit(solution)/shard_map/ppermute | solution.py:985
  209.5 6.1 %copy-start = (bf16[512,768]{1,0:T(8,128)(2,1)S(1)}, bf16[512,768]{1,0:T(8,128)(2,1)}, u32[]{:S(2)}) copy-start(bf16[512,768]{1,0:T(8,128)(2,1)} %get-tuple-element.165) | copy-start | bytes 2359300
  209.5 6.0 %collective-permute-start.31 = (bf16[80,768]{1,0:T(8,128)(2,1)}, bf16[80,768]{1,0:T(8,128)(2,1)S(1)}, u32[]{:S(2)}, u32[]{:S(2)}) collective-permute-start(bf16[80,768]{1,0:T(8,128)(2,1)} %get-tuple-element.162.refs_2_.refs_0_), channel_id=1, source_target_pairs={{0,1},{1,0},{2,3},{3,2},{4,5},{5,4},{6,7},{7,6},{8,9},{9,8},{10,11... | collective-permute-start | bytes 368648 | tf_op jit(solution)/shard_map/ppermute | solution.py:985
  211.8 36.9 %collective-permute-start.36 = (bf16[2,192,768]{2,1,0:T(8,128)(2,1)}, bf16[2,192,768]{2,1,0:T(8,128)(2,1)}, u32[]{:S(2)}, u32[]{:S(2)}) collective-permute-start(bf16[2,192,768]{2,1,0:T(8,128)(2,1)} %shard_map.253.refs_7_.refs_3_), channel_id=1, source_target_pairs={{0,12},{1,13},{2,14},{3,15},{4,8},{5,9},{6,10},{7,11},{8,4},{9,5},... | collective-permute-start | bytes 1769480 | tf_op jit(solution)/shard_map/ppermute | solution.py:985
  214.8 33.9 %collective-permute-start.35 = (bf16[2,192,768]{2,1,0:T(8,128)(2,1)}, bf16[2,192,768]{2,1,0:T(8,128)(2,1)}, u32[]{:S(2)}, u32[]{:S(2)}) collective-permute-start(bf16[2,192,768]{2,1,0:T(8,128)(2,1)} %shard_map.253.refs_7_.refs_3_), channel_id=1, source_target_pairs={{0,4},{1,5},{2,10},{3,11},{4,0},{5,1},{6,14},{7,15},{8,12},{9,13},... | collective-permute-start | bytes 1769480 | tf_op jit(solution)/shard_map/ppermute | solution.py:985
  214.8 33.9 %collective-permute-start.34 = (bf16[2,192,768]{2,1,0:T(8,128)(2,1)}, bf16[2,192,768]{2,1,0:T(8,128)(2,1)}, u32[]{:S(2)}, u32[]{:S(2)}) collective-permute-start(bf16[2,192,768]{2,1,0:T(8,128)(2,1)} %shard_map.253.refs_7_.refs_3_), channel_id=1, source_target_pairs={{0,8},{1,9},{2,6},{3,7},{4,12},{5,13},{6,2},{7,3},{8,0},{9,1},{10,... | collective-permute-start | bytes 1769480 | tf_op jit(solution)/shard_map/ppermute | solution.py:985
  215.6 3.8 %copy-start.21 = (bf16[80,768]{1,0:T(8,128)(2,1)}, bf16[80,768]{1,0:T(8,128)(2,1)S(1)}, u32[]{:S(2)}) copy-start(bf16[80,768]{1,0:T(8,128)(2,1)S(1)} %collective-permute-done.31.refs_1_) | copy-start | bytes 368644
  215.6 7.5 %collective-permute-start.37 = (bf16[512,768]{1,0:T(8,128)(2,1)S(1)}, bf16[512,768]{1,0:T(8,128)(2,1)S(1)}, u32[]{:S(2)}, u32[]{:S(2)}) collective-permute-start(bf16[512,768]{1,0:T(8,128)(2,1)S(1)} %copy-done), channel_id=1, source_target_pairs={{0,2},{1,3},{2,0},{3,1},{4,6},{5,7},{6,4},{7,5},{8,10},{9,11},{10,... | collective-permute-start | bytes 2359304 | tf_op jit(solution)/shard_map/ppermute | solution.py:985
  221.8 1.4 copy-start.14
  221.8 26.2 %collective-permute-start.33 = (bf16[272,768]{1,0:T(8,128)(2,1)}, bf16[272,768]{1,0:T(8,128)(2,1)S(1)}, u32[]{:S(2)}, u32[]{:S(2)}) collective-permute-start(bf16[272,768]{1,0:T(8,128)(2,1)} %shard_map.254.refs_8_.refs_1_), channel_id=1, source_target_pairs={{0,16},{1,17},{2,18},{3,19},{4,20},{5,21},{6,22},{7,23},{8,24},{9,... | collective-permute-start | bytes 1253384 | tf_op jit(solution)/shard_map/ppermute | solution.py:985
  223.1 0.9 copy-start.18
  252.3 10.0 %collective-permute-start.43 = (bf16[2,768,768]{2,1,0:T(8,128)(2,1)}, bf16[2,768,768]{2,1,0:T(8,128)(2,1)S(1)}, u32[]{:S(2)}, u32[]{:S(2)}) collective-permute-start(bf16[2,768,768]{2,1,0:T(8,128)(2,1)} %get-tuple-element.170.refs_1_.refs_3_), channel_id=1, source_target_pairs={{0,2},{1,3},{2,0},{3,1},{4,6},{5,7},{6,4},{7,5},{8,10},{9,11},{10,... | collective-permute-start | bytes 7077896 | tf_op jit(solution)/shard_map/ppermute | solution.py:985
  254.7 15.9 %collective-permute-start.41 = (bf16[272,768]{1,0:T(8,128)(2,1)}, bf16[272,768]{1,0:T(8,128)(2,1)}, u32[]{:S(2)}, u32[]{:S(2)}) collective-permute-start(bf16[272,768]{1,0:T(8,128)(2,1)} %get-tuple-element.169.refs_1_), channel_id=1, source_target_pairs={{0,12},{1,13},{2,14},{3,15},{4,8},{5,9},{6,10},{7,11},{8,4},{9,5},... | collective-permute-start | bytes 1253384 | tf_op jit(solution)/shard_map/ppermute | solution.py:985
  258.0 18.4 %collective-permute-start.40 = (bf16[272,768]{1,0:T(8,128)(2,1)}, bf16[272,768]{1,0:T(8,128)(2,1)}, u32[]{:S(2)}, u32[]{:S(2)}) collective-permute-start(bf16[272,768]{1,0:T(8,128)(2,1)} %get-tuple-element.169.refs_1_), channel_id=1, source_target_pairs={{0,4},{1,5},{2,10},{3,11},{4,0},{5,1},{6,14},{7,15},{8,12},{9,13},... | collective-permute-start | bytes 1253384 | tf_op jit(solution)/shard_map/ppermute | solution.py:985
  258.0 19.4 %collective-permute-start.39 = (bf16[272,768]{1,0:T(8,128)(2,1)}, bf16[272,768]{1,0:T(8,128)(2,1)}, u32[]{:S(2)}, u32[]{:S(2)}) collective-permute-start(bf16[272,768]{1,0:T(8,128)(2,1)} %get-tuple-element.169.refs_1_), channel_id=1, source_target_pairs={{0,8},{1,9},{2,6},{3,7},{4,12},{5,13},{6,2},{7,3},{8,0},{9,1},{10,... | collective-permute-start | bytes 1253384 | tf_op jit(solution)/shard_map/ppermute | solution.py:985
  258.2 22.5 %collective-permute-start.42 = (bf16[2,512,768]{2,1,0:T(8,128)(2,1)}, bf16[2,512,768]{2,1,0:T(8,128)(2,1)}, u32[]{:S(2)}, u32[]{:S(2)}) collective-permute-start(bf16[2,512,768]{2,1,0:T(8,128)(2,1)} %shard_map.256.refs_7_), channel_id=1, source_target_pairs={{0,0},{1,2},{2,1},{3,3},{4,4},{5,6},{6,5},{7,7},{8,8},{9,10},{10,9... | collective-permute-start | bytes 4718600 | tf_op jit(solution)/shard_map/ppermute | solution.py:985
  262.4 1.5 copy-start.8
  284.4 3.2 %collective-permute-start.44 = (bf16[848,768]{1,0:T(8,128)(2,1)}, bf16[848,768]{1,0:T(8,128)(2,1)S(1)}, u32[]{:S(2)}, u32[]{:S(2)}) collective-permute-start(bf16[848,768]{1,0:T(8,128)(2,1)} %get-tuple-element.174.refs_1_), channel_id=1, source_target_pairs={{0,2},{1,3},{2,0},{3,1},{4,6},{5,7},{6,4},{7,5},{8,10},{9,11},{10,... | collective-permute-start | bytes 3907592 | tf_op jit(solution)/shard_map/ppermute | solution.py:985
  287.7 1.1 copy-start.10
  (3 other events, 2.5 us)
where the time goes:
time: 294 us; the launch traced here: 293 us
  Pallas kernels  172 us (59%)
  starting transfers between devices  62.8 us (21%)
  waiting for transfers between devices  44.6 us (15%)
  local copies, waits for them, and re-layouts  12.2 us (4%)
    pallas_call x24, Pallas kernels, run(): pl.pallas_call(body, out_shape=out_shape, in_specs=in_specs, compiler_par...  172 us
    ppermute x45, starting transfers between devices, move(): return lax.ppermute(value, axes, how)  62.8 us
    ppermute x45, waiting for transfers between devices, move(): return lax.ppermute(value, axes, how)  44.6 us
    unnamed x44, local copies, waits for them, and re-layouts  8.59 us
  transfers between devices with their start and end apart: 45, of which 10 were waited for; matrix products, arithmetic and copies ran while one was open for 1% of the time, Pallas kernels for 55%

commit v1 on v0

--- a/solution.py
+++ b/solution.py
@@ -70,7 +70,7 @@
         self.last = out[-1] if isinstance(out, (list, tuple)) else out
         return out
 
-    def hold(self, values, after):
+    def hold(self, values, after, us=0):
         count = len(values)
 
         def kernel(*refs):
@@ -83,7 +83,9 @@
             out_specs=[ANY] * count,
             input_output_aliases={i: i for i in range(count)},
             compiler_params=pltpu.CompilerParams(has_side_effects=True),
-            cost_estimate=pl.CostEstimate(flops=0, bytes_accessed=0, transcendentals=0),
+            cost_estimate=pl.CostEstimate(
+                flops=int(us * WEIGHT * 1.15e9), bytes_accessed=0, transcendentals=0
+            ),
         )(*values, *after)
         for value, same in zip(values, held):
             if self.last is value:
@@ -850,7 +852,7 @@
     gather(place, parts, ff)
 
 
-def step2_call(order, place, size, own, got, parts):
+def step2_call(order, place, size, own, got, parts, after=()):
     groups, rows, dim = parts[0].shape
     return order.run(
         4.5,
@@ -858,32 +860,51 @@
         (place, own, got, *parts),
         [sds(own.shape, BF16), sds((groups, 4 * rows, dim), BF16)],
         [SMEM] + [VMEM] * 6,
+        after,
     )
 
 
 def step3_kernel(size, place, *refs):
     parts, refs = refs[:4], refs[4:]
-    results, both, mixed_out, grad_out = refs
+    (both,) = refs
     for partner, part in enumerate(parts):
         both[part_rows(quarter(place) ^ partner, size), :] = part[:size, :]
     add_late([part.at[size:, :] for part in parts], both.at[4 * size :, :])
-    mixed_out[...] = results[0]
-    grad_out[...] = results[1]
-
-
-def step3_call(order, place, size, parts, results):
+
+
+def step3_call(order, place, size, parts):
     rows, dim = parts[0].shape
-    half = sds(results.shape[1:], BF16)
     return order.run(
         3.5,
         functools.partial(step3_kernel, size),
-        (place, *parts, results),
-        [sds((rows + 3 * size, dim), BF16), half, half],
-        [SMEM] + [VMEM] * 5,
-    )
-
-
-def finish_attention_kernel(place, near, far, w_query, w_key, w_value, w_out, *norms):
+        (place, *parts),
+        sds((rows + 3 * size, dim), BF16),
+        [SMEM] + [VMEM] * 4,
+    )
+
+
+def copy_kernel(place, results, moved, mixed, tokens_grad):
+    stays = place[0] == place[1]
+    for source, wanted in ((results, stays), (moved, jnp.logical_not(stays))):
+
+        @pl.when(wanted)
+        def _():
+            mixed[...] = source[0]
+            tokens_grad[...] = source[1]
+
+
+def copy_call(order, place, results, moved):
+    return order.run(
+        2,
+        copy_kernel,
+        (place, results, moved),
+        [sds(results.shape[1:], BF16)] * 2,
+        [SMEM] + [VMEM] * 2,
+    )
+
+
+def finish_attention_kernel(place, near, far, *outs):
+    w_query, w_key, w_value, w_out, *norms = outs
     width = w_out.shape[0] // 2
     late = 4 * width
     rows = late + HEAD_DIM
@@ -967,6 +988,7 @@
         )
 
     by_role = pairs(lambda chip, core, part: (chip, part, core))
+    swapped = [pair for pair in by_role if pair[0] != pair[1]]
     by_core = pairs(lambda chip, core, part: (chip, 1 - core, part))
     by_part = pairs(lambda chip, core, part: (chip, core, 1 - part))
     from_first_part = [pair for pair in by_part if pair[0] % parts == 0]
@@ -1038,7 +1060,7 @@
         )
         out_r = move(out_l, by_part)
         up_near = move(up_s, by_part)
-        grad_own = move(grad, by_role)
+        grad_moved = move(grad, swapped)
         down_near = move(down_s, by_part)
         n1, penalty, qk0, first = penalty_call(
             order, place, n1_own, n1_other, first, first_moved, seg_pad
@@ -1056,14 +1078,16 @@
             (up_near,),
         )
         (send,) = order.hold((send,), (down_near,))
-        (up_near,) = order.hold((up_near,), (lse_r,))
-        up_far = move(up_near, by_chip[0])
-        (grad_own,) = order.hold((grad_own,), (lse_r,))
-        grad_other = move(grad_own, by_core)
-        (down_near,) = order.hold((down_near,), (lse_r,))
-        down_far = move(down_near, by_chip[0])
+        (mine,) = order.hold((mine,), (send,), 5)
         hidden, n2_own = norm2_call(order, mine, own, move(send, by_core), gain2, shift2)
         n2_other = move(n2_own, by_core)
+        up_near, down_near = order.hold((up_near, down_near), (mine,))
+        up_far = move(up_near, by_chip[0])
+        down_far = move(down_near, by_chip[0])
+        (grad_moved,) = order.hold((grad_moved,), (n2_own,))
+        grad_own = jnp.where(core == part, grad, grad_moved)
+        grad_other = move(grad_own, by_core)
+        (up_l,) = order.hold((up_l,), (n2_own,), 5)
         *before, keep, send = mlp_call(
             order, place, n2_other, n2_own, grad_other, grad_own, (up_l, down_l)
         )
@@ -1135,14 +1159,16 @@
             move(mixed_send, by_core),
         )
         (results,) = order.hold((results,), (both_got,))
-        results = move(results, by_role)
+        moved = move(results, swapped)
         both, ff = step2_call(order, place, size, both, both_got, ff)
         both = exchange([add_more(both)] * 4)
         ff_far = move(ff, by_core)
         up_grad, down_grad = finish_mlp_call(order, place, ff, ff_far)
-        both, mixed, tokens_grad = step3_call(order, place, size, both, results)
+        both = step3_call(order, place, size, both)
+        both_far = move(both, by_core)
+        mixed, tokens_grad = copy_call(order, place, results, moved)
         query_grad, key_grad, value_grad, out_grad, *norms = finish_attention_call(
-            order, place, size, both, move(both, by_core)
+            order, place, size, both, both_far
         )
         return (
             mixed,

time: 294 us -> 280 us (0.952); the launches traced: 293 us -> 275 us
  Pallas kernels: 172 us -> 161 us
  waiting for transfers between devices: 44.6 us -> 38.5 us
  starting transfers between devices: 62.8 us -> 58.8 us
    pallas_call x24 -> x25, Pallas kernels: 172 us -> 161 us  [run(): pl.pallas_call(body, out_shape=out_shape, in_specs=in_specs, compiler_par...]
    ppermute x45, waiting for transfers between devices: 44.6 us -> 38.5 us  [move(): return lax.ppermute(value, axes, how)]
    ppermute x45, starting transfers between devices: 62.8 us -> 58.8 us  [move(): return lax.ppermute(value, axes, how)]
    unnamed x44 -> x48, local copies, waits for them, and re-layouts: 8.59 us -> 9.6 us
  transfers between devices with their start and end apart: 45 -> 45, of which waited for: 10 -> 11; matrix products, arithmetic and copies ran while one was open for 1% -> 2% of each run, Pallas kernels for 55% -> 56%
where the time goes in v1:
time: 280 us; the launch traced here: 275 us
  Pallas kernels  161 us (58%)
  starting transfers between devices  58.8 us (21%)
  waiting for transfers between devices  38.5 us (14%)
  local copies, waits for them, and re-layouts  13.2 us (5%)
    pallas_call x25, Pallas kernels, run(): pl.pallas_call(body, out_shape=out_shape, in_specs=in_specs, compiler_par...  161 us
    ppermute x45, starting transfers between devices, move(): return lax.ppermute(value, axes, how)  58.8 us
    ppermute x45, waiting for transfers between devices, move(): return lax.ppermute(value, axes, how)  38.5 us
    unnamed x48, local copies, waits for them, and re-layouts  9.6 us
  transfers between devices with their start and end apart: 45, of which 11 were waited for; matrix products, arithmetic and copies ran while one was open for 2% of the time, Pallas kernels for 56%

profile of v1, /device:TPU:1, one launch (start us, length us, event | category | flops | bytes accessed | tf_op | source)
XLA Modules:
  0.0 275.0 jit_solution(8949483679917253986)
XLA Ops:
  1.5 4.5 %collective-permute-start = (bf16[512,768]{1,0:T(8,128)(2,1)}, bf16[512,768]{1,0:T(8,128)(2,1)S(1)}, u32[]{:S(2)}, u32[]{:S(2)}) collective-permute-start(bf16[512,768]{1,0:T(8,128)(2,1)} %param.14), channel_id=1, source_target_pairs={{0,0},{1,2},{2,1},{3,3},{4,4},{5,6},{6,5},{7,7},{8,8},{9,10},{10,9... | collective-permute-start | bytes 2359304 | tf_op jit(solution)/shard_map/ppermute | solution.py:1007
  6.7 3.1 %shard_map.229 = (bf16[768,576]{1,0:T(8,128)(2,1)}, bf16[384,576]{1,0:T(8,128)(2,1)}, bf16[768,128]{1,0:T(8,128)(2,1)}) custom-call(s32[5]{0:T(128)} %stack.35.refs_0_, bf16[768,384]{1,0:T(8,128)(2,1)} %refs_1_.2, bf16[768,384]{1,0:T(8,128)(2,1)} %refs_2_.2, bf16[768,384]{1,0:T(8,128)(2,1)} %refs_3_.2), custom_call_target="tpu_custom_call" | custom-call | flops 92000002048 | tf_op jit(solution)/shard_map/pallas_call | solution.py:60
  9.8 2.5 collective-permute-start.2
  15.3 2.1 collective-permute-done.refs_0_
  18.3 2.6 shard_map.230.refs_5_.refs_1_
  20.9 5.1 %shard_map.231 = (bf16[192,768]{1,0:T(8,128)(2,1)}, bf16[768,768]{1,0:T(8,128)(2,1)}, bf16[384,768]{1,0:T(8,128)(2,1)}, bf16[768,768]{1,0:T(8,128)(2,1)}, bf16[3...) custom-call(s32[5]{0:T(128)} %stack.35.refs_0_, bf16[384,768]{1,0:T(8,128)(2,1)} %refs_1_.3, bf16[768,1536]{1,0:T(8,128)(2,1)} %refs_2_.3, ...), custom_call_target="tpu_custom_call" | custom-call | flops 115000000512 | tf_op jit(solution)/shard_map/pallas_call | solution.py:60
  26.0 2.5 collective-permute-start.6
  28.5 1.4 collective-permute-start.8
  29.9 2.4 collective-permute-start.11
  32.3 6.4 %shard_map.232 = (bf16[1024,768]{1,0:T(8,128)(2,1)}, f32[1024,1024]{1,0:T(8,128)}, bf16[128,1024]{1,0:T(8,128)(2,1)}, bf16[768,128]{1,0:T(8,128)(2,1)}) custom-call(s32[5]{0:T(128)} %stack.35.refs_0_, bf16[512,768]{1,0:T(8,128)(2,1)} %shard_map.230.refs_5_.refs_1_, bf16[512,768]{1,0:T(8,128)(2,1)} %copy-done.19, bf16[768,128]{1,0:T(8,128)(2,1)} %get-tuple-element.99.refs_3_, ...), custom_call_target="tpu_custom_call" | custom-call | flops 149500002304 | tf_op jit(solution)/shard_map/pallas_call | solution.py:60
  38.7 1.6 collective-permute-start.5
  40.3 9.4 %shard_map.234 = (bf16[576,1024]{1,0:T(8,128)(2,1)}, bf16[192,1024]{1,0:T(8,128)(2,1)}, f32[3,1,1024]{2,1,0:T(1,128)}) custom-call(bf16[1024,768]{1,0:T(8,128)(2,1)} %get-tuple-element.101.refs_0_.refs_1_.refs_5_, bf16[768,576]{1,0:T(8,128)(2,1)} %get-tuple-element.104.refs_1_.refs_7_, f32[1024,1024]{1,0:T(8,128)} %get-tuple-element.103.refs_1_.refs_2_.refs_4_.refs_7_, ...), custom_call_target="tpu_custom_call" | custom-call | flops 230000001024 | tf_op jit(solution)/shard_map/pallas_call | solution.py:60
  49.7 12.2 %shard_map.235 = (bf16[576,1024]{1,0:T(8,128)(2,1)}, bf16[192,1024]{1,0:T(8,128)(2,1)}, f32[3,1,1024]{2,1,0:T(1,128)}, bf16[768,576]{1,0:T(8,128)(2,1)}, f32[512,768]{1,0:T(8,128)}, /*index=5*/bf16[512,768]{1,0:T(8,128)(2,1)}) custom-call(s32[5]{0:T(128)} %stack.35.refs_0_, bf16[1024,768]{1,0:T(8,128)(2,1)} %get-tuple-element.101.refs_0_.refs_1_.refs_5_, ...), custom_call_target="tpu_custom_call" | custom-call | flops 230000001024 | tf_op jit(solution)/shard_map/pallas_call | solution.py:60
  62.1 1.3 collective-permute-start.13
  63.6 0.9 collective-permute-done.9.refs_2_
  64.5 0.9 copy-done.21
  65.4 3.0 %shard_map.238 = (f32[512,768]{1,0:T(8,128)}, bf16[512,768]{1,0:T(8,128)(2,1)}) custom-call(bf16[512,768]{1,0:T(8,128)(2,1)} %shard_map.237.refs_0_.refs_2_, f32[512,768]{1,0:T(8,128)} %get-tuple-element.112.refs_1_, bf16[512,768]{1,0:T(8,128)(2,1)} %copy-done.21, f32[1,768]{1,0:T(1,128)} %broadcast_in_dim.15.refs_3_.refs_4_, ...), custom_call_target="tpu_custom_call" | custom-call | flops 92000002048 | tf_op jit(solution)/shard_map/pallas_call | solution.py:60
  68.6 1.4 collective-permute-done.11.refs_0_
  70.0 1.2 broadcast_select_fusion.refs_4_.refs_3_
  72.1 1.5 collective-permute-done.12.refs_3_
  73.6 0.9 copy-done.18
  74.8 13.3 %shard_map.242 = (bf16[512,768]{1,0:T(8,128)(2,1)}, bf16[512,768]{1,0:T(8,128)(2,1)}, bf16[512,768]{1,0:T(8,128)(2,1)}, bf16[512,768]{1,0:T(8,128)(2,1)}, bf16[2...) custom-call(s32[5]{0:T(128)} %stack.35.refs_0_, bf16[512,768]{1,0:T(8,128)(2,1)} %copy-done.17, ...), custom_call_target="tpu_custom_call" | custom-call | flops 335800008704 | tf_op jit(solution)/shard_map/pallas_call | solution.py:60
  88.1 1.2 collective-permute-start.15
  89.3 14.8 %shard_map.243 = (bf16[512,768]{1,0:T(8,128)(2,1)}, bf16[512,768]{1,0:T(8,128)(2,1)}, bf16[512,768]{1,0:T(8,128)(2,1)}, bf16[512,768]{1,0:T(8,128)(2,1)}, bf16[2...) custom-call(s32[5]{0:T(128)} %stack.35.refs_0_, ...), custom_call_target="tpu_custom_call" | custom-call | flops 335800008704 | tf_op jit(solution)/shard_map/pallas_call | solution.py:60
  104.8 1.2 collective-permute-start.19
  105.9 1.3 collective-permute-start.20
  107.4 0.9 copy-done.22
  108.3 4.0 %shard_map.245 = (f32[512,768]{1,0:T(8,128)}, bf16[512,768]{1,0:T(8,128)(2,1)}, f32[8,768]{1,0:T(8,128)}) custom-call(f32[512,768]{1,0:T(8,128)} %get-tuple-element.113.refs_0_.refs_5_, bf16[512,768]{1,0:T(8,128)(2,1)} %get-tuple-element.124.refs_1_, bf16[512,768]{1,0:T(8,128)(2,1)} %copy-done.22, bf16[512,768]{1,0:T(8,128)(2,1)} %copy-done.1, ...), custom_call_target="tpu_custom_call" | custom-call | flops 115000000512 | tf_op jit(solution)/shard_map/pallas_call | solution.py:60
  113.1 2.9 %shard_map.246 = (bf16[2,192,768]{2,1,0:T(8,128)(2,1)}, bf16[2,192,768]{2,1,0:T(8,128)(2,1)}) custom-call(s32[5]{0:T(128)} %stack.35.refs_0_, bf16[2,384,768]{2,1,0:T(8,128)(2,1)} %get-tuple-element.137.refs_1_, bf16[2,384,768]{2,1,0:T(8,128)(2,1)} %collective-permute-done.15.refs_5_.refs_2_, f32[8,768]{1,0:T(8,128)} %get-tuple-element.138.refs_3_.refs_13_), custom_call_target="tpu_custom_call" | custom-call | flops 69000003584 | tf_op jit(solution)/shard_map/pallas_call | solution.py:60
  116.0 1.2 collective-permute-start.18
  118.1 14.1 %shard_map.247 = (bf16[576,1024]{1,0:T(8,128)(2,1)}, bf16[192,768]{1,0:T(8,128)(2,1)}, f32[1024,1024]{1,0:T(8,128)}) custom-call(s32[5]{0:T(128)} %stack.35.refs_0_, bf16[512,768]{1,0:T(8,128)(2,1)} %get-tuple-element.132.refs_1_, bf16[512,768]{1,0:T(8,128)(2,1)} %copy-done.15, bf16[192,768]{1,0:T(8,128)(2,1)} %collective-permute-done.6.refs_7_.refs_3_, ...), custom_call_target="tpu_custom_call" | custom-call | flops 368000008192 | tf_op jit(solution)/shard_map/pallas_call | solution.py:60
  132.2 4.0 %shard_map.248 = (bf16[1,192,768]{2,1,0:T(8,128)(2,1)}, bf16[1,192,768]{2,1,0:T(8,128)(2,1)}, bf16[1,192,768]{2,1,0:T(8,128)(2,1)}, bf16[1,192,768]{2,1,0:T(8,128)(2,1)}) custom-call(s32[5]{0:T(128)} %stack.35.refs_0_, bf16[1024,768]{1,0:T(8,128)(2,1)} %get-tuple-element.101.refs_0_.refs_1_.refs_5_, bf16[576,1024]{1,0:T(8,128)(2,1)} %get-tuple-element.145.refs_2_.refs_9_, ...), custom_call_target="tpu_custom_call" | custom-call | flops 92000002048 | tf_op jit(solution)/shard_map/pallas_call | solution.py:60
  136.4 1.2 collective-permute-start.24
  137.7 1.1 collective-permute-start.25
  139.4 3.2 %shard_map.249 = (bf16[2,192,768]{2,1,0:T(8,128)(2,1)}, bf16[2,192,768]{2,1,0:T(8,128)(2,1)}) custom-call(bf16[2,192,768]{2,1,0:T(8,128)(2,1)} %get-tuple-element.141.refs_0_, bf16[2,192,768]{2,1,0:T(8,128)(2,1)} %collective-permute-done.18.refs_1_, bf16[2,192,768]{2,1,0:T(8,128)(2,1)} %get-tuple-element.142.refs_2_, ...), custom_call_target="tpu_custom_call" | custom-call | flops 69000003584 | tf_op jit(solution)/shard_map/pallas_call | solution.py:60
  142.6 2.4 collective-permute-start.26
  145.0 14.4 %shard_map.250 = (bf16[576,1024]{1,0:T(8,128)(2,1)}, bf16[192,768]{1,0:T(8,128)(2,1)}, bf16[1024,1024]{1,0:T(8,128)(2,1)}) custom-call(s32[5]{0:T(128)} %stack.35.refs_0_, bf16[512,768]{1,0:T(8,128)(2,1)} %get-tuple-element.132.refs_1_, bf16[512,768]{1,0:T(8,128)(2,1)} %copy-done.15, bf16[192,768]{1,0:T(8,128)(2,1)} %get-tuple-element.107.refs_6_.refs_3_, ...), custom_call_target="tpu_custom_call" | custom-call | flops 368000008192 | tf_op jit(solution)/shard_map/pallas_call | solution.py:60
  159.4 1.5 collective-permute-start.22
  160.9 5.0 %shard_map.251 = (bf16[1,192,768]{2,1,0:T(8,128)(2,1)}, bf16[2,192,768]{2,1,0:T(8,128)(2,1)}, bf16[1,192,768]{2,1,0:T(8,128)(2,1)}, bf16[1,192,768]{2,1,0:T(8,12...) custom-call(s32[5]{0:T(128)} %stack.35.refs_0_, ...), custom_call_target="tpu_custom_call" | custom-call | flops 138000007168 | tf_op jit(solution)/shard_map/pallas_call | solution.py:60
  166.9 1.3 collective-permute-start.28
  168.7 2.3 collective-permute-start.34
  171.0 13.4 %shard_map.252 = (f32[512,768]{1,0:T(8,128)}, bf16[512,768]{1,0:T(8,128)(2,1)}, bf16[80,768]{1,0:T(8,128)(2,1)}) custom-call(s32[5]{0:T(128)} %stack.35.refs_0_, bf16[1024,1024]{1,0:T(8,128)(2,1)} %get-tuple-element.149.refs_10_.refs_1_, bf16[1024,1024]{1,0:T(8,128)(2,1)} %copy-done.12, bf16[128,1024]{1,0:T(8,128)(2,1)} %get-tuple-element.150.refs_3_, ...), custom_call_target="tpu_custom_call" | custom-call | flops 321999994880 | tf_op jit(solution)/shard_map/pallas_call | solution.py:60
  184.5 3.1 %collective-permute-start.32 = (bf16[512,768]{1,0:T(8,128)(2,1)S(1)}, bf16[512,768]{1,0:T(8,128)(2,1)S(1)}, u32[]{:S(2)}, u32[]{:S(2)}) collective-permute-start(bf16[512,768]{1,0:T(8,128)(2,1)S(1)} %copy-done.14), channel_id=1, source_target_pairs={{0,2},{1,3},{2,0},{3,1},{4,6},{5,7},{6,4},{7,5},{8,10},{9,11},{10,... | collective-permute-start | bytes 2359304 | tf_op jit(solution)/shard_map/ppermute | solution.py:1007
  187.9 6.5 %collective-permute-done.29.refs_5_ = bf16[1,192,768]{2,1,0:T(8,128)(2,1)} collective-permute-done((bf16[1,192,768]{2,1,0:T(8,128)(2,1)}, bf16[1,192,768]{2,1,0:T(8,128)(2,1)}, u32[]{:S(2)}, u32[]{:S(2)}) %collective-permute-start.29) | collective-permute-done | bytes 294944 | tf_op jit(solution)/shard_map/ppermute | solution.py:1007
  194.4 2.3 shard_map.254.refs_7_.refs_3_
  196.6 3.1 %collective-permute-start.39 = (bf16[2,192,768]{2,1,0:T(8,128)(2,1)}, bf16[2,192,768]{2,1,0:T(8,128)(2,1)}, u32[]{:S(2)}, u32[]{:S(2)}) collective-permute-start(bf16[2,192,768]{2,1,0:T(8,128)(2,1)} %shard_map.254.refs_7_.refs_3_), channel_id=1, source_target_pairs={{0,12},{1,13},{2,14},{3,15},{4,8},{5,9},{6,10},{7,11},{8,4},{9,5},... | collective-permute-start | bytes 1769480 | tf_op jit(solution)/shard_map/ppermute | solution.py:1007
  200.3 3.8 %collective-permute-start.31 = (bf16[512,768]{1,0:T(8,128)(2,1)S(1)}, bf16[512,768]{1,0:T(8,128)(2,1)S(1)}, u32[]{:S(2)}, u32[]{:S(2)}) collective-permute-start(bf16[512,768]{1,0:T(8,128)(2,1)S(1)} %copy-done.3), channel_id=1, source_target_pairs={{0,2},{1,3},{2,0},{3,1},{4,6},{5,7},{6,4},{7,5},{8,10},{9,11},{10,... | collective-permute-start | bytes 2359304 | tf_op jit(solution)/shard_map/ppermute | solution.py:1007
  204.1 2.4 shard_map.255.refs_8_.refs_1_
  206.5 1.9 collective-permute-start.35
  209.3 5.2 %shard_map.256.refs_0_ = bf16[2,512,768]{2,1,0:T(8,128)(2,1)} custom-call(bf16[512,768]{1,0:T(8,128)(2,1)} %shard_map.237.refs_0_.refs_2_, f32[512,768]{1,0:T(8,128)} %get-tuple-element.159.refs_1_, bf16[512,768]{1,0:T(8,128)(2,1)} %copy-done.20, f32[512,768]{1,0:T(8,128)} %get-tuple-element.167.refs_3_, f32[1,768]{1,0:T(1,128)} %broadcast_in_dim.13.refs_1_.refs_11_.refs_4_, ...), custom_call_target="tpu_custom_call" | custom-call | flops 115000000512 | tf_op jit(solution)/shard_map/pallas_call | solution.py:60
  214.4 18.0 %collective-permute-done.35.refs_1_.refs_2_ = bf16[272,768]{1,0:T(8,128)(2,1)S(1)} collective-permute-done((bf16[272,768]{1,0:T(8,128)(2,1)}, bf16[272,768]{1,0:T(8,128)(2,1)S(1)}, u32[]{:S(2)}, u32[]{:S(2)}) %collective-permute-start.35) | collective-permute-done | bytes 417824 | tf_op jit(solution)/shard_map/ppermute | solution.py:1007
  233.2 3.6 %shard_map.258 = (bf16[272,768]{1,0:T(8,128)(2,1)}, bf16[2,768,768]{2,1,0:T(8,128)(2,1)}) custom-call(s32[5]{0:T(128)} %stack.35.refs_0_, bf16[272,768]{1,0:T(8,128)(2,1)} %shard_map.255.refs_8_.refs_1_, bf16[272,768]{1,0:T(8,128)(2,1)} %copy-done.4, bf16[2,192,768]{2,1,0:T(8,128)(2,1)} %shard_map.254.refs_7_.refs_3_, ...), custom_call_target="tpu_custom_call" | custom-call | flops 103499997184 | tf_op jit(solution)/shard_map/pallas_call | solution.py:60
  236.8 2.8 %collective-permute-start.43 = (bf16[2,768,768]{2,1,0:T(8,128)(2,1)}, bf16[2,768,768]{2,1,0:T(8,128)(2,1)S(1)}, u32[]{:S(2)}, u32[]{:S(2)}) collective-permute-start(bf16[2,768,768]{2,1,0:T(8,128)(2,1)} %get-tuple-element.173.refs_1_.refs_3_), channel_id=1, source_target_pairs={{0,2},{1,3},{2,0},{3,1},{4,6},{5,7},{6,4},{7,5},{8,10},{9,11},{10,... | collective-permute-start | bytes 7077896 | tf_op jit(solution)/shard_map/ppermute | solution.py:1007
  239.6 3.0 %collective-permute-start.42 = (bf16[272,768]{1,0:T(8,128)(2,1)}, bf16[272,768]{1,0:T(8,128)(2,1)}, u32[]{:S(2)}, u32[]{:S(2)}) collective-permute-start(bf16[272,768]{1,0:T(8,128)(2,1)} %get-tuple-element.172.refs_1_), channel_id=1, source_target_pairs={{0,12},{1,13},{2,14},{3,15},{4,8},{5,9},{6,10},{7,11},{8,4},{9,5},... | collective-permute-start | bytes 1253384 | tf_op jit(solution)/shard_map/ppermute | solution.py:1007
  242.6 1.1 collective-permute-start.40
  243.7 3.9 %collective-permute-start.36 = (bf16[2,512,768]{2,1,0:T(8,128)(2,1)}, bf16[2,512,768]{2,1,0:T(8,128)(2,1)}, u32[]{:S(2)}, u32[]{:S(2)}) collective-permute-start(bf16[2,512,768]{2,1,0:T(8,128)(2,1)} %shard_map.257.refs_7_.refs_1_), channel_id=1, source_target_pairs={{1,2},{2,1},{5,6},{6,5},{9,10},{10,9},{13,14},{14,13},{17,18},{18,... | collective-permute-start | bytes 4718600 | tf_op jit(solution)/shard_map/ppermute | solution.py:1007
  247.6 1.4 copy-done.11
  249.0 6.7 %shard_map.259 = (f32[768,1536]{1,0:T(8,128)}, f32[1536,768]{1,0:T(8,128)}) custom-call(s32[5]{0:T(128)} %stack.35.refs_0_, bf16[2,768,768]{2,1,0:T(8,128)(2,1)} %get-tuple-element.173.refs_1_.refs_3_, bf16[2,768,768]{2,1,0:T(8,128)(2,1)} %copy-done.11, bf16[2,768,768]{2,1,0:T(8,128)(2,1)} %get-tuple-element.173.refs_1_.refs_3_), custom_call_target="tpu_custom_call" | custom-call | flops 156399992832 | tf_op jit(solution)/shard_map/pallas_call | solution.py:60
  255.8 6.1 %collective-permute-done.41.refs_3_ = bf16[272,768]{1,0:T(8,128)(2,1)} collective-permute-done((bf16[272,768]{1,0:T(8,128)(2,1)}, bf16[272,768]{1,0:T(8,128)(2,1)}, u32[]{:S(2)}, u32[]{:S(2)}) %collective-permute-start.41) | collective-permute-done | bytes 417824 | tf_op jit(solution)/shard_map/ppermute | solution.py:1007
  262.0 2.6 shard_map.260.refs_3_.refs_1_
  265.0 1.0 collective-permute-done.36.refs_2_
  266.0 3.1 %shard_map.261 = (bf16[512,768]{1,0:T(8,128)(2,1)}, bf16[512,768]{1,0:T(8,128)(2,1)}) custom-call(s32[5]{0:T(128)} %stack.35.refs_0_, bf16[2,512,768]{2,1,0:T(8,128)(2,1)} %shard_map.257.refs_7_.refs_1_, bf16[2,512,768]{2,1,0:T(8,128)(2,1)} %collective-permute-done.36.refs_2_, bf16[848,768]{1,0:T(8,128)(2,1)} %shard_map.260.refs_3_.refs_1_), custom_call_target="tpu_custom_call" | custom-call | flops 46000001024 | tf_op jit(solution)/shard_map/pallas_call | solution.py:60
  269.1 1.1 copy-done.13
  270.2 4.6 %shard_map.262 = (f32[768,384]{1,0:T(8,128)}, f32[768,384]{1,0:T(8,128)}, f32[768,384]{1,0:T(8,128)}, f32[384,768]{1,0:T(8,128)}, f32[768]{0:T(1024)}, /*index=5*/f32[768]{0:T(1024)}, f32[768]{0:T(1024)}, f32[768]{0:T(1024)}) custom-call(s32[5]{0:T(128)} %stack.35.refs_0_, bf16[848,768]{1,0:T(8,128)(2,1)} %shard_map.260.refs_3_.refs_1_, ...), custom_call_target="tpu_custom_call" | custom-call | flops 103499997184 | tf_op jit(solution)/shard_map/pallas_call | solution.py:60
  (117 shorter events, 14.9 us)
Async XLA Ops:
  1.4 13.3 %collective-permute-start.3 = (s32[2,1024]{1,0:T(2,128)S(1)}, s32[2,1024]{1,0:T(2,128)S(1)}, u32[]{:S(2)}, u32[]{:S(2)}) collective-permute-start(s32[2,1024]{1,0:T(2,128)S(1)} %pad_add_fusion), channel_id=1, source_target_pairs={{0,2},{1,3},{2,0},{3,1},{4,6},{5,7},{6,4},{7,5},{8,10},{9,11},{10,... | collective-permute-start | bytes 24584 | tf_op jit(solution)/shard_map/ppermute | solution.py:1007
  1.5 15.9 %collective-permute-start = (bf16[512,768]{1,0:T(8,128)(2,1)}, bf16[512,768]{1,0:T(8,128)(2,1)S(1)}, u32[]{:S(2)}, u32[]{:S(2)}) collective-permute-start(bf16[512,768]{1,0:T(8,128)(2,1)} %param.14), channel_id=1, source_target_pairs={{0,0},{1,2},{2,1},{3,3},{4,4},{5,6},{6,5},{7,7},{8,8},{9,10},{10,9... | collective-permute-start | bytes 2359304 | tf_op jit(solution)/shard_map/ppermute | solution.py:1007
  6.7 5.6 %copy-start.7 = (f32[768]{0:T(1024)S(1)}, f32[768]{0:T(1024)}, u32[]{:S(2)}) copy-start(f32[768]{0:T(1024)} %param.17) | copy-start | bytes 9220
  6.7 6.2 %copy-start.8 = (f32[768]{0:T(1024)S(1)}, f32[768]{0:T(1024)}, u32[]{:S(2)}) copy-start(f32[768]{0:T(1024)} %param.18) | copy-start | bytes 9220
  6.7 6.8 %copy-start.9 = (f32[768]{0:T(1024)S(1)}, f32[768]{0:T(1024)}, u32[]{:S(2)}) copy-start(f32[768]{0:T(1024)} %param.23) | copy-start | bytes 9220
  6.7 7.4 %copy-start.10 = (f32[768]{0:T(1024)S(1)}, f32[768]{0:T(1024)}, u32[]{:S(2)}) copy-start(f32[768]{0:T(1024)} %param.24) | copy-start | bytes 9220
  6.7 7.9 %copy-start.5 = (s32[1,1024]{1,0:T(1,128)S(1)}, s32[1,1024]{1,0:T(1,128)}, u32[]{:S(2)}) copy-start(s32[1,1024]{1,0:T(1,128)} %param.16) | copy-start | bytes 12292
  6.7 7.9 %copy-start.6 = (s32[1,1024]{1,0:T(1,128)S(1)}, s32[1,1024]{1,0:T(1,128)}, u32[]{:S(2)}) copy-start(s32[1,1024]{1,0:T(1,128)} %param.15) | copy-start | bytes 12292
  9.8 18.7 %collective-permute-start.2 = (bf16[768,128]{1,0:T(8,128)(2,1)}, bf16[768,128]{1,0:T(8,128)(2,1)}, u32[]{:S(2)}, u32[]{:S(2)}) collective-permute-start(bf16[768,128]{1,0:T(8,128)(2,1)} %get-tuple-element.99.refs_3_), channel_id=1, source_target_pairs={{0,1},{2,3},{4,5},{6,7},{8,9},{10,11},{12,13},{14,15},{16,17},{18,... | collective-permute-start | bytes 589832 | tf_op jit(solution)/shard_map/ppermute | solution.py:1007
  12.3 26.4 %collective-permute-start.4 = (bf16[384,576]{1,0:T(8,128)(2,1)}, bf16[384,576]{1,0:T(8,128)(2,1)}, u32[]{:S(2)}, u32[]{:S(2)}) collective-permute-start(bf16[384,576]{1,0:T(8,128)(2,1)} %get-tuple-element.102), channel_id=1, source_target_pairs={{0,1},{1,0},{2,3},{3,2},{4,5},{5,4},{6,7},{7,6},{8,9},{9,8},{10,11... | collective-permute-start | bytes 1327112 | tf_op jit(solution)/shard_map/ppermute | solution.py:1007
  20.9 9.1 %collective-permute-start.1 = (bf16[512,768]{1,0:T(8,128)(2,1)}, bf16[512,768]{1,0:T(8,128)(2,1)S(1)}, u32[]{:S(2)}, u32[]{:S(2)}) collective-permute-start(bf16[512,768]{1,0:T(8,128)(2,1)} %shard_map.230.refs_5_.refs_1_), channel_id=1, source_target_pairs={{0,2},{1,3},{2,0},{3,1},{4,6},{5,7},{6,4},{7,5},{8,10},{9,11},{10,... | collective-permute-start | bytes 2359304 | tf_op jit(solution)/shard_map/ppermute | solution.py:1007
  26.0 23.8 %collective-permute-start.6 = (bf16[192,768]{1,0:T(8,128)(2,1)}, bf16[192,768]{1,0:T(8,128)(2,1)}, u32[]{:S(2)}, u32[]{:S(2)}) collective-permute-start(bf16[192,768]{1,0:T(8,128)(2,1)} %get-tuple-element.107.refs_6_.refs_3_), channel_id=1, source_target_pairs={{0,1},{1,0},{2,3},{3,2},{4,5},{5,4},{6,7},{7,6},{8,9},{9,8},{10,11... | collective-permute-start | bytes 884744 | tf_op jit(solution)/shard_map/ppermute | solution.py:1007
  28.5 21.3 %collective-permute-start.7 = (bf16[384,768]{1,0:T(8,128)(2,1)}, bf16[384,768]{1,0:T(8,128)(2,1)}, u32[]{:S(2)}, u32[]{:S(2)}) collective-permute-start(bf16[384,768]{1,0:T(8,128)(2,1)} %get-tuple-element.108), channel_id=1, source_target_pairs={{0,1},{1,0},{2,3},{3,2},{4,5},{5,4},{6,7},{7,6},{8,9},{9,8},{10,11... | collective-permute-start | bytes 1769480 | tf_op jit(solution)/shard_map/ppermute | solution.py:1007
  28.5 33.5 %collective-permute-start.8 = (bf16[384,768]{1,0:T(8,128)(2,1)}, bf16[384,768]{1,0:T(8,128)(2,1)}, u32[]{:S(2)}, u32[]{:S(2)}) collective-permute-start(bf16[384,768]{1,0:T(8,128)(2,1)} %get-tuple-element.111), channel_id=1, source_target_pairs={{0,1},{1,0},{2,3},{3,2},{4,5},{5,4},{6,7},{7,6},{8,9},{9,8},{10,11... | collective-permute-start | bytes 1769480 | tf_op jit(solution)/shard_map/ppermute | solution.py:1007
  29.9 2.4 copy-start.19
  29.9 40.1 %collective-permute-start.11 = (bf16[512,768]{1,0:T(8,128)(2,1)}, bf16[512,768]{1,0:T(8,128)(2,1)}, u32[]{:S(2)}, u32[]{:S(2)}) collective-permute-start(bf16[512,768]{1,0:T(8,128)(2,1)} %get-tuple-element.100.refs_6_), channel_id=1, source_target_pairs={{1,2},{2,1},{5,6},{6,5},{9,10},{10,9},{13,14},{14,13},{17,18},{18,... | collective-permute-start | bytes 2359304 | tf_op jit(solution)/shard_map/ppermute | solution.py:1007
  38.7 11.0 %collective-permute-start.5 = (bf16[384,576]{1,0:T(8,128)(2,1)}, bf16[384,576]{1,0:T(8,128)(2,1)}, u32[]{:S(2)}, u32[]{:S(2)}) collective-permute-start(bf16[384,576]{1,0:T(8,128)(2,1)} %shard_map.233.refs_2_), channel_id=1, source_target_pairs={{0,4},{1,5},{2,10},{3,11},{4,0},{5,1},{6,14},{7,15},{8,12},{9,13},... | collective-permute-start | bytes 1327112 | tf_op jit(solution)/shard_map/ppermute | solution.py:1007
  62.0 2.6 collective-permute-start.9
  62.1 27.3 %collective-permute-start.13 = (bf16[384,768]{1,0:T(8,128)(2,1)}, bf16[384,768]{1,0:T(8,128)(2,1)}, u32[]{:S(2)}, u32[]{:S(2)}) collective-permute-start(bf16[384,768]{1,0:T(8,128)(2,1)} %get-tuple-element.115.refs_5_), channel_id=1, source_target_pairs={{0,4},{1,5},{2,10},{3,11},{4,0},{5,1},{6,14},{7,15},{8,12},{9,13},... | collective-permute-start | bytes 1769480 | tf_op jit(solution)/shard_map/ppermute | solution.py:1007
  63.4 26.0 %collective-permute-start.14 = (bf16[384,768]{1,0:T(8,128)(2,1)}, bf16[384,768]{1,0:T(8,128)(2,1)}, u32[]{:S(2)}, u32[]{:S(2)}) collective-permute-start(bf16[384,768]{1,0:T(8,128)(2,1)} %get-tuple-element.116.refs_7_), channel_id=1, source_target_pairs={{0,4},{1,5},{2,10},{3,11},{4,0},{5,1},{6,14},{7,15},{8,12},{9,13},... | collective-permute-start | bytes 1769480 | tf_op jit(solution)/shard_map/ppermute | solution.py:1007
  64.5 0.9 copy-start.21
  68.5 1.6 copy-start
  68.5 5.2 %collective-permute-start.10 = (bf16[512,768]{1,0:T(8,128)(2,1)}, bf16[512,768]{1,0:T(8,128)(2,1)S(1)}, u32[]{:S(2)}, u32[]{:S(2)}) collective-permute-start(bf16[512,768]{1,0:T(8,128)(2,1)} %get-tuple-element.114.refs_1_.refs_2_.refs_7_), channel_id=1, source_target_pairs={{0,2},{1,3},{2,0},{3,1},{4,6},{5,7},{6,4},{7,5},{8,10},{9,11},{10,... | collective-permute-start | bytes 2359304 | tf_op jit(solution)/shard_map/ppermute | solution.py:1007
  71.3 0.9 copy-start.1
  71.3 2.4 collective-permute-start.12
  73.6 0.9 copy-start.18
  73.6 1.1 copy-start.17
  88.1 16.1 %collective-permute-start.15 = (bf16[2,384,768]{2,1,0:T(8,128)(2,1)}, bf16[2,384,768]{2,1,0:T(8,128)(2,1)}, u32[]{:S(2)}, u32[]{:S(2)}) collective-permute-start(bf16[2,384,768]{2,1,0:T(8,128)(2,1)} %get-tuple-element.123.refs_13_), channel_id=1, source_target_pairs={{0,4},{1,5},{2,10},{3,11},{4,0},{5,1},{6,14},{7,15},{8,12},{9,13},... | collective-permute-start | bytes 3538952 | tf_op jit(solution)/shard_map/ppermute | solution.py:1007
  104.2 3.2 %collective-permute-start.16 = (bf16[512,768]{1,0:T(8,128)(2,1)}, bf16[512,768]{1,0:T(8,128)(2,1)S(1)}, u32[]{:S(2)}, u32[]{:S(2)}) collective-permute-start(bf16[512,768]{1,0:T(8,128)(2,1)} %get-tuple-element.130), channel_id=1, source_target_pairs={{0,2},{1,3},{2,0},{3,1},{4,6},{5,7},{6,4},{7,5},{8,10},{9,11},{10,... | collective-permute-start | bytes 2359304 | tf_op jit(solution)/shard_map/ppermute | solution.py:1007
  104.8 31.7 %collective-permute-start.19 = (bf16[2,192,768]{2,1,0:T(8,128)(2,1)}, bf16[2,192,768]{2,1,0:T(8,128)(2,1)}, u32[]{:S(2)}, u32[]{:S(2)}) collective-permute-start(bf16[2,192,768]{2,1,0:T(8,128)(2,1)} %get-tuple-element.143), channel_id=1, source_target_pairs={{0,8},{1,9},{2,6},{3,7},{4,12},{5,13},{6,2},{7,3},{8,0},{9,1},{10,... | collective-permute-start | bytes 1769480 | tf_op jit(solution)/shard_map/ppermute | solution.py:1007
  105.9 31.8 %collective-permute-start.20 = (bf16[2,192,768]{2,1,0:T(8,128)(2,1)}, bf16[2,192,768]{2,1,0:T(8,128)(2,1)}, u32[]{:S(2)}, u32[]{:S(2)}) collective-permute-start(bf16[2,192,768]{2,1,0:T(8,128)(2,1)} %get-tuple-element.144), channel_id=1, source_target_pairs={{0,4},{1,5},{2,10},{3,11},{4,0},{5,1},{6,14},{7,15},{8,12},{9,13},... | collective-permute-start | bytes 1769480 | tf_op jit(solution)/shard_map/ppermute | solution.py:1007
  107.2 31.6 %collective-permute-start.21 = (bf16[2,192,768]{2,1,0:T(8,128)(2,1)}, bf16[2,192,768]{2,1,0:T(8,128)(2,1)}, u32[]{:S(2)}, u32[]{:S(2)}) collective-permute-start(bf16[2,192,768]{2,1,0:T(8,128)(2,1)} %get-tuple-element.131.refs_5_), channel_id=1, source_target_pairs={{0,12},{1,13},{2,14},{3,15},{4,8},{5,9},{6,10},{7,11},{8,4},{9,5},... | collective-permute-start | bytes 1769480 | tf_op jit(solution)/shard_map/ppermute | solution.py:1007
  112.3 4.9 %collective-permute-start.17 = (bf16[512,768]{1,0:T(8,128)(2,1)}, bf16[512,768]{1,0:T(8,128)(2,1)S(1)}, u32[]{:S(2)}, u32[]{:S(2)}) collective-permute-start(bf16[512,768]{1,0:T(8,128)(2,1)} %get-tuple-element.132.refs_1_), channel_id=1, source_target_pairs={{0,2},{1,3},{2,0},{3,1},{4,6},{5,7},{6,4},{7,5},{8,10},{9,11},{10,... | collective-permute-start | bytes 2359304 | tf_op jit(solution)/shard_map/ppermute | solution.py:1007
  116.0 23.4 %collective-permute-start.18 = (bf16[2,192,768]{2,1,0:T(8,128)(2,1)}, bf16[2,192,768]{2,1,0:T(8,128)(2,1)}, u32[]{:S(2)}, u32[]{:S(2)}) collective-permute-start(bf16[2,192,768]{2,1,0:T(8,128)(2,1)} %get-tuple-element.139.refs_8_), channel_id=1, source_target_pairs={{0,8},{1,9},{2,6},{3,7},{4,12},{5,13},{6,2},{7,3},{8,0},{9,1},{10,... | collective-permute-start | bytes 1769480 | tf_op jit(solution)/shard_map/ppermute | solution.py:1007
  136.2 24.8 %collective-permute-start.23 = (bf16[1,192,768]{2,1,0:T(8,128)(2,1)}, bf16[1,192,768]{2,1,0:T(8,128)(2,1)}, u32[]{:S(2)}, u32[]{:S(2)}) collective-permute-start(bf16[1,192,768]{2,1,0:T(8,128)(2,1)} %get-tuple-element.155), channel_id=1, source_target_pairs={{0,8},{1,9},{2,6},{3,7},{4,12},{5,13},{6,2},{7,3},{8,0},{9,1},{10,... | collective-permute-start | bytes 884744 | tf_op jit(solution)/shard_map/ppermute | solution.py:1007
  136.4 24.5 %collective-permute-start.24 = (bf16[1,192,768]{2,1,0:T(8,128)(2,1)}, bf16[1,192,768]{2,1,0:T(8,128)(2,1)}, u32[]{:S(2)}, u32[]{:S(2)}) collective-permute-start(bf16[1,192,768]{2,1,0:T(8,128)(2,1)} %get-tuple-element.156), channel_id=1, source_target_pairs={{0,4},{1,5},{2,10},{3,11},{4,0},{5,1},{6,14},{7,15},{8,12},{9,13},... | collective-permute-start | bytes 884744 | tf_op jit(solution)/shard_map/ppermute | solution.py:1007
  137.7 23.3 %collective-permute-start.25 = (bf16[1,192,768]{2,1,0:T(8,128)(2,1)}, bf16[1,192,768]{2,1,0:T(8,128)(2,1)}, u32[]{:S(2)}, u32[]{:S(2)}) collective-permute-start(bf16[1,192,768]{2,1,0:T(8,128)(2,1)} %get-tuple-element.147.refs_6_), channel_id=1, source_target_pairs={{0,12},{1,13},{2,14},{3,15},{4,8},{5,9},{6,10},{7,11},{8,4},{9,5},... | collective-permute-start | bytes 884744 | tf_op jit(solution)/shard_map/ppermute | solution.py:1007
  142.6 18.4 %collective-permute-start.26 = (bf16[2,192,768]{2,1,0:T(8,128)(2,1)}, bf16[2,192,768]{2,1,0:T(8,128)(2,1)}, u32[]{:S(2)}, u32[]{:S(2)}) collective-permute-start(bf16[2,192,768]{2,1,0:T(8,128)(2,1)} %get-tuple-element.148.refs_9_), channel_id=1, source_target_pairs={{0,1},{1,0},{2,3},{3,2},{4,5},{5,4},{6,7},{7,6},{8,9},{9,8},{10,11... | collective-permute-start | bytes 1769480 | tf_op jit(solution)/shard_map/ppermute | solution.py:1007
  159.4 9.3 %collective-permute-start.22 = (bf16[1024,1024]{1,0:T(8,128)(2,1)}, bf16[1024,1024]{1,0:T(8,128)(2,1)S(1)}, u32[]{:S(2)}, u32[]{:S(2)}) collective-permute-start(bf16[1024,1024]{1,0:T(8,128)(2,1)} %get-tuple-element.149.refs_10_.refs_1_), channel_id=1, source_target_pairs={{0,2},{1,3},{2,0},{3,1},{4,6},{5,7},{6,4},{7,5},{8,10},{9,11},{10,... | collective-permute-start | bytes 6291464 | tf_op jit(solution)/shard_map/ppermute | solution.py:1007
  166.0 18.5 %collective-permute-start.27 = (bf16[1,192,768]{2,1,0:T(8,128)(2,1)}, bf16[1,192,768]{2,1,0:T(8,128)(2,1)}, u32[]{:S(2)}, u32[]{:S(2)}) collective-permute-start(bf16[1,192,768]{2,1,0:T(8,128)(2,1)} %get-tuple-element.163), channel_id=1, source_target_pairs={{0,8},{1,9},{2,6},{3,7},{4,12},{5,13},{6,2},{7,3},{8,0},{9,1},{10,... | collective-permute-start | bytes 884744 | tf_op jit(solution)/shard_map/ppermute | solution.py:1007
  166.9 21.0 %collective-permute-start.28 = (bf16[1,192,768]{2,1,0:T(8,128)(2,1)}, bf16[1,192,768]{2,1,0:T(8,128)(2,1)}, u32[]{:S(2)}, u32[]{:S(2)}) collective-permute-start(bf16[1,192,768]{2,1,0:T(8,128)(2,1)} %get-tuple-element.164), channel_id=1, source_target_pairs={{0,4},{1,5},{2,10},{3,11},{4,0},{5,1},{6,14},{7,15},{8,12},{9,13},... | collective-permute-start | bytes 884744 | tf_op jit(solution)/shard_map/ppermute | solution.py:1007
  168.1 19.7 %collective-permute-start.30 = (bf16[1,192,768]{2,1,0:T(8,128)(2,1)}, bf16[1,192,768]{2,1,0:T(8,128)(2,1)}, u32[]{:S(2)}, u32[]{:S(2)}) collective-permute-start(bf16[1,192,768]{2,1,0:T(8,128)(2,1)} %get-tuple-element.165), channel_id=1, source_target_pairs={{0,1},{1,0},{2,3},{3,2},{4,5},{5,4},{6,7},{7,6},{8,9},{9,8},{10,11... | collective-permute-start | bytes 884744 | tf_op jit(solution)/shard_map/ppermute | solution.py:1007
  168.1 26.2 %collective-permute-start.29 = (bf16[1,192,768]{2,1,0:T(8,128)(2,1)}, bf16[1,192,768]{2,1,0:T(8,128)(2,1)}, u32[]{:S(2)}, u32[]{:S(2)}) collective-permute-start(bf16[1,192,768]{2,1,0:T(8,128)(2,1)} %get-tuple-element.158.refs_14_), channel_id=1, source_target_pairs={{0,12},{1,13},{2,14},{3,15},{4,8},{5,9},{6,10},{7,11},{8,4},{9,5},... | collective-permute-start | bytes 884744 | tf_op jit(solution)/shard_map/ppermute | solution.py:1007
  168.7 2.3 copy-start.12
  168.7 25.7 %collective-permute-start.34 = (bf16[2,192,768]{2,1,0:T(8,128)(2,1)}, bf16[2,192,768]{2,1,0:T(8,128)(2,1)}, u32[]{:S(2)}, u32[]{:S(2)}) collective-permute-start(bf16[2,192,768]{2,1,0:T(8,128)(2,1)} %get-tuple-element.171.refs_0_), channel_id=1, source_target_pairs={{0,16},{1,17},{2,18},{3,19},{4,20},{5,21},{6,22},{7,23},{8,24},{9,... | collective-permute-start | bytes 1769480 | tf_op jit(solution)/shard_map/ppermute | solution.py:1007
  171.0 13.4 %copy-start.14 = (bf16[512,768]{1,0:T(8,128)(2,1)S(1)}, bf16[512,768]{1,0:T(8,128)(2,1)}, u32[]{:S(2)}) copy-start(bf16[512,768]{1,0:T(8,128)(2,1)} %get-tuple-element.169) | copy-start | bytes 2359300
  184.5 22.0 %collective-permute-start.32 = (bf16[512,768]{1,0:T(8,128)(2,1)S(1)}, bf16[512,768]{1,0:T(8,128)(2,1)S(1)}, u32[]{:S(2)}, u32[]{:S(2)}) collective-permute-start(bf16[512,768]{1,0:T(8,128)(2,1)S(1)} %copy-done.14), channel_id=1, source_target_pairs={{0,2},{1,3},{2,0},{3,1},{4,6},{5,7},{6,4},{7,5},{8,10},{9,11},{10,... | collective-permute-start | bytes 2359304 | tf_op jit(solution)/shard_map/ppermute | solution.py:1007
  194.4 6.0 %copy-start.3 = (bf16[512,768]{1,0:T(8,128)(2,1)S(1)}, bf16[512,768]{1,0:T(8,128)(2,1)}, u32[]{:S(2)}) copy-start(bf16[512,768]{1,0:T(8,128)(2,1)} %get-tuple-element.166) | copy-start | bytes 2359300
  194.4 6.0 %collective-permute-start.33 = (bf16[80,768]{1,0:T(8,128)(2,1)}, bf16[80,768]{1,0:T(8,128)(2,1)S(1)}, u32[]{:S(2)}, u32[]{:S(2)}) collective-permute-start(bf16[80,768]{1,0:T(8,128)(2,1)} %get-tuple-element.170.refs_2_.refs_0_), channel_id=1, source_target_pairs={{0,1},{1,0},{2,3},{3,2},{4,5},{5,4},{6,7},{7,6},{8,9},{9,8},{10,11... | collective-permute-start | bytes 368648 | tf_op jit(solution)/shard_map/ppermute | solution.py:1007
  196.6 36.5 %collective-permute-start.39 = (bf16[2,192,768]{2,1,0:T(8,128)(2,1)}, bf16[2,192,768]{2,1,0:T(8,128)(2,1)}, u32[]{:S(2)}, u32[]{:S(2)}) collective-permute-start(bf16[2,192,768]{2,1,0:T(8,128)(2,1)} %shard_map.254.refs_7_.refs_3_), channel_id=1, source_target_pairs={{0,12},{1,13},{2,14},{3,15},{4,8},{5,9},{6,10},{7,11},{8,4},{9,5},... | collective-permute-start | bytes 1769480 | tf_op jit(solution)/shard_map/ppermute | solution.py:1007
  199.7 33.5 %collective-permute-start.38 = (bf16[2,192,768]{2,1,0:T(8,128)(2,1)}, bf16[2,192,768]{2,1,0:T(8,128)(2,1)}, u32[]{:S(2)}, u32[]{:S(2)}) collective-permute-start(bf16[2,192,768]{2,1,0:T(8,128)(2,1)} %shard_map.254.refs_7_.refs_3_), channel_id=1, source_target_pairs={{0,4},{1,5},{2,10},{3,11},{4,0},{5,1},{6,14},{7,15},{8,12},{9,13},... | collective-permute-start | bytes 1769480 | tf_op jit(solution)/shard_map/ppermute | solution.py:1007
  199.7 33.5 %collective-permute-start.37 = (bf16[2,192,768]{2,1,0:T(8,128)(2,1)}, bf16[2,192,768]{2,1,0:T(8,128)(2,1)}, u32[]{:S(2)}, u32[]{:S(2)}) collective-permute-start(bf16[2,192,768]{2,1,0:T(8,128)(2,1)} %shard_map.254.refs_7_.refs_3_), channel_id=1, source_target_pairs={{0,8},{1,9},{2,6},{3,7},{4,12},{5,13},{6,2},{7,3},{8,0},{9,1},{10,... | collective-permute-start | bytes 1769480 | tf_op jit(solution)/shard_map/ppermute | solution.py:1007
  200.3 3.8 %copy-start.23 = (bf16[80,768]{1,0:T(8,128)(2,1)}, bf16[80,768]{1,0:T(8,128)(2,1)S(1)}, u32[]{:S(2)}) copy-start(bf16[80,768]{1,0:T(8,128)(2,1)S(1)} %collective-permute-done.33.refs_1_) | copy-start | bytes 368644
  200.3 8.0 %collective-permute-start.31 = (bf16[512,768]{1,0:T(8,128)(2,1)S(1)}, bf16[512,768]{1,0:T(8,128)(2,1)S(1)}, u32[]{:S(2)}, u32[]{:S(2)}) collective-permute-start(bf16[512,768]{1,0:T(8,128)(2,1)S(1)} %copy-done.3), channel_id=1, source_target_pairs={{0,2},{1,3},{2,0},{3,1},{4,6},{5,7},{6,4},{7,5},{8,10},{9,11},{10,... | collective-permute-start | bytes 2359304 | tf_op jit(solution)/shard_map/ppermute | solution.py:1007
  206.5 1.9 copy-start.16
  206.5 25.9 %collective-permute-start.35 = (bf16[272,768]{1,0:T(8,128)(2,1)}, bf16[272,768]{1,0:T(8,128)(2,1)S(1)}, u32[]{:S(2)}, u32[]{:S(2)}) collective-permute-start(bf16[272,768]{1,0:T(8,128)(2,1)} %shard_map.255.refs_8_.refs_1_), channel_id=1, source_target_pairs={{0,16},{1,17},{2,18},{3,19},{4,20},{5,21},{6,22},{7,23},{8,24},{9,... | collective-permute-start | bytes 1253384 | tf_op jit(solution)/shard_map/ppermute | solution.py:1007
  236.8 10.8 %collective-permute-start.43 = (bf16[2,768,768]{2,1,0:T(8,128)(2,1)}, bf16[2,768,768]{2,1,0:T(8,128)(2,1)S(1)}, u32[]{:S(2)}, u32[]{:S(2)}) collective-permute-start(bf16[2,768,768]{2,1,0:T(8,128)(2,1)} %get-tuple-element.173.refs_1_.refs_3_), channel_id=1, source_target_pairs={{0,2},{1,3},{2,0},{3,1},{4,6},{5,7},{6,4},{7,5},{8,10},{9,11},{10,... | collective-permute-start | bytes 7077896 | tf_op jit(solution)/shard_map/ppermute | solution.py:1007
  239.6 16.2 %collective-permute-start.42 = (bf16[272,768]{1,0:T(8,128)(2,1)}, bf16[272,768]{1,0:T(8,128)(2,1)}, u32[]{:S(2)}, u32[]{:S(2)}) collective-permute-start(bf16[272,768]{1,0:T(8,128)(2,1)} %get-tuple-element.172.refs_1_), channel_id=1, source_target_pairs={{0,12},{1,13},{2,14},{3,15},{4,8},{5,9},{6,10},{7,11},{8,4},{9,5},... | collective-permute-start | bytes 1253384 | tf_op jit(solution)/shard_map/ppermute | solution.py:1007
  242.6 19.3 %collective-permute-start.41 = (bf16[272,768]{1,0:T(8,128)(2,1)}, bf16[272,768]{1,0:T(8,128)(2,1)}, u32[]{:S(2)}, u32[]{:S(2)}) collective-permute-start(bf16[272,768]{1,0:T(8,128)(2,1)} %get-tuple-element.172.refs_1_), channel_id=1, source_target_pairs={{0,4},{1,5},{2,10},{3,11},{4,0},{5,1},{6,14},{7,15},{8,12},{9,13},... | collective-permute-start | bytes 1253384 | tf_op jit(solution)/shard_map/ppermute | solution.py:1007
  242.6 19.4 %collective-permute-start.40 = (bf16[272,768]{1,0:T(8,128)(2,1)}, bf16[272,768]{1,0:T(8,128)(2,1)}, u32[]{:S(2)}, u32[]{:S(2)}) collective-permute-start(bf16[272,768]{1,0:T(8,128)(2,1)} %get-tuple-element.172.refs_1_), channel_id=1, source_target_pairs={{0,8},{1,9},{2,6},{3,7},{4,12},{5,13},{6,2},{7,3},{8,0},{9,1},{10,... | collective-permute-start | bytes 1253384 | tf_op jit(solution)/shard_map/ppermute | solution.py:1007
  243.7 22.3 %collective-permute-start.36 = (bf16[2,512,768]{2,1,0:T(8,128)(2,1)}, bf16[2,512,768]{2,1,0:T(8,128)(2,1)}, u32[]{:S(2)}, u32[]{:S(2)}) collective-permute-start(bf16[2,512,768]{2,1,0:T(8,128)(2,1)} %shard_map.257.refs_7_.refs_1_), channel_id=1, source_target_pairs={{1,2},{2,1},{5,6},{6,5},{9,10},{10,9},{13,14},{14,13},{17,18},{18,... | collective-permute-start | bytes 4718600 | tf_op jit(solution)/shard_map/ppermute | solution.py:1007
  247.6 1.4 copy-start.11
  264.6 4.6 %collective-permute-start.44 = (bf16[848,768]{1,0:T(8,128)(2,1)}, bf16[848,768]{1,0:T(8,128)(2,1)S(1)}, u32[]{:S(2)}, u32[]{:S(2)}) collective-permute-start(bf16[848,768]{1,0:T(8,128)(2,1)} %shard_map.260.refs_3_.refs_1_), channel_id=1, source_target_pairs={{0,2},{1,3},{2,0},{3,1},{4,6},{5,7},{6,4},{7,5},{8,10},{9,11},{10,... | collective-permute-start | bytes 3907592 | tf_op jit(solution)/shard_map/ppermute | solution.py:1007
  269.1 1.1 copy-start.13
  (5 other events, 4.3 us)

commit v2 on v1

--- a/solution.py
+++ b/solution.py
@@ -223,8 +223,10 @@
     )
 
 
-def norm1_kernel(tokens, gain, shift, out):
-    scaled, _ = normalize(tokens[...].astype(F32))
+def norm1_kernel(place, tokens, moved, gain, shift, mine, out):
+    rows = jnp.where(place[0] == place[1], tokens[...], moved[...])
+    mine[...] = rows
+    scaled, _ = normalize(rows.astype(F32))
     out[...] = (scaled * gain[...] + shift[...]).astype(BF16)
 
 
@@ -232,8 +234,15 @@
     return pl.BlockSpec((block, dim), lambda i: (i, 0))
 
 
-def norm1_call(order, tokens, gain, shift):
-    return order.run(2.5, norm1_kernel, (tokens, gain, shift), sds(tokens.shape, BF16))
+def norm1_call(order, place, tokens, moved, gain, shift):
+    shape = sds(tokens.shape, BF16)
+    return order.run(
+        2.5,
+        norm1_kernel,
+        (place, tokens, moved, gain, shift),
+        [shape, shape],
+        [SMEM] + [VMEM] * 4,
+    )
 
 
 def masks(seg_pad, cols, low, high):
@@ -747,9 +756,7 @@
     norms = jnp.concatenate([gain_sum, shift_sum, sums2[0:2, :], sums2[4:8, :]], axis=0)
     rows = extra_w.shape[0]
     late[:rows, :] = extra_w[...]
-    high, low = halves(norms)
-    late[rows : rows + 8, :] = high
-    late[rows + 8 :, :] = low
+    late[rows:, :] = pack_norms(norms)
 
 
 def norm1_grad_call(order, place, logits, qk0, seg_pad, n1, grads, weights, first, *rest):
@@ -796,6 +803,16 @@
     )
 
 
+def pack_norms(norms):
+    high = norms.astype(BF16).astype(F32)
+    return jnp.concatenate([high, norms - high], axis=0).astype(BF16)
+
+
+def unpack_norms(ref, rows):
+    both = ref[rows:, :].astype(F32)
+    return both[:8] + both[8:]
+
+
 def add_late(terms, out):
     def pairs(values):
         while len(values) > 1:
@@ -804,12 +821,7 @@
 
     rows = out.shape[0] - 16
     out[:rows, :] = pairs([term[:rows, :].astype(F32) for term in terms]).astype(BF16)
-    norms = pairs(
-        [term[rows : rows + 8, :].astype(F32) + term[rows + 8 :, :].astype(F32) for term in terms]
-    )
-    high, low = halves(norms)
-    out[rows : rows + 8, :] = high
-    out[rows + 8 :, :] = low
+    out[rows:, :] = pack_norms(pairs([unpack_norms(term, rows) for term in terms]))
 
 
 def first_sums_kernel(*refs):
@@ -908,9 +920,7 @@
     width = w_out.shape[0] // 2
     late = 4 * width
     rows = late + HEAD_DIM
-    total = jnp.zeros((8, near.shape[1]), F32)
-    for ref in (near, far):
-        total = total + (ref[rows : rows + 8, :].astype(F32) + ref[rows + 8 :, :].astype(F32))
+    total = unpack_norms(near, rows) + unpack_norms(far, rows)
     for i, out in enumerate(norms):
         out[...] = total[i]
     here = (place[1] == 0).astype(F32)
@@ -987,8 +997,11 @@
             lambda chip, core, part: (chip ^ (turned if core else in_order)[bit], core, part)
         )
 
-    by_role = pairs(lambda chip, core, part: (chip, part, core))
-    swapped = [pair for pair in by_role if pair[0] != pair[1]]
+    swapped = [
+        pair
+        for pair in pairs(lambda chip, core, part: (chip, part, core))
+        if pair[0] != pair[1]
+    ]
     by_core = pairs(lambda chip, core, part: (chip, 1 - core, part))
     by_part = pairs(lambda chip, core, part: (chip, core, 1 - part))
     from_first_part = [pair for pair in by_part if pair[0] % parts == 0]
@@ -1045,7 +1058,7 @@
             vector[None, :] for vector in (norm1_gain, norm1_shift, norm2_gain, norm2_shift)
         )
 
-        mine = move(tokens, by_role)
+        moved = move(tokens, swapped)
         ints = jnp.concatenate([segment_ids, pad_mask], axis=0)
         ints = jnp.where(core == part, ints, move(ints, by_core)).astype(F32)
         seg_pad = jnp.concatenate([ints, jnp.zeros((6, ints.shape[1]), F32)], axis=0)
@@ -1053,7 +1066,7 @@
         qkv_l, qkv_s, first = pack_first_call(order, place, w_query, w_key, w_value)
         first_moved = move(first, from_first_part)
         qkv_near = move(qkv_s, by_part)
-        n1_own = norm1_call(order, mine, gain1, shift1)
+        mine, n1_own = norm1_call(order, place, tokens, moved, gain1, shift1)
         n1_other = move(n1_own, by_core)
         out_l, up_l, up_s, down_l, down_s, grad = pack_last_call(
             order, place, w_out, w_up, w_down, cotangent

time: 280 us -> 280 us (level)
  no operation moved by 1% of the time
where the time goes in v2:
time: 280 us; the launch traced here: 275 us
  Pallas kernels  162 us (58%)
  starting transfers between devices  58.3 us (21%)
  waiting for transfers between devices  38.6 us (14%)
  local copies, waits for them, and re-layouts  13.2 us (5%)
    pallas_call x25, Pallas kernels, run(): pl.pallas_call(body, out_shape=out_shape, in_specs=in_specs, compiler_par...  162 us
    ppermute x45, starting transfers between devices, move(): return lax.ppermute(value, axes, how)  58.3 us
    ppermute x45, waiting for transfers between devices, move(): return lax.ppermute(value, axes, how)  38.6 us
    unnamed x48, local copies, waits for them, and re-layouts  9.66 us
  transfers between devices with their start and end apart: 45, of which 11 were waited for; matrix products, arithmetic and copies ran while one was open for 2% of the time, Pallas kernels for 56%

profile of v2, /device:TPU:1, one launch (start us, length us, event | category | flops | bytes accessed | tf_op | source)
XLA Modules:
  0.0 275.0 jit_solution(16019081237364901896)
XLA Ops:
  1.5 4.5 %collective-permute-start = (bf16[512,768]{1,0:T(8,128)(2,1)}, bf16[512,768]{1,0:T(8,128)(2,1)S(1)}, u32[]{:S(2)}, u32[]{:S(2)}) collective-permute-start(bf16[512,768]{1,0:T(8,128)(2,1)} %refs_1_.4), channel_id=1, source_target_pairs={{1,2},{2,1},{5,6},{6,5},{9,10},{10,9},{13,14},{14,13},{17,18},{18,... | collective-permute-start | bytes 2359304 | tf_op jit(solution)/shard_map/ppermute | solution.py:1020
  6.7 3.1 %shard_map.229 = (bf16[768,576]{1,0:T(8,128)(2,1)}, bf16[384,576]{1,0:T(8,128)(2,1)}, bf16[768,128]{1,0:T(8,128)(2,1)}) custom-call(s32[5]{0:T(128)} %stack.35.refs_0_, bf16[768,384]{1,0:T(8,128)(2,1)} %refs_1_.3, bf16[768,384]{1,0:T(8,128)(2,1)} %refs_2_.2, bf16[768,384]{1,0:T(8,128)(2,1)} %refs_3_.2), custom_call_target="tpu_custom_call" | custom-call | flops 92000002048 | tf_op jit(solution)/shard_map/pallas_call | solution.py:60
  9.8 2.0 collective-permute-start.2
  14.7 2.7 collective-permute-done.refs_2_
  18.3 2.9 %shard_map.230 = (bf16[512,768]{1,0:T(8,128)(2,1)}, bf16[512,768]{1,0:T(8,128)(2,1)}) custom-call(s32[5]{0:T(128)} %stack.35.refs_0_, bf16[512,768]{1,0:T(8,128)(2,1)} %refs_1_.4, bf16[512,768]{1,0:T(8,128)(2,1)} %copy-done.14, f32[1,768]{1,0:T(1,128)} %broadcast_in_dim.13.refs_3_.refs_11_.refs_4_, f32[1,768]{1,0:T(1,128)} %broadcast_in_dim.14.refs_4_.refs_12_, ...), custom_call_target="tpu_custom_call" | custom-call | flops 57500000256 | tf_op jit(solution)/shard_map/pallas_call | solution.py:60
  21.2 5.1 %shard_map.231 = (bf16[192,768]{1,0:T(8,128)(2,1)}, bf16[768,768]{1,0:T(8,128)(2,1)}, bf16[384,768]{1,0:T(8,128)(2,1)}, bf16[768,768]{1,0:T(8,128)(2,1)}, bf16[3...) custom-call(s32[5]{0:T(128)} %stack.35.refs_0_, bf16[384,768]{1,0:T(8,128)(2,1)} %refs_1_.5, bf16[768,1536]{1,0:T(8,128)(2,1)} %refs_2_.3, ...), custom_call_target="tpu_custom_call" | custom-call | flops 115000000512 | tf_op jit(solution)/shard_map/pallas_call | solution.py:60
  26.3 2.5 collective-permute-start.6
  28.8 1.4 collective-permute-start.8
  30.3 2.4 collective-permute-start.11
  32.7 6.4 %shard_map.232 = (bf16[1024,768]{1,0:T(8,128)(2,1)}, f32[1024,1024]{1,0:T(8,128)}, bf16[128,1024]{1,0:T(8,128)(2,1)}, bf16[768,128]{1,0:T(8,128)(2,1)}) custom-call(s32[5]{0:T(128)} %stack.35.refs_0_, bf16[512,768]{1,0:T(8,128)(2,1)} %get-tuple-element.103.refs_5_.refs_1_, bf16[512,768]{1,0:T(8,128)(2,1)} %copy-done.19, ...), custom_call_target="tpu_custom_call" | custom-call | flops 149500002304 | tf_op jit(solution)/shard_map/pallas_call | solution.py:60
  39.1 2.1 collective-permute-start.5
  41.2 9.4 %shard_map.234 = (bf16[576,1024]{1,0:T(8,128)(2,1)}, bf16[192,1024]{1,0:T(8,128)(2,1)}, f32[3,1,1024]{2,1,0:T(1,128)}) custom-call(bf16[1024,768]{1,0:T(8,128)(2,1)} %get-tuple-element.105.refs_0_.refs_1_.refs_5_, bf16[768,576]{1,0:T(8,128)(2,1)} %get-tuple-element.108.refs_1_.refs_7_, f32[1024,1024]{1,0:T(8,128)} %get-tuple-element.107.refs_1_.refs_2_.refs_4_.refs_7_, ...), custom_call_target="tpu_custom_call" | custom-call | flops 230000001024 | tf_op jit(solution)/shard_map/pallas_call | solution.py:60
  50.6 12.2 %shard_map.235 = (bf16[576,1024]{1,0:T(8,128)(2,1)}, bf16[192,1024]{1,0:T(8,128)(2,1)}, f32[3,1,1024]{2,1,0:T(1,128)}, bf16[768,576]{1,0:T(8,128)(2,1)}, f32[512,768]{1,0:T(8,128)}, /*index=5*/bf16[512,768]{1,0:T(8,128)(2,1)}) custom-call(s32[5]{0:T(128)} %stack.35.refs_0_, bf16[1024,768]{1,0:T(8,128)(2,1)} %get-tuple-element.105.refs_0_.refs_1_.refs_5_, ...), custom_call_target="tpu_custom_call" | custom-call | flops 230000001024 | tf_op jit(solution)/shard_map/pallas_call | solution.py:60
  62.9 1.3 collective-permute-start.13
  64.5 0.9 collective-permute-done.9.refs_2_
  65.4 0.9 copy-done.21
  66.3 3.0 %shard_map.238 = (f32[512,768]{1,0:T(8,128)}, bf16[512,768]{1,0:T(8,128)(2,1)}) custom-call(bf16[512,768]{1,0:T(8,128)(2,1)} %shard_map.237.refs_0_.refs_2_, f32[512,768]{1,0:T(8,128)} %get-tuple-element.116.refs_1_, bf16[512,768]{1,0:T(8,128)(2,1)} %copy-done.21, f32[1,768]{1,0:T(1,128)} %broadcast_in_dim.15.refs_3_.refs_4_, ...), custom_call_target="tpu_custom_call" | custom-call | flops 92000002048 | tf_op jit(solution)/shard_map/pallas_call | solution.py:60
  69.5 0.9 collective-permute-done.11.refs_0_
  70.5 1.2 broadcast_select_fusion.refs_4_.refs_3_
  72.6 1.5 collective-permute-done.12.refs_3_
  74.0 0.9 copy-done.18
  75.2 13.3 %shard_map.242 = (bf16[512,768]{1,0:T(8,128)(2,1)}, bf16[512,768]{1,0:T(8,128)(2,1)}, bf16[512,768]{1,0:T(8,128)(2,1)}, bf16[512,768]{1,0:T(8,128)(2,1)}, bf16[2...) custom-call(s32[5]{0:T(128)} %stack.35.refs_0_, bf16[512,768]{1,0:T(8,128)(2,1)} %copy-done.17, ...), custom_call_target="tpu_custom_call" | custom-call | flops 335800008704 | tf_op jit(solution)/shard_map/pallas_call | solution.py:60
  88.5 1.2 collective-permute-start.15
  89.8 14.8 %shard_map.243 = (bf16[512,768]{1,0:T(8,128)(2,1)}, bf16[512,768]{1,0:T(8,128)(2,1)}, bf16[512,768]{1,0:T(8,128)(2,1)}, bf16[512,768]{1,0:T(8,128)(2,1)}, bf16[2...) custom-call(s32[5]{0:T(128)} %stack.35.refs_0_, ...), custom_call_target="tpu_custom_call" | custom-call | flops 335800008704 | tf_op jit(solution)/shard_map/pallas_call | solution.py:60
  105.2 1.2 collective-permute-start.19
  106.4 1.2 collective-permute-start.20
  108.7 4.0 %shard_map.245 = (f32[512,768]{1,0:T(8,128)}, bf16[512,768]{1,0:T(8,128)(2,1)}, f32[8,768]{1,0:T(8,128)}) custom-call(f32[512,768]{1,0:T(8,128)} %get-tuple-element.117.refs_0_.refs_5_, bf16[512,768]{1,0:T(8,128)(2,1)} %get-tuple-element.128.refs_1_, bf16[512,768]{1,0:T(8,128)(2,1)} %copy-done.22, bf16[512,768]{1,0:T(8,128)(2,1)} %copy-done.1, ...), custom_call_target="tpu_custom_call" | custom-call | flops 115000000512 | tf_op jit(solution)/shard_map/pallas_call | solution.py:60
  112.7 0.9 collective-permute-start.17
  113.6 2.9 %shard_map.246 = (bf16[2,192,768]{2,1,0:T(8,128)(2,1)}, bf16[2,192,768]{2,1,0:T(8,128)(2,1)}) custom-call(s32[5]{0:T(128)} %stack.35.refs_0_, bf16[2,384,768]{2,1,0:T(8,128)(2,1)} %get-tuple-element.141.refs_1_, bf16[2,384,768]{2,1,0:T(8,128)(2,1)} %collective-permute-done.15.refs_5_.refs_2_, f32[8,768]{1,0:T(8,128)} %get-tuple-element.142.refs_3_.refs_13_), custom_call_target="tpu_custom_call" | custom-call | flops 69000003584 | tf_op jit(solution)/shard_map/pallas_call | solution.py:60
  116.4 1.2 collective-permute-start.18
  118.5 14.1 %shard_map.247 = (bf16[576,1024]{1,0:T(8,128)(2,1)}, bf16[192,768]{1,0:T(8,128)(2,1)}, f32[1024,1024]{1,0:T(8,128)}) custom-call(s32[5]{0:T(128)} %stack.35.refs_0_, bf16[512,768]{1,0:T(8,128)(2,1)} %get-tuple-element.136.refs_1_, bf16[512,768]{1,0:T(8,128)(2,1)} %copy-done.15, bf16[192,768]{1,0:T(8,128)(2,1)} %collective-permute-done.6.refs_7_.refs_3_, ...), custom_call_target="tpu_custom_call" | custom-call | flops 368000008192 | tf_op jit(solution)/shard_map/pallas_call | solution.py:60
  132.6 4.0 %shard_map.248 = (bf16[1,192,768]{2,1,0:T(8,128)(2,1)}, bf16[1,192,768]{2,1,0:T(8,128)(2,1)}, bf16[1,192,768]{2,1,0:T(8,128)(2,1)}, bf16[1,192,768]{2,1,0:T(8,128)(2,1)}) custom-call(s32[5]{0:T(128)} %stack.35.refs_0_, bf16[1024,768]{1,0:T(8,128)(2,1)} %get-tuple-element.105.refs_0_.refs_1_.refs_5_, bf16[576,1024]{1,0:T(8,128)(2,1)} %get-tuple-element.149.refs_2_.refs_9_, ...), custom_call_target="tpu_custom_call" | custom-call | flops 92000002048 | tf_op jit(solution)/shard_map/pallas_call | solution.py:60
  136.9 1.2 collective-permute-start.24
  138.1 1.1 collective-permute-start.25
  139.8 3.2 %shard_map.249 = (bf16[2,192,768]{2,1,0:T(8,128)(2,1)}, bf16[2,192,768]{2,1,0:T(8,128)(2,1)}) custom-call(bf16[2,192,768]{2,1,0:T(8,128)(2,1)} %get-tuple-element.145.refs_0_, bf16[2,192,768]{2,1,0:T(8,128)(2,1)} %collective-permute-done.18.refs_1_, bf16[2,192,768]{2,1,0:T(8,128)(2,1)} %get-tuple-element.146.refs_2_, ...), custom_call_target="tpu_custom_call" | custom-call | flops 69000003584 | tf_op jit(solution)/shard_map/pallas_call | solution.py:60
  143.0 2.0 collective-permute-start.26
  145.0 14.4 %shard_map.250 = (bf16[576,1024]{1,0:T(8,128)(2,1)}, bf16[192,768]{1,0:T(8,128)(2,1)}, bf16[1024,1024]{1,0:T(8,128)(2,1)}) custom-call(s32[5]{0:T(128)} %stack.35.refs_0_, bf16[512,768]{1,0:T(8,128)(2,1)} %get-tuple-element.136.refs_1_, bf16[512,768]{1,0:T(8,128)(2,1)} %copy-done.15, bf16[192,768]{1,0:T(8,128)(2,1)} %get-tuple-element.111.refs_6_.refs_3_, ...), custom_call_target="tpu_custom_call" | custom-call | flops 368000008192 | tf_op jit(solution)/shard_map/pallas_call | solution.py:60
  159.4 1.5 collective-permute-start.22
  160.9 5.0 %shard_map.251 = (bf16[1,192,768]{2,1,0:T(8,128)(2,1)}, bf16[2,192,768]{2,1,0:T(8,128)(2,1)}, bf16[1,192,768]{2,1,0:T(8,128)(2,1)}, bf16[1,192,768]{2,1,0:T(8,12...) custom-call(s32[5]{0:T(128)} %stack.35.refs_0_, ...), custom_call_target="tpu_custom_call" | custom-call | flops 138000007168 | tf_op jit(solution)/shard_map/pallas_call | solution.py:60
  166.8 1.3 collective-permute-start.28
  168.7 2.3 collective-permute-start.34
  171.0 13.5 %shard_map.252 = (f32[512,768]{1,0:T(8,128)}, bf16[512,768]{1,0:T(8,128)(2,1)}, bf16[80,768]{1,0:T(8,128)(2,1)}) custom-call(s32[5]{0:T(128)} %stack.35.refs_0_, bf16[1024,1024]{1,0:T(8,128)(2,1)} %get-tuple-element.153.refs_10_.refs_1_, bf16[1024,1024]{1,0:T(8,128)(2,1)} %copy-done.11, bf16[128,1024]{1,0:T(8,128)(2,1)} %get-tuple-element.154.refs_3_, ...), custom_call_target="tpu_custom_call" | custom-call | flops 321999994880 | tf_op jit(solution)/shard_map/pallas_call | solution.py:60
  184.5 3.1 %collective-permute-start.32 = (bf16[512,768]{1,0:T(8,128)(2,1)S(1)}, bf16[512,768]{1,0:T(8,128)(2,1)S(1)}, u32[]{:S(2)}, u32[]{:S(2)}) collective-permute-start(bf16[512,768]{1,0:T(8,128)(2,1)S(1)} %copy-done.13), channel_id=1, source_target_pairs={{0,2},{1,3},{2,0},{3,1},{4,6},{5,7},{6,4},{7,5},{8,10},{9,11},{10,... | collective-permute-start | bytes 2359304 | tf_op jit(solution)/shard_map/ppermute | solution.py:1020
  187.8 6.5 %collective-permute-done.29.refs_5_ = bf16[1,192,768]{2,1,0:T(8,128)(2,1)} collective-permute-done((bf16[1,192,768]{2,1,0:T(8,128)(2,1)}, bf16[1,192,768]{2,1,0:T(8,128)(2,1)}, u32[]{:S(2)}, u32[]{:S(2)}) %collective-permute-start.29) | collective-permute-done | bytes 294944 | tf_op jit(solution)/shard_map/ppermute | solution.py:1020
  194.3 2.3 shard_map.254.refs_7_.refs_3_
  196.6 3.1 %collective-permute-start.39 = (bf16[2,192,768]{2,1,0:T(8,128)(2,1)}, bf16[2,192,768]{2,1,0:T(8,128)(2,1)}, u32[]{:S(2)}, u32[]{:S(2)}) collective-permute-start(bf16[2,192,768]{2,1,0:T(8,128)(2,1)} %shard_map.254.refs_7_.refs_3_), channel_id=1, source_target_pairs={{0,12},{1,13},{2,14},{3,15},{4,8},{5,9},{6,10},{7,11},{8,4},{9,5},... | collective-permute-start | bytes 1769480 | tf_op jit(solution)/shard_map/ppermute | solution.py:1020
  200.3 3.8 %collective-permute-start.31 = (bf16[512,768]{1,0:T(8,128)(2,1)S(1)}, bf16[512,768]{1,0:T(8,128)(2,1)S(1)}, u32[]{:S(2)}, u32[]{:S(2)}) collective-permute-start(bf16[512,768]{1,0:T(8,128)(2,1)S(1)} %copy-done.2), channel_id=1, source_target_pairs={{0,2},{1,3},{2,0},{3,1},{4,6},{5,7},{6,4},{7,5},{8,10},{9,11},{10,... | collective-permute-start | bytes 2359304 | tf_op jit(solution)/shard_map/ppermute | solution.py:1020
  204.1 2.4 shard_map.255.refs_8_.refs_1_
  206.5 1.9 collective-permute-start.35
  209.2 5.2 %shard_map.256.refs_0_ = bf16[2,512,768]{2,1,0:T(8,128)(2,1)} custom-call(bf16[512,768]{1,0:T(8,128)(2,1)} %shard_map.237.refs_0_.refs_2_, f32[512,768]{1,0:T(8,128)} %get-tuple-element.163.refs_1_, bf16[512,768]{1,0:T(8,128)(2,1)} %copy-done.20, f32[512,768]{1,0:T(8,128)} %get-tuple-element.171.refs_3_, f32[1,768]{1,0:T(1,128)} %broadcast_in_dim.13.refs_3_.refs_11_.refs_4_, ...), custom_call_target="tpu_custom_call" | custom-call | flops 115000000512 | tf_op jit(solution)/shard_map/pallas_call | solution.py:60
  214.4 18.0 %collective-permute-done.35.refs_1_.refs_2_ = bf16[272,768]{1,0:T(8,128)(2,1)S(1)} collective-permute-done((bf16[272,768]{1,0:T(8,128)(2,1)}, bf16[272,768]{1,0:T(8,128)(2,1)S(1)}, u32[]{:S(2)}, u32[]{:S(2)}) %collective-permute-start.35) | collective-permute-done | bytes 417824 | tf_op jit(solution)/shard_map/ppermute | solution.py:1020
  233.2 3.6 %shard_map.258 = (bf16[272,768]{1,0:T(8,128)(2,1)}, bf16[2,768,768]{2,1,0:T(8,128)(2,1)}) custom-call(s32[5]{0:T(128)} %stack.35.refs_0_, bf16[272,768]{1,0:T(8,128)(2,1)} %shard_map.255.refs_8_.refs_1_, bf16[272,768]{1,0:T(8,128)(2,1)} %copy-done.3, bf16[2,192,768]{2,1,0:T(8,128)(2,1)} %shard_map.254.refs_7_.refs_3_, ...), custom_call_target="tpu_custom_call" | custom-call | flops 103499997184 | tf_op jit(solution)/shard_map/pallas_call | solution.py:60
  236.8 2.7 collective-permute-start.43
  239.5 3.0 %collective-permute-start.42 = (bf16[272,768]{1,0:T(8,128)(2,1)}, bf16[272,768]{1,0:T(8,128)(2,1)}, u32[]{:S(2)}, u32[]{:S(2)}) collective-permute-start(bf16[272,768]{1,0:T(8,128)(2,1)} %get-tuple-element.176.refs_1_), channel_id=1, source_target_pairs={{0,12},{1,13},{2,14},{3,15},{4,8},{5,9},{6,10},{7,11},{8,4},{9,5},... | collective-permute-start | bytes 1253384 | tf_op jit(solution)/shard_map/ppermute | solution.py:1020
  242.5 1.1 collective-permute-start.40
  243.6 3.9 %collective-permute-start.36 = (bf16[2,512,768]{2,1,0:T(8,128)(2,1)}, bf16[2,512,768]{2,1,0:T(8,128)(2,1)}, u32[]{:S(2)}, u32[]{:S(2)}) collective-permute-start(bf16[2,512,768]{2,1,0:T(8,128)(2,1)} %shard_map.257.refs_7_.refs_1_), channel_id=1, source_target_pairs={{1,2},{2,1},{5,6},{6,5},{9,10},{10,9},{13,14},{14,13},{17,18},{18,... | collective-permute-start | bytes 4718600 | tf_op jit(solution)/shard_map/ppermute | solution.py:1020
  247.6 1.4 copy-done.10
  249.0 6.7 %shard_map.259 = (f32[768,1536]{1,0:T(8,128)}, f32[1536,768]{1,0:T(8,128)}) custom-call(s32[5]{0:T(128)} %stack.35.refs_0_, bf16[2,768,768]{2,1,0:T(8,128)(2,1)} %get-tuple-element.177.refs_1_.refs_3_, bf16[2,768,768]{2,1,0:T(8,128)(2,1)} %copy-done.10, bf16[2,768,768]{2,1,0:T(8,128)(2,1)} %get-tuple-element.177.refs_1_.refs_3_), custom_call_target="tpu_custom_call" | custom-call | flops 156399992832 | tf_op jit(solution)/shard_map/pallas_call | solution.py:60
  255.7 6.0 %collective-permute-done.41.refs_3_ = bf16[272,768]{1,0:T(8,128)(2,1)} collective-permute-done((bf16[272,768]{1,0:T(8,128)(2,1)}, bf16[272,768]{1,0:T(8,128)(2,1)}, u32[]{:S(2)}, u32[]{:S(2)}) %collective-permute-start.41) | collective-permute-done | bytes 417824 | tf_op jit(solution)/shard_map/ppermute | solution.py:1020
  261.9 2.6 shard_map.260.refs_3_.refs_1_
  265.0 1.0 collective-permute-done.36.refs_2_
  266.0 3.1 %shard_map.261 = (bf16[512,768]{1,0:T(8,128)(2,1)}, bf16[512,768]{1,0:T(8,128)(2,1)}) custom-call(s32[5]{0:T(128)} %stack.35.refs_0_, bf16[2,512,768]{2,1,0:T(8,128)(2,1)} %shard_map.257.refs_7_.refs_1_, bf16[2,512,768]{2,1,0:T(8,128)(2,1)} %collective-permute-done.36.refs_2_, bf16[848,768]{1,0:T(8,128)(2,1)} %shard_map.260.refs_3_.refs_1_), custom_call_target="tpu_custom_call" | custom-call | flops 46000001024 | tf_op jit(solution)/shard_map/pallas_call | solution.py:60
  269.1 1.1 copy-done.12
  270.2 4.6 %shard_map.262 = (f32[768,384]{1,0:T(8,128)}, f32[768,384]{1,0:T(8,128)}, f32[768,384]{1,0:T(8,128)}, f32[384,768]{1,0:T(8,128)}, f32[768]{0:T(1024)}, /*index=5*/f32[768]{0:T(1024)}, f32[768]{0:T(1024)}, f32[768]{0:T(1024)}) custom-call(s32[5]{0:T(128)} %stack.35.refs_0_, bf16[848,768]{1,0:T(8,128)(2,1)} %shard_map.260.refs_3_.refs_1_, ...), custom_call_target="tpu_custom_call" | custom-call | flops 103499997184 | tf_op jit(solution)/shard_map/pallas_call | solution.py:60
  (117 shorter events, 14.9 us)
Async XLA Ops:
  1.4 12.7 %collective-permute-start.3 = (s32[2,1024]{1,0:T(2,128)S(1)}, s32[2,1024]{1,0:T(2,128)S(1)}, u32[]{:S(2)}, u32[]{:S(2)}) collective-permute-start(s32[2,1024]{1,0:T(2,128)S(1)} %pad_add_fusion), channel_id=1, source_target_pairs={{0,2},{1,3},{2,0},{3,1},{4,6},{5,7},{6,4},{7,5},{8,10},{9,11},{10,... | collective-permute-start | bytes 24584 | tf_op jit(solution)/shard_map/ppermute | solution.py:1020
  1.5 16.0 %collective-permute-start = (bf16[512,768]{1,0:T(8,128)(2,1)}, bf16[512,768]{1,0:T(8,128)(2,1)S(1)}, u32[]{:S(2)}, u32[]{:S(2)}) collective-permute-start(bf16[512,768]{1,0:T(8,128)(2,1)} %refs_1_.4), channel_id=1, source_target_pairs={{1,2},{2,1},{5,6},{6,5},{9,10},{10,9},{13,14},{14,13},{17,18},{18,... | collective-permute-start | bytes 2359304 | tf_op jit(solution)/shard_map/ppermute | solution.py:1020
  6.6 5.1 %copy-start.6 = (f32[768]{0:T(1024)S(1)}, f32[768]{0:T(1024)}, u32[]{:S(2)}) copy-start(f32[768]{0:T(1024)} %param.17) | copy-start | bytes 9220
  6.7 5.7 %copy-start.7 = (f32[768]{0:T(1024)S(1)}, f32[768]{0:T(1024)}, u32[]{:S(2)}) copy-start(f32[768]{0:T(1024)} %param.18) | copy-start | bytes 9220
  6.7 6.2 %copy-start.8 = (f32[768]{0:T(1024)S(1)}, f32[768]{0:T(1024)}, u32[]{:S(2)}) copy-start(f32[768]{0:T(1024)} %param.23) | copy-start | bytes 9220
  6.7 6.8 %copy-start.9 = (f32[768]{0:T(1024)S(1)}, f32[768]{0:T(1024)}, u32[]{:S(2)}) copy-start(f32[768]{0:T(1024)} %param.24) | copy-start | bytes 9220
  6.7 7.4 %copy-start.4 = (s32[1,1024]{1,0:T(1,128)S(1)}, s32[1,1024]{1,0:T(1,128)}, u32[]{:S(2)}) copy-start(s32[1,1024]{1,0:T(1,128)} %param.16) | copy-start | bytes 12292
  6.7 7.4 %copy-start.5 = (s32[1,1024]{1,0:T(1,128)S(1)}, s32[1,1024]{1,0:T(1,128)}, u32[]{:S(2)}) copy-start(s32[1,1024]{1,0:T(1,128)} %param.15) | copy-start | bytes 12292
  9.8 19.1 %collective-permute-start.2 = (bf16[768,128]{1,0:T(8,128)(2,1)}, bf16[768,128]{1,0:T(8,128)(2,1)}, u32[]{:S(2)}, u32[]{:S(2)}) collective-permute-start(bf16[768,128]{1,0:T(8,128)(2,1)} %get-tuple-element.101.refs_5_.refs_3_), channel_id=1, source_target_pairs={{0,1},{2,3},{4,5},{6,7},{8,9},{10,11},{12,13},{14,15},{16,17},{18,... | collective-permute-start | bytes 589832 | tf_op jit(solution)/shard_map/ppermute | solution.py:1020
  11.7 27.3 %collective-permute-start.4 = (bf16[384,576]{1,0:T(8,128)(2,1)}, bf16[384,576]{1,0:T(8,128)(2,1)}, u32[]{:S(2)}, u32[]{:S(2)}) collective-permute-start(bf16[384,576]{1,0:T(8,128)(2,1)} %get-tuple-element.106), channel_id=1, source_target_pairs={{0,1},{1,0},{2,3},{3,2},{4,5},{5,4},{6,7},{7,6},{8,9},{9,8},{10,11... | collective-permute-start | bytes 1327112 | tf_op jit(solution)/shard_map/ppermute | solution.py:1020
  21.2 9.1 %collective-permute-start.1 = (bf16[512,768]{1,0:T(8,128)(2,1)}, bf16[512,768]{1,0:T(8,128)(2,1)S(1)}, u32[]{:S(2)}, u32[]{:S(2)}) collective-permute-start(bf16[512,768]{1,0:T(8,128)(2,1)} %get-tuple-element.103.refs_5_.refs_1_), channel_id=1, source_target_pairs={{0,2},{1,3},{2,0},{3,1},{4,6},{5,7},{6,4},{7,5},{8,10},{9,11},{10,... | collective-permute-start | bytes 2359304 | tf_op jit(solution)/shard_map/ppermute | solution.py:1020
  26.3 24.3 %collective-permute-start.6 = (bf16[192,768]{1,0:T(8,128)(2,1)}, bf16[192,768]{1,0:T(8,128)(2,1)}, u32[]{:S(2)}, u32[]{:S(2)}) collective-permute-start(bf16[192,768]{1,0:T(8,128)(2,1)} %get-tuple-element.111.refs_6_.refs_3_), channel_id=1, source_target_pairs={{0,1},{1,0},{2,3},{3,2},{4,5},{5,4},{6,7},{7,6},{8,9},{9,8},{10,11... | collective-permute-start | bytes 884744 | tf_op jit(solution)/shard_map/ppermute | solution.py:1020
  28.8 21.8 %collective-permute-start.7 = (bf16[384,768]{1,0:T(8,128)(2,1)}, bf16[384,768]{1,0:T(8,128)(2,1)}, u32[]{:S(2)}, u32[]{:S(2)}) collective-permute-start(bf16[384,768]{1,0:T(8,128)(2,1)} %get-tuple-element.112), channel_id=1, source_target_pairs={{0,1},{1,0},{2,3},{3,2},{4,5},{5,4},{6,7},{7,6},{8,9},{9,8},{10,11... | collective-permute-start | bytes 1769480 | tf_op jit(solution)/shard_map/ppermute | solution.py:1020
  28.8 34.0 %collective-permute-start.8 = (bf16[384,768]{1,0:T(8,128)(2,1)}, bf16[384,768]{1,0:T(8,128)(2,1)}, u32[]{:S(2)}, u32[]{:S(2)}) collective-permute-start(bf16[384,768]{1,0:T(8,128)(2,1)} %get-tuple-element.115), channel_id=1, source_target_pairs={{0,1},{1,0},{2,3},{3,2},{4,5},{5,4},{6,7},{7,6},{8,9},{9,8},{10,11... | collective-permute-start | bytes 1769480 | tf_op jit(solution)/shard_map/ppermute | solution.py:1020
  30.3 2.4 copy-start.19
  30.3 40.1 %collective-permute-start.11 = (bf16[512,768]{1,0:T(8,128)(2,1)}, bf16[512,768]{1,0:T(8,128)(2,1)}, u32[]{:S(2)}, u32[]{:S(2)}) collective-permute-start(bf16[512,768]{1,0:T(8,128)(2,1)} %get-tuple-element.104.refs_6_), channel_id=1, source_target_pairs={{1,2},{2,1},{5,6},{6,5},{9,10},{10,9},{13,14},{14,13},{17,18},{18,... | collective-permute-start | bytes 2359304 | tf_op jit(solution)/shard_map/ppermute | solution.py:1020
  39.1 11.5 %collective-permute-start.5 = (bf16[384,576]{1,0:T(8,128)(2,1)}, bf16[384,576]{1,0:T(8,128)(2,1)}, u32[]{:S(2)}, u32[]{:S(2)}) collective-permute-start(bf16[384,576]{1,0:T(8,128)(2,1)} %shard_map.233.refs_2_), channel_id=1, source_target_pairs={{0,4},{1,5},{2,10},{3,11},{4,0},{5,1},{6,14},{7,15},{8,12},{9,13},... | collective-permute-start | bytes 1327112 | tf_op jit(solution)/shard_map/ppermute | solution.py:1020
  62.8 2.6 collective-permute-start.9
  62.9 26.8 %collective-permute-start.13 = (bf16[384,768]{1,0:T(8,128)(2,1)}, bf16[384,768]{1,0:T(8,128)(2,1)}, u32[]{:S(2)}, u32[]{:S(2)}) collective-permute-start(bf16[384,768]{1,0:T(8,128)(2,1)} %get-tuple-element.119.refs_5_), channel_id=1, source_target_pairs={{0,4},{1,5},{2,10},{3,11},{4,0},{5,1},{6,14},{7,15},{8,12},{9,13},... | collective-permute-start | bytes 1769480 | tf_op jit(solution)/shard_map/ppermute | solution.py:1020
  64.3 25.5 %collective-permute-start.14 = (bf16[384,768]{1,0:T(8,128)(2,1)}, bf16[384,768]{1,0:T(8,128)(2,1)}, u32[]{:S(2)}, u32[]{:S(2)}) collective-permute-start(bf16[384,768]{1,0:T(8,128)(2,1)} %get-tuple-element.120.refs_7_), channel_id=1, source_target_pairs={{0,4},{1,5},{2,10},{3,11},{4,0},{5,1},{6,14},{7,15},{8,12},{9,13},... | collective-permute-start | bytes 1769480 | tf_op jit(solution)/shard_map/ppermute | solution.py:1020
  65.4 0.9 copy-start.21
  69.3 1.1 copy-start
  69.3 4.7 %collective-permute-start.10 = (bf16[512,768]{1,0:T(8,128)(2,1)}, bf16[512,768]{1,0:T(8,128)(2,1)S(1)}, u32[]{:S(2)}, u32[]{:S(2)}) collective-permute-start(bf16[512,768]{1,0:T(8,128)(2,1)} %get-tuple-element.118.refs_1_.refs_2_.refs_7_), channel_id=1, source_target_pairs={{0,2},{1,3},{2,0},{3,1},{4,6},{5,7},{6,4},{7,5},{8,10},{9,11},{10,... | collective-permute-start | bytes 2359304 | tf_op jit(solution)/shard_map/ppermute | solution.py:1020
  71.7 0.9 copy-start.1
  71.7 2.4 collective-permute-start.12
  74.0 0.9 copy-start.18
  74.0 1.1 copy-start.17
  88.5 16.1 %collective-permute-start.15 = (bf16[2,384,768]{2,1,0:T(8,128)(2,1)}, bf16[2,384,768]{2,1,0:T(8,128)(2,1)}, u32[]{:S(2)}, u32[]{:S(2)}) collective-permute-start(bf16[2,384,768]{2,1,0:T(8,128)(2,1)} %get-tuple-element.127.refs_13_), channel_id=1, source_target_pairs={{0,4},{1,5},{2,10},{3,11},{4,0},{5,1},{6,14},{7,15},{8,12},{9,13},... | collective-permute-start | bytes 3538952 | tf_op jit(solution)/shard_map/ppermute | solution.py:1020
  104.6 3.2 %collective-permute-start.16 = (bf16[512,768]{1,0:T(8,128)(2,1)}, bf16[512,768]{1,0:T(8,128)(2,1)S(1)}, u32[]{:S(2)}, u32[]{:S(2)}) collective-permute-start(bf16[512,768]{1,0:T(8,128)(2,1)} %get-tuple-element.134), channel_id=1, source_target_pairs={{0,2},{1,3},{2,0},{3,1},{4,6},{5,7},{6,4},{7,5},{8,10},{9,11},{10,... | collective-permute-start | bytes 2359304 | tf_op jit(solution)/shard_map/ppermute | solution.py:1020
  105.2 31.7 %collective-permute-start.19 = (bf16[2,192,768]{2,1,0:T(8,128)(2,1)}, bf16[2,192,768]{2,1,0:T(8,128)(2,1)}, u32[]{:S(2)}, u32[]{:S(2)}) collective-permute-start(bf16[2,192,768]{2,1,0:T(8,128)(2,1)} %get-tuple-element.147), channel_id=1, source_target_pairs={{0,8},{1,9},{2,6},{3,7},{4,12},{5,13},{6,2},{7,3},{8,0},{9,1},{10,... | collective-permute-start | bytes 1769480 | tf_op jit(solution)/shard_map/ppermute | solution.py:1020
  106.4 31.8 %collective-permute-start.20 = (bf16[2,192,768]{2,1,0:T(8,128)(2,1)}, bf16[2,192,768]{2,1,0:T(8,128)(2,1)}, u32[]{:S(2)}, u32[]{:S(2)}) collective-permute-start(bf16[2,192,768]{2,1,0:T(8,128)(2,1)} %get-tuple-element.148), channel_id=1, source_target_pairs={{0,4},{1,5},{2,10},{3,11},{4,0},{5,1},{6,14},{7,15},{8,12},{9,13},... | collective-permute-start | bytes 1769480 | tf_op jit(solution)/shard_map/ppermute | solution.py:1020
  107.6 31.7 %collective-permute-start.21 = (bf16[2,192,768]{2,1,0:T(8,128)(2,1)}, bf16[2,192,768]{2,1,0:T(8,128)(2,1)}, u32[]{:S(2)}, u32[]{:S(2)}) collective-permute-start(bf16[2,192,768]{2,1,0:T(8,128)(2,1)} %get-tuple-element.135.refs_5_), channel_id=1, source_target_pairs={{0,12},{1,13},{2,14},{3,15},{4,8},{5,9},{6,10},{7,11},{8,4},{9,5},... | collective-permute-start | bytes 1769480 | tf_op jit(solution)/shard_map/ppermute | solution.py:1020
  112.7 5.0 %collective-permute-start.17 = (bf16[512,768]{1,0:T(8,128)(2,1)}, bf16[512,768]{1,0:T(8,128)(2,1)S(1)}, u32[]{:S(2)}, u32[]{:S(2)}) collective-permute-start(bf16[512,768]{1,0:T(8,128)(2,1)} %get-tuple-element.136.refs_1_), channel_id=1, source_target_pairs={{0,2},{1,3},{2,0},{3,1},{4,6},{5,7},{6,4},{7,5},{8,10},{9,11},{10,... | collective-permute-start | bytes 2359304 | tf_op jit(solution)/shard_map/ppermute | solution.py:1020
  116.4 23.3 %collective-permute-start.18 = (bf16[2,192,768]{2,1,0:T(8,128)(2,1)}, bf16[2,192,768]{2,1,0:T(8,128)(2,1)}, u32[]{:S(2)}, u32[]{:S(2)}) collective-permute-start(bf16[2,192,768]{2,1,0:T(8,128)(2,1)} %get-tuple-element.143.refs_8_), channel_id=1, source_target_pairs={{0,8},{1,9},{2,6},{3,7},{4,12},{5,13},{6,2},{7,3},{8,0},{9,1},{10,... | collective-permute-start | bytes 1769480 | tf_op jit(solution)/shard_map/ppermute | solution.py:1020
  136.6 24.3 %collective-permute-start.23 = (bf16[1,192,768]{2,1,0:T(8,128)(2,1)}, bf16[1,192,768]{2,1,0:T(8,128)(2,1)}, u32[]{:S(2)}, u32[]{:S(2)}) collective-permute-start(bf16[1,192,768]{2,1,0:T(8,128)(2,1)} %get-tuple-element.159), channel_id=1, source_target_pairs={{0,8},{1,9},{2,6},{3,7},{4,12},{5,13},{6,2},{7,3},{8,0},{9,1},{10,... | collective-permute-start | bytes 884744 | tf_op jit(solution)/shard_map/ppermute | solution.py:1020
  136.9 24.0 %collective-permute-start.24 = (bf16[1,192,768]{2,1,0:T(8,128)(2,1)}, bf16[1,192,768]{2,1,0:T(8,128)(2,1)}, u32[]{:S(2)}, u32[]{:S(2)}) collective-permute-start(bf16[1,192,768]{2,1,0:T(8,128)(2,1)} %get-tuple-element.160), channel_id=1, source_target_pairs={{0,4},{1,5},{2,10},{3,11},{4,0},{5,1},{6,14},{7,15},{8,12},{9,13},... | collective-permute-start | bytes 884744 | tf_op jit(solution)/shard_map/ppermute | solution.py:1020
  138.1 22.8 %collective-permute-start.25 = (bf16[1,192,768]{2,1,0:T(8,128)(2,1)}, bf16[1,192,768]{2,1,0:T(8,128)(2,1)}, u32[]{:S(2)}, u32[]{:S(2)}) collective-permute-start(bf16[1,192,768]{2,1,0:T(8,128)(2,1)} %get-tuple-element.151.refs_6_), channel_id=1, source_target_pairs={{0,12},{1,13},{2,14},{3,15},{4,8},{5,9},{6,10},{7,11},{8,4},{9,5},... | collective-permute-start | bytes 884744 | tf_op jit(solution)/shard_map/ppermute | solution.py:1020
  143.0 17.9 %collective-permute-start.26 = (bf16[2,192,768]{2,1,0:T(8,128)(2,1)}, bf16[2,192,768]{2,1,0:T(8,128)(2,1)}, u32[]{:S(2)}, u32[]{:S(2)}) collective-permute-start(bf16[2,192,768]{2,1,0:T(8,128)(2,1)} %get-tuple-element.152.refs_9_), channel_id=1, source_target_pairs={{0,1},{1,0},{2,3},{3,2},{4,5},{5,4},{6,7},{7,6},{8,9},{9,8},{10,11... | collective-permute-start | bytes 1769480 | tf_op jit(solution)/shard_map/ppermute | solution.py:1020
  159.4 9.3 %collective-permute-start.22 = (bf16[1024,1024]{1,0:T(8,128)(2,1)}, bf16[1024,1024]{1,0:T(8,128)(2,1)S(1)}, u32[]{:S(2)}, u32[]{:S(2)}) collective-permute-start(bf16[1024,1024]{1,0:T(8,128)(2,1)} %get-tuple-element.153.refs_10_.refs_1_), channel_id=1, source_target_pairs={{0,2},{1,3},{2,0},{3,1},{4,6},{5,7},{6,4},{7,5},{8,10},{9,11},{10,... | collective-permute-start | bytes 6291464 | tf_op jit(solution)/shard_map/ppermute | solution.py:1020
  165.9 18.5 %collective-permute-start.27 = (bf16[1,192,768]{2,1,0:T(8,128)(2,1)}, bf16[1,192,768]{2,1,0:T(8,128)(2,1)}, u32[]{:S(2)}, u32[]{:S(2)}) collective-permute-start(bf16[1,192,768]{2,1,0:T(8,128)(2,1)} %get-tuple-element.167), channel_id=1, source_target_pairs={{0,8},{1,9},{2,6},{3,7},{4,12},{5,13},{6,2},{7,3},{8,0},{9,1},{10,... | collective-permute-start | bytes 884744 | tf_op jit(solution)/shard_map/ppermute | solution.py:1020
  166.8 21.0 %collective-permute-start.28 = (bf16[1,192,768]{2,1,0:T(8,128)(2,1)}, bf16[1,192,768]{2,1,0:T(8,128)(2,1)}, u32[]{:S(2)}, u32[]{:S(2)}) collective-permute-start(bf16[1,192,768]{2,1,0:T(8,128)(2,1)} %get-tuple-element.168), channel_id=1, source_target_pairs={{0,4},{1,5},{2,10},{3,11},{4,0},{5,1},{6,14},{7,15},{8,12},{9,13},... | collective-permute-start | bytes 884744 | tf_op jit(solution)/shard_map/ppermute | solution.py:1020
  168.1 19.7 %collective-permute-start.30 = (bf16[1,192,768]{2,1,0:T(8,128)(2,1)}, bf16[1,192,768]{2,1,0:T(8,128)(2,1)}, u32[]{:S(2)}, u32[]{:S(2)}) collective-permute-start(bf16[1,192,768]{2,1,0:T(8,128)(2,1)} %get-tuple-element.169), channel_id=1, source_target_pairs={{0,1},{1,0},{2,3},{3,2},{4,5},{5,4},{6,7},{7,6},{8,9},{9,8},{10,11... | collective-permute-start | bytes 884744 | tf_op jit(solution)/shard_map/ppermute | solution.py:1020
  168.1 26.2 %collective-permute-start.29 = (bf16[1,192,768]{2,1,0:T(8,128)(2,1)}, bf16[1,192,768]{2,1,0:T(8,128)(2,1)}, u32[]{:S(2)}, u32[]{:S(2)}) collective-permute-start(bf16[1,192,768]{2,1,0:T(8,128)(2,1)} %get-tuple-element.162.refs_14_), channel_id=1, source_target_pairs={{0,12},{1,13},{2,14},{3,15},{4,8},{5,9},{6,10},{7,11},{8,4},{9,5},... | collective-permute-start | bytes 884744 | tf_op jit(solution)/shard_map/ppermute | solution.py:1020
  168.7 2.3 copy-start.11
  168.7 25.7 %collective-permute-start.34 = (bf16[2,192,768]{2,1,0:T(8,128)(2,1)}, bf16[2,192,768]{2,1,0:T(8,128)(2,1)}, u32[]{:S(2)}, u32[]{:S(2)}) collective-permute-start(bf16[2,192,768]{2,1,0:T(8,128)(2,1)} %get-tuple-element.175.refs_0_), channel_id=1, source_target_pairs={{0,16},{1,17},{2,18},{3,19},{4,20},{5,21},{6,22},{7,23},{8,24},{9,... | collective-permute-start | bytes 1769480 | tf_op jit(solution)/shard_map/ppermute | solution.py:1020
  171.0 13.5 %copy-start.13 = (bf16[512,768]{1,0:T(8,128)(2,1)S(1)}, bf16[512,768]{1,0:T(8,128)(2,1)}, u32[]{:S(2)}) copy-start(bf16[512,768]{1,0:T(8,128)(2,1)} %get-tuple-element.173) | copy-start | bytes 2359300
  184.5 22.0 %collective-permute-start.32 = (bf16[512,768]{1,0:T(8,128)(2,1)S(1)}, bf16[512,768]{1,0:T(8,128)(2,1)S(1)}, u32[]{:S(2)}, u32[]{:S(2)}) collective-permute-start(bf16[512,768]{1,0:T(8,128)(2,1)S(1)} %copy-done.13), channel_id=1, source_target_pairs={{0,2},{1,3},{2,0},{3,1},{4,6},{5,7},{6,4},{7,5},{8,10},{9,11},{10,... | collective-permute-start | bytes 2359304 | tf_op jit(solution)/shard_map/ppermute | solution.py:1020
  194.3 6.0 %copy-start.2 = (bf16[512,768]{1,0:T(8,128)(2,1)S(1)}, bf16[512,768]{1,0:T(8,128)(2,1)}, u32[]{:S(2)}) copy-start(bf16[512,768]{1,0:T(8,128)(2,1)} %get-tuple-element.170) | copy-start | bytes 2359300
  194.3 6.0 %collective-permute-start.33 = (bf16[80,768]{1,0:T(8,128)(2,1)}, bf16[80,768]{1,0:T(8,128)(2,1)S(1)}, u32[]{:S(2)}, u32[]{:S(2)}) collective-permute-start(bf16[80,768]{1,0:T(8,128)(2,1)} %get-tuple-element.174.refs_2_.refs_0_), channel_id=1, source_target_pairs={{0,1},{1,0},{2,3},{3,2},{4,5},{5,4},{6,7},{7,6},{8,9},{9,8},{10,11... | collective-permute-start | bytes 368648 | tf_op jit(solution)/shard_map/ppermute | solution.py:1020
  196.6 36.6 %collective-permute-start.39 = (bf16[2,192,768]{2,1,0:T(8,128)(2,1)}, bf16[2,192,768]{2,1,0:T(8,128)(2,1)}, u32[]{:S(2)}, u32[]{:S(2)}) collective-permute-start(bf16[2,192,768]{2,1,0:T(8,128)(2,1)} %shard_map.254.refs_7_.refs_3_), channel_id=1, source_target_pairs={{0,12},{1,13},{2,14},{3,15},{4,8},{5,9},{6,10},{7,11},{8,4},{9,5},... | collective-permute-start | bytes 1769480 | tf_op jit(solution)/shard_map/ppermute | solution.py:1020
  199.7 33.5 %collective-permute-start.38 = (bf16[2,192,768]{2,1,0:T(8,128)(2,1)}, bf16[2,192,768]{2,1,0:T(8,128)(2,1)}, u32[]{:S(2)}, u32[]{:S(2)}) collective-permute-start(bf16[2,192,768]{2,1,0:T(8,128)(2,1)} %shard_map.254.refs_7_.refs_3_), channel_id=1, source_target_pairs={{0,4},{1,5},{2,10},{3,11},{4,0},{5,1},{6,14},{7,15},{8,12},{9,13},... | collective-permute-start | bytes 1769480 | tf_op jit(solution)/shard_map/ppermute | solution.py:1020
  199.7 33.5 %collective-permute-start.37 = (bf16[2,192,768]{2,1,0:T(8,128)(2,1)}, bf16[2,192,768]{2,1,0:T(8,128)(2,1)}, u32[]{:S(2)}, u32[]{:S(2)}) collective-permute-start(bf16[2,192,768]{2,1,0:T(8,128)(2,1)} %shard_map.254.refs_7_.refs_3_), channel_id=1, source_target_pairs={{0,8},{1,9},{2,6},{3,7},{4,12},{5,13},{6,2},{7,3},{8,0},{9,1},{10,... | collective-permute-start | bytes 1769480 | tf_op jit(solution)/shard_map/ppermute | solution.py:1020
  200.3 3.8 %copy-start.23 = (bf16[80,768]{1,0:T(8,128)(2,1)}, bf16[80,768]{1,0:T(8,128)(2,1)S(1)}, u32[]{:S(2)}) copy-start(bf16[80,768]{1,0:T(8,128)(2,1)S(1)} %collective-permute-done.33.refs_1_) | copy-start | bytes 368644
  200.3 8.0 %collective-permute-start.31 = (bf16[512,768]{1,0:T(8,128)(2,1)S(1)}, bf16[512,768]{1,0:T(8,128)(2,1)S(1)}, u32[]{:S(2)}, u32[]{:S(2)}) collective-permute-start(bf16[512,768]{1,0:T(8,128)(2,1)S(1)} %copy-done.2), channel_id=1, source_target_pairs={{0,2},{1,3},{2,0},{3,1},{4,6},{5,7},{6,4},{7,5},{8,10},{9,11},{10,... | collective-permute-start | bytes 2359304 | tf_op jit(solution)/shard_map/ppermute | solution.py:1020
  206.5 1.9 copy-start.16
  206.5 26.0 %collective-permute-start.35 = (bf16[272,768]{1,0:T(8,128)(2,1)}, bf16[272,768]{1,0:T(8,128)(2,1)S(1)}, u32[]{:S(2)}, u32[]{:S(2)}) collective-permute-start(bf16[272,768]{1,0:T(8,128)(2,1)} %shard_map.255.refs_8_.refs_1_), channel_id=1, source_target_pairs={{0,16},{1,17},{2,18},{3,19},{4,20},{5,21},{6,22},{7,23},{8,24},{9,... | collective-permute-start | bytes 1253384 | tf_op jit(solution)/shard_map/ppermute | solution.py:1020
  236.8 10.8 %collective-permute-start.43 = (bf16[2,768,768]{2,1,0:T(8,128)(2,1)}, bf16[2,768,768]{2,1,0:T(8,128)(2,1)S(1)}, u32[]{:S(2)}, u32[]{:S(2)}) collective-permute-start(bf16[2,768,768]{2,1,0:T(8,128)(2,1)} %get-tuple-element.177.refs_1_.refs_3_), channel_id=1, source_target_pairs={{0,2},{1,3},{2,0},{3,1},{4,6},{5,7},{6,4},{7,5},{8,10},{9,11},{10,... | collective-permute-start | bytes 7077896 | tf_op jit(solution)/shard_map/ppermute | solution.py:1020
  239.5 16.2 %collective-permute-start.42 = (bf16[272,768]{1,0:T(8,128)(2,1)}, bf16[272,768]{1,0:T(8,128)(2,1)}, u32[]{:S(2)}, u32[]{:S(2)}) collective-permute-start(bf16[272,768]{1,0:T(8,128)(2,1)} %get-tuple-element.176.refs_1_), channel_id=1, source_target_pairs={{0,12},{1,13},{2,14},{3,15},{4,8},{5,9},{6,10},{7,11},{8,4},{9,5},... | collective-permute-start | bytes 1253384 | tf_op jit(solution)/shard_map/ppermute | solution.py:1020
  242.5 19.2 %collective-permute-start.41 = (bf16[272,768]{1,0:T(8,128)(2,1)}, bf16[272,768]{1,0:T(8,128)(2,1)}, u32[]{:S(2)}, u32[]{:S(2)}) collective-permute-start(bf16[272,768]{1,0:T(8,128)(2,1)} %get-tuple-element.176.refs_1_), channel_id=1, source_target_pairs={{0,4},{1,5},{2,10},{3,11},{4,0},{5,1},{6,14},{7,15},{8,12},{9,13},... | collective-permute-start | bytes 1253384 | tf_op jit(solution)/shard_map/ppermute | solution.py:1020
  242.5 19.4 %collective-permute-start.40 = (bf16[272,768]{1,0:T(8,128)(2,1)}, bf16[272,768]{1,0:T(8,128)(2,1)}, u32[]{:S(2)}, u32[]{:S(2)}) collective-permute-start(bf16[272,768]{1,0:T(8,128)(2,1)} %get-tuple-element.176.refs_1_), channel_id=1, source_target_pairs={{0,8},{1,9},{2,6},{3,7},{4,12},{5,13},{6,2},{7,3},{8,0},{9,1},{10,... | collective-permute-start | bytes 1253384 | tf_op jit(solution)/shard_map/ppermute | solution.py:1020
  243.6 22.3 %collective-permute-start.36 = (bf16[2,512,768]{2,1,0:T(8,128)(2,1)}, bf16[2,512,768]{2,1,0:T(8,128)(2,1)}, u32[]{:S(2)}, u32[]{:S(2)}) collective-permute-start(bf16[2,512,768]{2,1,0:T(8,128)(2,1)} %shard_map.257.refs_7_.refs_1_), channel_id=1, source_target_pairs={{1,2},{2,1},{5,6},{6,5},{9,10},{10,9},{13,14},{14,13},{17,18},{18,... | collective-permute-start | bytes 4718600 | tf_op jit(solution)/shard_map/ppermute | solution.py:1020
  247.6 1.4 copy-start.10
  264.5 4.6 %collective-permute-start.44 = (bf16[848,768]{1,0:T(8,128)(2,1)}, bf16[848,768]{1,0:T(8,128)(2,1)S(1)}, u32[]{:S(2)}, u32[]{:S(2)}) collective-permute-start(bf16[848,768]{1,0:T(8,128)(2,1)} %shard_map.260.refs_3_.refs_1_), channel_id=1, source_target_pairs={{0,2},{1,3},{2,0},{3,1},{4,6},{5,7},{6,4},{7,5},{8,10},{9,11},{10,... | collective-permute-start | bytes 3907592 | tf_op jit(solution)/shard_map/ppermute | solution.py:1020
  269.1 1.1 copy-start.12
  (5 other events, 4.3 us)
